TPU v7x, 32 devices: a whole 2x2x4 slice. The times are simulated.
32 devices in a mesh: copy: 2 (over x), tm: 2 (over core), space: 8 (over z, y).
Axes of the slice: x: 2, y: 2, z: 4, core: 2. Of those that a mesh axis runs over, the one named last changes fastest.
Arguments:
- initial: float32 [4, 16, 128, 128], P(('copy', 'tm'), 'space'), parts along dimension 0, may hold values from 0.1 to 2
- source: bfloat16 [4, 16, 128, 128], P(('copy', 'tm'), 'space'), parts along dimension 0, may hold values from 0.049804688 to 1
- diffusion: float32 [16, 128, 128], P('space'), may hold values from 0.02 to 0.5
- wind_field: float32 [3, 16, 128, 128], P(None, 'space'), may hold values from -0.6 to 0.6
- buildings: int32 [16, 128, 128], P('space'), may hold values from 0 to 1, as said below
- strength: float32 [2, 4], P('tm'), may hold values from 0.5 to 2
Outputs:
- advanced: float32 [4, 16, 128, 128], P(('copy', 'tm'), 'space'), parts along dimension 0
- final_fine: float32 [4, 16, 128, 128], P(('copy', 'tm'), 'space'), parts along dimension 0
There are 2 independent parts, one for each index of `copy`. A program takes and returns all parts, laid end to end along the dimension named above; an argument that names none is the same for every part. Nothing has to cross between parts.
Inputs may be any that keep to these rules, and one draw needn't show every extreme that they name: buildings stand on the ground as columns.
All inputs are finite; a program needn't handle non-finite values.
Results may differ from a plain program's by a relative error of at most 0.0003.
Values sent between devices are 32-bit elements; how exact they have to be, the bound alone decides.
No kernel may reach another device: no remote copies, remote signals or barrier semaphores. Data moves between devices by JAX's collectives and lax.ppermute only.
A program may use at most 64 MiB of HBM per device.

v0:
```python
import jax
import jax.numpy as jnp
from jax import lax
from jax.sharding import PartitionSpec as P

FINE = 4


lower_bound = 0.5


def extended(block, sides, width):
    for axis, dim in sides:
        count = lax.axis_size(axis)
        forward = [(i, i + 1) for i in range(count - 1)]
        backward = [(target, source) for source, target in forward]
        low = lax.ppermute(
            lax.slice_in_dim(block, block.shape[dim] - width, None, axis=dim), axis, forward
        )
        high = lax.ppermute(lax.slice_in_dim(block, 0, width, axis=dim), axis, backward)
        block = jnp.concatenate([low, block, high], axis=dim)
    return block


def shifted(array, axis, by):
    peers = lax.axis_size(axis)
    pairs = [(i, i + by) for i in range(peers) if 0 <= i + by < peers]
    return lax.ppermute(array, axis, pairs)


def ahead(values, direction):
    length = values.shape[direction]
    tail = lax.slice_in_dim(values, 1, length, axis=direction)
    blank = jnp.zeros_like(lax.slice_in_dim(values, 0, 1, axis=direction))
    return jnp.concatenate([tail, blank], axis=direction)


def behind(values, direction):
    length = values.shape[direction]
    head = lax.slice_in_dim(values, 0, length - 1, axis=direction)
    blank = jnp.zeros_like(lax.slice_in_dim(values, 0, 1, axis=direction))
    return jnp.concatenate([blank, head], axis=direction)


def face_terms(masked, winds):
    opened = jnp.where(masked > 0.0, 1.0, 0.0).astype(masked.dtype)
    result = []
    for direction in range(3):
        conduct = jnp.sqrt(masked * ahead(masked, direction))
        velocity = (
            0.5
            * (winds[direction] + ahead(winds[direction], direction))
            * opened
            * ahead(opened, direction)
        )
        result.append((conduct, velocity))
    return tuple(result)


def disk_fields(face_set):
    conduct_sum = jnp.zeros_like(face_set[0][0])
    speed_sum = jnp.zeros_like(face_set[0][0])
    for direction in range(3):
        conduct, velocity = face_set[direction]
        speed = jnp.abs(velocity)
        conduct_sum = conduct_sum + conduct + behind(conduct, direction)
        speed_sum = speed_sum + speed + behind(speed, direction)
    return (conduct_sum, speed_sum)


def operate(values, face_set, rate):
    total = values
    for direction in range(3):
        conduct, velocity = face_set[direction]
        neighbor = ahead(values, direction)
        flowing = conduct * (values - neighbor) + rate * (
            jnp.maximum(velocity, 0.0) * values + jnp.minimum(velocity, 0.0) * neighbor
        )
        total = total + flowing - behind(flowing, direction)
    return total


def coefficients(bound):
    theta = (bound + lower_bound) * 0.5
    delta = (bound - lower_bound) * 0.5
    sigma = theta / delta
    rho_one = 1.0 / sigma
    rho_two = 1.0 / (2.0 * sigma - rho_one)
    return (theta, delta, rho_one, rho_two)


def shards(initial, source, diffusion, wind_field, buildings, strength):
    opened = (1 - buildings).astype(jnp.float32)
    masked = diffusion * opened
    forcing = source[0].astype(jnp.float32) * opened
    rates = strength[0]
    margin = 2
    stacked = jnp.stack([masked, wind_field[0], wind_field[1], wind_field[2], forcing])
    border = extended(stacked, (("space", 1),), 2)
    face_set = face_terms(border[0], (border[1], border[2], border[3]))
    inner_set = tuple(((pair[0][1:-1], pair[1][1:-1]) for pair in face_set))
    forcing_ext = border[4]
    conduct_sum, speed_sum = disk_fields(face_set)
    conduct_sum = conduct_sum[margin:-margin]
    speed_sum = speed_sum[margin:-margin]

    def advance(current, fine_step, bound):
        rate = rates[fine_step]
        theta, delta, rho_one, rho_two = coefficients(bound)
        widened = extended(current, (("space", 0),), 2)
        residual = widened[1:-1] + forcing_ext[1:-1] - operate(widened, face_set, rate)[1:-1]
        update = residual / theta
        moved = current + update[1:-1]
        residual = residual[1:-1] - operate(update, inner_set, rate)[1:-1]
        update = update[1:-1]
        update = rho_two * rho_one * update + 2.0 * rho_two / delta * residual
        return moved + update

    bound_row = []
    starting = initial[0] * opened
    current = starting
    for fine_step in range(FINE):
        local = jnp.max(1.0 + 2.0 * conduct_sum + rates[fine_step] * speed_sum)
        bound_row.append(lax.pmax(local, "space"))
        current = advance(current, fine_step, bound_row[fine_step])
    advanced = current
    incoming = shifted(advanced, "tm", 1)
    current = jnp.where(lax.axis_index("tm") == 0, starting, incoming)
    for fine_step in range(FINE - 1):
        current = advance(current, fine_step, bound_row[fine_step])
    return (advanced[None], current[None])


def solution(mesh):
    in_specs = (
        P(("copy", "tm"), "space", None, None),
        P(("copy", "tm"), "space", None, None),
        P("space", None, None),
        P(None, "space", None, None),
        P("space", None, None),
        P("tm", None),
    )
    out_specs = (P(("copy", "tm"), "space", None, None), P(("copy", "tm"), "space", None, None))
    return jax.shard_map(shards, mesh=mesh, in_specs=in_specs, out_specs=out_specs, check_vma=False)
```

profile of v0, /device:TPU:0, one launch (start us, length us, event | category | flops | bytes accessed | tf_op | source)
XLA Modules:
  0.0 163.1 jit_solution(1393754445144058209)
XLA Ops:
  0.6 1.1 multiply_bitcast_fusion
  1.8 1.1 pad_maximum_fusion.1
  2.9 4.9 %collective-permute-start.2 = (f32[5,2,128,128]{3,2,1,0:T(8,128)S(1)}, f32[5,2,128,128]{3,2,1,0:T(8,128)S(1)}, u32[]{:S(2)}, u32[]{:S(2)}) collective-permute-start(f32[5,2,128,128]{3,2,1,0:T(8,128)S(1)} %pad_maximum_fusion.1), channel_id=1, source_target_pairs={{0,1},{1,2},{2,3},{3,4},{4,5},{5,6},{6,7},{8,9},{9,10},{10,11},{11... | collective-permute-start | bytes 1966088 | tf_op jit(solution)/shard_map/ppermute | solution.py:17
  7.8 1.3 collective-permute-start.3
  9.1 4.6 %collective-permute-start = (f32[2,128,128]{2,1,0:T(8,128)S(1)}, f32[2,128,128]{2,1,0:T(8,128)S(1)}, u32[]{:S(2)}, u32[]{:S(2)}) collective-permute-start(f32[2,128,128]{2,1,0:T(8,128)S(1)} %get-tuple-element.89), channel_id=1, source_target_pairs={{0,1},{1,2},{2,3},{3,4},{4,5},{5,6},{6,7},{8,9},{9,10},{10,11},{11... | collective-permute-start | bytes 393224 | tf_op jit(solution)/shard_map/ppermute | solution.py:17
  13.7 1.3 collective-permute-start.1
  15.0 0.6 fusion.110
  15.6 25.8 %collective-permute-done = f32[2,128,128]{2,1,0:T(8,128)S(1)} collective-permute-done((f32[2,128,128]{2,1,0:T(8,128)S(1)}, f32[2,128,128]{2,1,0:T(8,128)S(1)}, u32[]{:S(2)}, u32[]{:S(2)}) %collective-permute-start) | collective-permute-done | bytes 131104 | tf_op jit(solution)/shard_map/ppermute | solution.py:17
  41.9 0.3 copy-done
  42.2 0.4 copy-done.3
  43.6 0.2 fusion.106
  43.8 0.7 slice-done
  44.5 2.1 %fusion.1 = (f32[6,128,128]{2,1,0:T(8,128)}, f32[6,128,128]{2,1,0:T(8,128)S(1)}, f32[6,128,128]{2,1,0:T(8,128)}, f32[6,128,128]{2,1,0:T(8,128)S(1)}, f32[6,128,128]{2,1,0:T(8,128)S(1)}, /*index=5*/f32[6,128,128]{2,1,0:T(8,128)S(1)}) fusion(f32[5,128,128]{2,1,0:T(8,128)S(1)} %slice-done, f32[6,128,128]{2,1,0:T(8,128)S(1)} %get-tuple-element.26, f32[]{:T(128)} %bitcast.7, ...), kind=kLoop, calls=%fused_computation.17 | loop fusion | flops 2850816 | bytes 6541316 | tf_op jit(solution)/shard_map/add | solution.py:76
  46.6 1.6 %multiply_add_fusion.12 = (f32[6,128,128]{2,1,0:T(8,128)}, f32[6,128,128]{2,1,0:T(8,128)S(1)}) fusion(f32[6,128,127]{2,1,0:T(8,128)S(1)} %slice.663, f32[6,128,128]{2,1,0:T(8,128)S(1)} %get-tuple-element.40, f32[]{:T(128)} %bitcast.7, f32[2,128,128]{2,1,0:T(8,128)S(1)} %collective-permute-done.1, f32[2,128,128]{2,1,0:T(8,128)S(1)} %get-tuple-element.89, ...), kind=kLoop, calls=%fused_computation.71 | loop fusion | flops 1179648 | bytes 2746372 | tf_op jit(solution)/shard_map/add | solution.py:76
  48.3 3.5 %add_reduce_fusion = (f32[]{:T(128)}, f32[]{:T(128)}, f32[]{:T(128)}, f32[]{:T(128)}) fusion(f32[]{:T(128)} %bitcast.14, f32[]{:T(128)} %bitcast.13, f32[]{:T(128)} %bitcast.12, f32[]{:T(128)} %bitcast.7, f32[6,128,127]{2,1,0:T(8,128)S(1)} %bitcast.98, f32[6,128,128]{2,1,0:T(8,128)S(1)} %get-tuple-element.36, f32[6,127,128]{2,1,0:T(8,128)S(1)} %bitcast.99, ...), kind=kLoop, calls=%fused_computation.280 | loop fusion | flops 786428 | bytes 3002400 | tf_op jit(solution)/shard_map/reduce_max | solution.py:123
  51.7 22.3 %all-reduce.99 = (f32[]{:T(128)}, f32[]{:T(128)}, f32[]{:T(128)}, f32[]{:T(128)}) all-reduce(f32[]{:T(128)} %get-tuple-element.5, f32[]{:T(128)} %get-tuple-element.4, f32[]{:T(128)} %get-tuple-element.3, f32[]{:T(128)} %get-tuple-element.2), channel_id=1, replica_groups=mesh['copy'=2,'tm'=2,'space'=8] {'space'}, use_global_device_ids=true, to_apply=%region_1.2 | all-reduce | flops 4 | bytes 32 | tf_op jit(solution)/shard_map/pmax | solution.py:124
  75.5 1.0 slice.655
  76.5 2.2 %broadcast_divide_fusion.6 = (f32[4,128,128]{2,1,0:T(8,128)S(1)}, f32[4,128,128]{2,1,0:T(8,128)}, f32[4,128,128]{2,1,0:T(8,128)S(1)}) fusion(f32[]{:T(128)S(6)} %mul.815, f32[6,128,127]{2,1,0:T(8,128)} %bitcast.100, f32[6,128,128]{2,1,0:T(8,128)} %get-tuple-element.35, f32[6,127,128]{2,1,0:T(8,128)} %bitcast.101, f32[6,128,128]{2,1,0:T(8,128)} %get-tuple-element.37, ...), kind=kLoop, calls=%fused_computation.288 | loop fusion | flops 851968 | bytes 4909060 | tf_op jit(solution)/shard_map/div | solution.py:112
  78.7 0.7 slice.691
  79.5 0.8 slice.695
  80.3 0.7 slice.687
  81.0 2.0 %fusion.33 = (f32[4,128,128]{2,1,0:T(8,128)S(1)}, f32[4,128,128]{2,1,0:T(8,128)S(1)}, f32[4,128,128]{2,1,0:T(8,128)S(1)}) fusion(f32[4,128,128]{2,1,0:T(8,128)S(1)} %get-tuple-element.22, f32[3,128,128]{2,1,0:T(8,128)} %slice.687, f32[6,128,128]{2,1,0:T(8,128)S(1)} %get-tuple-element.32, f32[]{:T(128)} %bitcast.7, f32[6,128,128]{2,1,0:T(8,128)S(1)} %get-tuple-element.26, ...), kind=kLoop, calls=%fused_computation.96 | loop fusion | flops 1769472 | bytes 3338244 | tf_op jit(solution)/shard_map/add | solution.py:76
  83.3 1.7 %collective-permute-start.4 = (f32[2,128,128]{2,1,0:T(8,128)S(1)}, f32[2,128,128]{2,1,0:T(8,128)S(1)}, u32[]{:S(2)}, u32[]{:S(2)}) collective-permute-start(f32[2,128,128]{2,1,0:T(8,128)S(1)} %fusion.95), channel_id=1, source_target_pairs={{0,1},{1,2},{2,3},{3,4},{4,5},{5,6},{6,7},{8,9},{9,10},{10,11},{11... | collective-permute-start | bytes 393224 | tf_op jit(solution)/shard_map/ppermute | solution.py:17
  85.0 1.3 collective-permute-start.5
  87.6 4.2 %collective-permute-done.5 = f32[2,128,128]{2,1,0:T(8,128)S(1)} collective-permute-done((f32[2,128,128]{2,1,0:T(8,128)S(1)}, f32[2,128,128]{2,1,0:T(8,128)S(1)}, u32[]{:S(2)}, u32[]{:S(2)}) %collective-permute-start.5) | collective-permute-done | bytes 131104 | tf_op jit(solution)/shard_map/ppermute | solution.py:20
  92.1 1.0 fusion.5
  93.1 0.2 broadcast_divide_fusion.4
  93.5 0.9 fusion.37
  94.6 3.3 %collective-permute-start.6 = (f32[2,128,128]{2,1,0:T(8,128)S(1)}, f32[2,128,128]{2,1,0:T(8,128)S(1)}, u32[]{:S(2)}, u32[]{:S(2)}) collective-permute-start(f32[2,128,128]{2,1,0:T(8,128)S(1)} %fusion.91), channel_id=1, source_target_pairs={{0,1},{1,2},{2,3},{3,4},{4,5},{5,6},{6,7},{8,9},{9,10},{10,11},{11... | collective-permute-start | bytes 393224 | tf_op jit(solution)/shard_map/ppermute | solution.py:17
  97.9 1.3 collective-permute-start.7
  100.7 4.0 %collective-permute-done.7 = f32[2,128,128]{2,1,0:T(8,128)S(1)} collective-permute-done((f32[2,128,128]{2,1,0:T(8,128)S(1)}, f32[2,128,128]{2,1,0:T(8,128)S(1)}, u32[]{:S(2)}, u32[]{:S(2)}) %collective-permute-start.7) | collective-permute-done | bytes 131104 | tf_op jit(solution)/shard_map/ppermute | solution.py:20
  105.0 1.0 fusion.9
  106.0 0.2 broadcast_divide_fusion.2
  106.4 0.9 fusion.41
  107.5 2.8 %collective-permute-start.8 = (f32[2,128,128]{2,1,0:T(8,128)S(1)}, f32[2,128,128]{2,1,0:T(8,128)S(1)}, u32[]{:S(2)}, u32[]{:S(2)}) collective-permute-start(f32[2,128,128]{2,1,0:T(8,128)S(1)} %fusion.87), channel_id=1, source_target_pairs={{0,1},{1,2},{2,3},{3,4},{4,5},{5,6},{6,7},{8,9},{9,10},{10,11},{11... | collective-permute-start | bytes 393224 | tf_op jit(solution)/shard_map/ppermute | solution.py:17
  110.3 1.3 collective-permute-start.9
  112.9 4.3 %collective-permute-done.9 = f32[2,128,128]{2,1,0:T(8,128)S(1)} collective-permute-done((f32[2,128,128]{2,1,0:T(8,128)S(1)}, f32[2,128,128]{2,1,0:T(8,128)S(1)}, u32[]{:S(2)}, u32[]{:S(2)}) %collective-permute-start.9) | collective-permute-done | bytes 131104 | tf_op jit(solution)/shard_map/ppermute | solution.py:20
  117.5 1.0 fusion.13
  118.5 0.2 broadcast_divide_fusion
  118.9 0.9 fusion.45
  120.0 1.3 collective-permute-start.10
  121.3 1.0 collective-permute-done.10
  122.3 2.8 %collective-permute-start.11 = (f32[2,128,128]{2,1,0:T(8,128)S(1)}, f32[2,128,128]{2,1,0:T(8,128)S(1)}, u32[]{:S(2)}, u32[]{:S(2)}) collective-permute-start(f32[2,128,128]{2,1,0:T(8,128)S(1)} %broadcast_select_fusion), channel_id=1, source_target_pairs={{0,1},{1,2},{2,3},{3,4},{4,5},{5,6},{6,7},{8,9},{9,10},{10,11},{11... | collective-permute-start | bytes 393224 | tf_op jit(solution)/shard_map/ppermute | solution.py:17
  125.2 1.3 collective-permute-start.12
  126.5 1.9 %collective-permute-done.11 = f32[2,128,128]{2,1,0:T(8,128)S(1)} collective-permute-done((f32[2,128,128]{2,1,0:T(8,128)S(1)}, f32[2,128,128]{2,1,0:T(8,128)S(1)}, u32[]{:S(2)}, u32[]{:S(2)}) %collective-permute-start.11) | collective-permute-done | bytes 131104 | tf_op jit(solution)/shard_map/ppermute | solution.py:17
  128.4 4.1 %collective-permute-done.12 = f32[2,128,128]{2,1,0:T(8,128)S(1)} collective-permute-done((f32[2,128,128]{2,1,0:T(8,128)S(1)}, f32[2,128,128]{2,1,0:T(8,128)S(1)}, u32[]{:S(2)}, u32[]{:S(2)}) %collective-permute-start.12) | collective-permute-done | bytes 131104 | tf_op jit(solution)/shard_map/ppermute | solution.py:20
  132.8 1.0 fusion.17
  133.9 0.2 broadcast_divide_fusion.5
  134.3 0.9 fusion.49
  135.3 3.3 %collective-permute-start.13 = (f32[2,128,128]{2,1,0:T(8,128)S(1)}, f32[2,128,128]{2,1,0:T(8,128)S(1)}, u32[]{:S(2)}, u32[]{:S(2)}) collective-permute-start(f32[2,128,128]{2,1,0:T(8,128)S(1)} %fusion.79), channel_id=1, source_target_pairs={{0,1},{1,2},{2,3},{3,4},{4,5},{5,6},{6,7},{8,9},{9,10},{10,11},{11... | collective-permute-start | bytes 393224 | tf_op jit(solution)/shard_map/ppermute | solution.py:17
  138.6 1.3 collective-permute-start.14
  139.9 1.2 collective-permute-done.13
  141.1 4.4 %collective-permute-done.14 = f32[2,128,128]{2,1,0:T(8,128)S(1)} collective-permute-done((f32[2,128,128]{2,1,0:T(8,128)S(1)}, f32[2,128,128]{2,1,0:T(8,128)S(1)}, u32[]{:S(2)}, u32[]{:S(2)}) %collective-permute-start.14) | collective-permute-done | bytes 131104 | tf_op jit(solution)/shard_map/ppermute | solution.py:20
  145.8 1.0 fusion.21
  146.8 0.2 broadcast_divide_fusion.3
  147.2 0.9 fusion.53
  148.3 4.5 %collective-permute-start.15 = (f32[2,128,128]{2,1,0:T(8,128)S(1)}, f32[2,128,128]{2,1,0:T(8,128)S(1)}, u32[]{:S(2)}, u32[]{:S(2)}) collective-permute-start(f32[2,128,128]{2,1,0:T(8,128)S(1)} %fusion.75), channel_id=1, source_target_pairs={{0,1},{1,2},{2,3},{3,4},{4,5},{5,6},{6,7},{8,9},{9,10},{10,11},{11... | collective-permute-start | bytes 393224 | tf_op jit(solution)/shard_map/ppermute | solution.py:17
  152.8 1.3 collective-permute-start.16
  154.1 1.3 collective-permute-done.15
  155.4 4.3 %collective-permute-done.16 = f32[2,128,128]{2,1,0:T(8,128)S(1)} collective-permute-done((f32[2,128,128]{2,1,0:T(8,128)S(1)}, f32[2,128,128]{2,1,0:T(8,128)S(1)}, u32[]{:S(2)}, u32[]{:S(2)}) %collective-permute-start.16) | collective-permute-done | bytes 131104 | tf_op jit(solution)/shard_map/ppermute | solution.py:20
  160.0 1.0 fusion.25
  161.0 0.2 broadcast_divide_fusion.1
  161.4 0.9 fusion.57
  162.3 0.8 fusion.71
  (101 shorter events, 4.8 us)
Async XLA Ops:
  0.6 14.3 %copy-start.8 = (f32[1,4]{1,0:T(1,128)S(1)}, f32[1,4]{1,0:T(1,128)}, u32[]{:S(2)}) copy-start(f32[1,4]{1,0:T(1,128)} %param.11) | copy-start | bytes 52
  1.7 39.9 %copy-start.5 = (f32[1,2,128,128]{3,2,1,0:T(8,128)}, f32[1,2,128,128]{3,2,1,0:T(8,128)S(1)}, u32[]{:S(2)}) copy-start(f32[1,2,128,128]{3,2,1,0:T(8,128)S(1)} %get-tuple-element.88) | copy-start | bytes 393220
  1.8 39.9 %copy-start.2 = (f32[3,2,128,128]{3,2,1,0:T(8,128)S(1)}, f32[3,2,128,128]{3,2,1,0:T(8,128)}, u32[]{:S(2)}) copy-start(f32[3,2,128,128]{3,2,1,0:T(8,128)} %param.9) | copy-start | bytes 1179652
  2.9 38.8 %collective-permute-start.2 = (f32[5,2,128,128]{3,2,1,0:T(8,128)S(1)}, f32[5,2,128,128]{3,2,1,0:T(8,128)S(1)}, u32[]{:S(2)}, u32[]{:S(2)}) collective-permute-start(f32[5,2,128,128]{3,2,1,0:T(8,128)S(1)} %pad_maximum_fusion.1), channel_id=1, source_target_pairs={{0,1},{1,2},{2,3},{3,4},{4,5},{5,6},{6,7},{8,9},{9,10},{10,11},{11... | collective-permute-start | bytes 1966088 | tf_op jit(solution)/shard_map/ppermute | solution.py:17
  7.8 33.9 %collective-permute-start.3 = (f32[5,2,128,128]{3,2,1,0:T(8,128)S(1)}, f32[5,2,128,128]{3,2,1,0:T(8,128)S(1)}, u32[]{:S(2)}, u32[]{:S(2)}) collective-permute-start(f32[5,2,128,128]{3,2,1,0:T(8,128)S(1)} %pad_maximum_fusion.1), channel_id=1, source_target_pairs={{1,0},{2,1},{3,2},{4,3},{5,4},{6,5},{7,6},{9,8},{10,9},{11,10},{12... | collective-permute-start | bytes 1966088 | tf_op jit(solution)/shard_map/ppermute | solution.py:20
  9.1 32.3 %collective-permute-start = (f32[2,128,128]{2,1,0:T(8,128)S(1)}, f32[2,128,128]{2,1,0:T(8,128)S(1)}, u32[]{:S(2)}, u32[]{:S(2)}) collective-permute-start(f32[2,128,128]{2,1,0:T(8,128)S(1)} %get-tuple-element.89), channel_id=1, source_target_pairs={{0,1},{1,2},{2,3},{3,4},{4,5},{5,6},{6,7},{8,9},{9,10},{10,11},{11... | collective-permute-start | bytes 393224 | tf_op jit(solution)/shard_map/ppermute | solution.py:17
  13.7 27.7 %collective-permute-start.1 = (f32[2,128,128]{2,1,0:T(8,128)S(1)}, f32[2,128,128]{2,1,0:T(8,128)S(1)}, u32[]{:S(2)}, u32[]{:S(2)}) collective-permute-start(f32[2,128,128]{2,1,0:T(8,128)S(1)} %get-tuple-element.89), channel_id=1, source_target_pairs={{1,0},{2,1},{3,2},{4,3},{5,4},{6,5},{7,6},{9,8},{10,9},{11,10},{12... | collective-permute-start | bytes 393224 | tf_op jit(solution)/shard_map/ppermute | solution.py:20
  41.4 0.7 copy-start
  41.6 0.9 copy-start.3
  41.7 1.0 copy-start.4
  43.5 1.0 slice-start
  48.3 28.2 %copy-start.1 = (f32[6,128,128]{2,1,0:T(8,128)S(1)}, f32[6,128,128]{2,1,0:T(8,128)}, u32[]{:S(2)}) copy-start(f32[6,128,128]{2,1,0:T(8,128)} %copy-done) | copy-start | bytes 1179652
  81.0 2.1 %copy-start.6 = (f32[4,128,128]{2,1,0:T(8,128)S(1)}, f32[4,128,128]{2,1,0:T(8,128)}, u32[]{:S(2)}) copy-start(f32[4,128,128]{2,1,0:T(8,128)} %get-tuple-element.23) | copy-start | bytes 786436
  83.3 4.3 %collective-permute-start.4 = (f32[2,128,128]{2,1,0:T(8,128)S(1)}, f32[2,128,128]{2,1,0:T(8,128)S(1)}, u32[]{:S(2)}, u32[]{:S(2)}) collective-permute-start(f32[2,128,128]{2,1,0:T(8,128)S(1)} %fusion.95), channel_id=1, source_target_pairs={{0,1},{1,2},{2,3},{3,4},{4,5},{5,6},{6,7},{8,9},{9,10},{10,11},{11... | collective-permute-start | bytes 393224 | tf_op jit(solution)/shard_map/ppermute | solution.py:17
  85.0 6.9 %collective-permute-start.5 = (f32[2,128,128]{2,1,0:T(8,128)S(1)}, f32[2,128,128]{2,1,0:T(8,128)S(1)}, u32[]{:S(2)}, u32[]{:S(2)}) collective-permute-start(f32[2,128,128]{2,1,0:T(8,128)S(1)} %fusion.95), channel_id=1, source_target_pairs={{1,0},{2,1},{3,2},{4,3},{5,4},{6,5},{7,6},{9,8},{10,9},{11,10},{12... | collective-permute-start | bytes 393224 | tf_op jit(solution)/shard_map/ppermute | solution.py:20
  94.6 6.1 %collective-permute-start.6 = (f32[2,128,128]{2,1,0:T(8,128)S(1)}, f32[2,128,128]{2,1,0:T(8,128)S(1)}, u32[]{:S(2)}, u32[]{:S(2)}) collective-permute-start(f32[2,128,128]{2,1,0:T(8,128)S(1)} %fusion.91), channel_id=1, source_target_pairs={{0,1},{1,2},{2,3},{3,4},{4,5},{5,6},{6,7},{8,9},{9,10},{10,11},{11... | collective-permute-start | bytes 393224 | tf_op jit(solution)/shard_map/ppermute | solution.py:17
  97.9 6.9 %collective-permute-start.7 = (f32[2,128,128]{2,1,0:T(8,128)S(1)}, f32[2,128,128]{2,1,0:T(8,128)S(1)}, u32[]{:S(2)}, u32[]{:S(2)}) collective-permute-start(f32[2,128,128]{2,1,0:T(8,128)S(1)} %fusion.91), channel_id=1, source_target_pairs={{1,0},{2,1},{3,2},{4,3},{5,4},{6,5},{7,6},{9,8},{10,9},{11,10},{12... | collective-permute-start | bytes 393224 | tf_op jit(solution)/shard_map/ppermute | solution.py:20
  107.5 5.4 %collective-permute-start.8 = (f32[2,128,128]{2,1,0:T(8,128)S(1)}, f32[2,128,128]{2,1,0:T(8,128)S(1)}, u32[]{:S(2)}, u32[]{:S(2)}) collective-permute-start(f32[2,128,128]{2,1,0:T(8,128)S(1)} %fusion.87), channel_id=1, source_target_pairs={{0,1},{1,2},{2,3},{3,4},{4,5},{5,6},{6,7},{8,9},{9,10},{10,11},{11... | collective-permute-start | bytes 393224 | tf_op jit(solution)/shard_map/ppermute | solution.py:17
  110.3 6.9 %collective-permute-start.9 = (f32[2,128,128]{2,1,0:T(8,128)S(1)}, f32[2,128,128]{2,1,0:T(8,128)S(1)}, u32[]{:S(2)}, u32[]{:S(2)}) collective-permute-start(f32[2,128,128]{2,1,0:T(8,128)S(1)} %fusion.87), channel_id=1, source_target_pairs={{1,0},{2,1},{3,2},{4,3},{5,4},{6,5},{7,6},{9,8},{10,9},{11,10},{12... | collective-permute-start | bytes 393224 | tf_op jit(solution)/shard_map/ppermute | solution.py:20
  120.0 13.8 %copy-start.7 = (f32[2,128,128]{2,1,0:T(8,128)}, f32[2,128,128]{2,1,0:T(8,128)S(1)}, u32[]{:S(2)}) copy-start(f32[2,128,128]{2,1,0:T(8,128)S(1)} %fusion.83) | copy-start | bytes 393220
  120.0 2.3 %collective-permute-start.10 = (f32[2,128,128]{2,1,0:T(8,128)S(1)}, f32[2,128,128]{2,1,0:T(8,128)S(1)}, u32[]{:S(2)}, u32[]{:S(2)}) collective-permute-start(f32[2,128,128]{2,1,0:T(8,128)S(1)} %fusion.83), channel_id=1, source_target_pairs={{0,8},{1,9},{2,10},{3,11},{4,12},{5,13},{6,14},{7,15},{16,24},{17,... | collective-permute-start | bytes 393224 | tf_op jit(solution)/shard_map/ppermute | solution.py:28
  122.3 6.1 %collective-permute-start.11 = (f32[2,128,128]{2,1,0:T(8,128)S(1)}, f32[2,128,128]{2,1,0:T(8,128)S(1)}, u32[]{:S(2)}, u32[]{:S(2)}) collective-permute-start(f32[2,128,128]{2,1,0:T(8,128)S(1)} %broadcast_select_fusion), channel_id=1, source_target_pairs={{0,1},{1,2},{2,3},{3,4},{4,5},{5,6},{6,7},{8,9},{9,10},{10,11},{11... | collective-permute-start | bytes 393224 | tf_op jit(solution)/shard_map/ppermute | solution.py:17
  125.2 7.4 %collective-permute-start.12 = (f32[2,128,128]{2,1,0:T(8,128)S(1)}, f32[2,128,128]{2,1,0:T(8,128)S(1)}, u32[]{:S(2)}, u32[]{:S(2)}) collective-permute-start(f32[2,128,128]{2,1,0:T(8,128)S(1)} %broadcast_select_fusion), channel_id=1, source_target_pairs={{1,0},{2,1},{3,2},{4,3},{5,4},{6,5},{7,6},{9,8},{10,9},{11,10},{12... | collective-permute-start | bytes 393224 | tf_op jit(solution)/shard_map/ppermute | solution.py:20
  135.3 5.8 %collective-permute-start.13 = (f32[2,128,128]{2,1,0:T(8,128)S(1)}, f32[2,128,128]{2,1,0:T(8,128)S(1)}, u32[]{:S(2)}, u32[]{:S(2)}) collective-permute-start(f32[2,128,128]{2,1,0:T(8,128)S(1)} %fusion.79), channel_id=1, source_target_pairs={{0,1},{1,2},{2,3},{3,4},{4,5},{5,6},{6,7},{8,9},{9,10},{10,11},{11... | collective-permute-start | bytes 393224 | tf_op jit(solution)/shard_map/ppermute | solution.py:17
  138.6 6.9 %collective-permute-start.14 = (f32[2,128,128]{2,1,0:T(8,128)S(1)}, f32[2,128,128]{2,1,0:T(8,128)S(1)}, u32[]{:S(2)}, u32[]{:S(2)}) collective-permute-start(f32[2,128,128]{2,1,0:T(8,128)S(1)} %fusion.79), channel_id=1, source_target_pairs={{1,0},{2,1},{3,2},{4,3},{5,4},{6,5},{7,6},{9,8},{10,9},{11,10},{12... | collective-permute-start | bytes 393224 | tf_op jit(solution)/shard_map/ppermute | solution.py:20
  148.3 7.1 %collective-permute-start.15 = (f32[2,128,128]{2,1,0:T(8,128)S(1)}, f32[2,128,128]{2,1,0:T(8,128)S(1)}, u32[]{:S(2)}, u32[]{:S(2)}) collective-permute-start(f32[2,128,128]{2,1,0:T(8,128)S(1)} %fusion.75), channel_id=1, source_target_pairs={{0,1},{1,2},{2,3},{3,4},{4,5},{5,6},{6,7},{8,9},{9,10},{10,11},{11... | collective-permute-start | bytes 393224 | tf_op jit(solution)/shard_map/ppermute | solution.py:17
  152.8 6.9 %collective-permute-start.16 = (f32[2,128,128]{2,1,0:T(8,128)S(1)}, f32[2,128,128]{2,1,0:T(8,128)S(1)}, u32[]{:S(2)}, u32[]{:S(2)}) collective-permute-start(f32[2,128,128]{2,1,0:T(8,128)S(1)} %fusion.75), channel_id=1, source_target_pairs={{1,0},{2,1},{3,2},{4,3},{5,4},{6,5},{7,6},{9,8},{10,9},{11,10},{12... | collective-permute-start | bytes 393224 | tf_op jit(solution)/shard_map/ppermute | solution.py:20
where the time goes:
time: 164 us; the launch traced here: 163 us
  waiting for transfers between devices  56.4 us (34%)
  starting transfers between devices  39.5 us (24%)
  other arithmetic  28.7 us (18%)
  blocking collectives  22.3 us (14%)
  local copies, waits for them, and re-layouts  8.9 us (5%)
  between operations  7.29 us (4%)
    ppermute x8, waiting for transfers between devices, extended(): lax.ppermute(lax.slice_in_dim(block, block.shape[dim] - width, None, axis...  30.2 us
    ppermute x8, starting transfers between devices, extended(): lax.ppermute(lax.slice_in_dim(block, block.shape[dim] - width, None, axis...  27.9 us
    ppermute x8, waiting for transfers between devices, extended(): lax.ppermute(lax.slice_in_dim(block, 0, width, axis=dim), axis, backward)  25.3 us
    pmax x1, blocking collectives, shards(): bound_row.append(lax.pmax(local, 'space'))  22.3 us
    add x15, other arithmetic, operate(): conduct * (values - neighbor)  17.3 us
    ppermute x8, starting transfers between devices, extended(): lax.ppermute(lax.slice_in_dim(block, 0, width, axis=dim), axis, backward)  10.3 us
    slice x51, local copies, waits for them, and re-layouts, ahead(): tail = lax.slice_in_dim(values, 1, length, axis=direction)  6.02 us
    div x7, other arithmetic, advance(): update = residual / theta  3.55 us
  transfers between devices with their start and end apart: 17, of which 11 were waited for; matrix products, arithmetic and copies ran while one was open for 1% of the time, Pallas kernels for 0%

commit v1 on v0

v1 whole, which is shorter than its diff:
```python
import functools

import jax
import jax.numpy as jnp
from jax import lax
from jax.experimental import pallas as pl
from jax.experimental.pallas import tpu as pltpu
from jax.sharding import PartitionSpec as P

FINE = 4
LOW = 2 * FINE
lower_bound = 0.5
AXES = ("copy", "tm", "space")
VMEM = pl.BlockSpec(memory_space=pltpu.VMEM)
SMEM = pl.BlockSpec(memory_space=pltpu.SMEM)


def windows(values, place, rows, width):
    total, lanes = values.shape
    start = rows * place - LOW
    first, last = max(start, 0), min(start + width, total)
    parts = []
    if first > start:
        parts.append(jnp.zeros((first - start, lanes), values.dtype))
    parts.append(values[first:last])
    if last < start + width:
        parts.append(jnp.zeros((start + width - last, lanes), values.dtype))
    return jnp.concatenate(parts, axis=0) if len(parts) > 1 else parts[0]


def pack_shared(rows, width, info, diffusion, wind, buildings, out):
    first = info[0] == 0
    for layer in range(diffusion.shape[0]):
        masked = diffusion[layer] * (1 - buildings[layer]).astype(jnp.float32)
        pair = (
            jnp.where(first, masked, wind[1, layer]),
            jnp.where(first, wind[0, layer], wind[2, layer]),
        )
        for field in range(2):
            for place in range(out.shape[0]):
                out[place, field, layer] = windows(pair[field], place, rows, width)


def roll_back(values, axis):
    return pltpu.roll(values, values.shape[axis] - 1, axis)


def face_kernel(rows, width, info, rates, mine, other, initial, source, buildings, *outs):
    faces, packed = outs[:6], outs[6]
    count, layers = mine.shape[0], mine.shape[2]
    total = count * layers
    lanes = mine.shape[-1]
    first = info[0] == 0
    row = lax.broadcasted_iota(jnp.int32, (width, lanes), 0)
    lane = lax.broadcasted_iota(jnp.int32, (width, lanes), 1)
    inner_row = row < width - 1
    inner_lane = lane < lanes - 1
    zero = jnp.zeros((width, lanes), jnp.float32)

    def fields(place):
        spot, layer = place // layers, place % layers
        here = (mine[spot, 0, layer], mine[spot, 1, layer])
        there = (other[spot, 0, layer], other[spot, 1, layer])
        masked = jnp.where(first, here[0], there[0])
        wind_x = jnp.where(first, here[1], there[1])
        wind_y = jnp.where(first, there[0], here[0])
        wind_z = jnp.where(first, there[1], here[1])
        return masked, wind_x, wind_y, wind_z

    def body(place, carry):
        masked, wind_x, wind_y, wind_z, low_conduct, low_speed, peaks = carry
        following = fields(jnp.minimum(place + 1, total - 1))
        inside = place < total - 1
        next_masked = jnp.where(inside, following[0], zero)
        opened = jnp.where(masked > 0.0, 1.0, 0.0)

        def face(masked_ahead, wind_here, wind_ahead, keep):
            conduct = jnp.sqrt(masked * masked_ahead)
            speed = 0.5 * (wind_here + wind_ahead) * opened * jnp.where(masked_ahead > 0.0, 1.0, 0.0)
            if keep is not None:
                conduct, speed = jnp.where(keep, conduct, 0.0), jnp.where(keep, speed, 0.0)
            return conduct, speed

        along_x = face(next_masked, wind_x, following[1], None)
        along_y = face(roll_back(masked, 0), wind_y, roll_back(wind_y, 0), inner_row)
        along_z = face(roll_back(masked, 1), wind_z, roll_back(wind_z, 1), inner_lane)
        for number, value in enumerate(along_x + along_y + along_z):
            faces[number][place] = value
        speeds = [jnp.abs(pair[1]) for pair in (along_x, along_y, along_z)]
        conduct_sum = (
            along_x[0]
            + low_conduct
            + along_y[0]
            + pltpu.roll(along_y[0], 1, 0)
            + along_z[0]
            + pltpu.roll(along_z[0], 1, 1)
        )
        speed_sum = (
            speeds[0]
            + low_speed
            + speeds[1]
            + pltpu.roll(speeds[1], 1, 0)
            + speeds[2]
            + pltpu.roll(speeds[2], 1, 1)
        )
        still = (1.0 + 2.0 * conduct_sum)[LOW : LOW + rows]
        speed_sum = speed_sum[LOW : LOW + rows]
        peaks = tuple(jnp.maximum(peaks[k], still + rates[0, k] * speed_sum) for k in range(FINE))
        return next_masked, *following[1:], along_x[0], speeds[0], peaks

    start = (*fields(0), zero, zero, (jnp.zeros((rows, lanes), jnp.float32),) * FINE)
    peaks = lax.fori_loop(0, total, body, start)[-1]
    bounds = jnp.zeros((8, lanes), jnp.float32)
    place = lax.broadcasted_iota(jnp.int32, (8, lanes), 0)
    for k in range(FINE):
        bounds = jnp.where(place == k, jnp.max(peaks[k]), bounds)
    for layer in range(layers):
        opened = (1 - buildings[layer]).astype(jnp.float32)
        state = initial[0, layer] * opened
        forcing = source[0, layer].astype(jnp.float32) * opened
        for spot in range(count):
            packed[spot, pl.ds(layer * width, width)] = windows(state, spot, rows, width)
            packed[spot, pl.ds((layers + layer) * width, width)] = windows(forcing, spot, rows, width)
    for spot in range(count):
        packed[spot, pl.ds(2 * layers * width, 8)] = bounds


def coefficients(bound):
    theta = (bound + lower_bound) * 0.5
    delta = (bound - lower_bound) * 0.5
    sigma = theta / delta
    rho_one = 1.0 / sigma
    rho_two = 1.0 / (2.0 * sigma - rho_one)
    beta = 2.0 * rho_two / (delta * theta)
    alpha = (1.0 + rho_one * rho_two) / theta + 2.0 * rho_two / delta
    return alpha - beta, beta


def one_step(total, width, layers, state, residual, ahead, faces, packed, rate, near, far):
    lanes = state.shape[-1]
    zero = jnp.zeros((width, lanes), jnp.float32)

    def difference(place, values, values_ahead, low_flow, pairs):
        flow_x = pairs[0] * values + pairs[1] * values_ahead
        flow_y = pairs[2] * values + pairs[3] * roll_back(values, 0)
        flow_z = pairs[4] * values + pairs[5] * roll_back(values, 1)
        change = (flow_x - low_flow) + (flow_y - pltpu.roll(flow_y, 1, 0)) + (flow_z - pltpu.roll(flow_z, 1, 1))
        return change, flow_x

    def first_sweep(place, carry):
        values, low_flow = carry
        values_ahead = state[place + 1]
        pairs = []
        for dim in range(3):
            conduct, speed = faces[2 * dim][place], faces[2 * dim + 1][place]
            pairs.append(conduct + rate * jnp.maximum(speed, 0.0))
            pairs.append(rate * jnp.minimum(speed, 0.0) - conduct)
        for number in range(6):
            ahead[number, place] = pairs[number]
        change, low_flow = difference(place, values, values_ahead, low_flow, pairs)
        spot, layer = place // layers, place % layers
        offset = pl.multiple_of((layers + layer) * width, 8)
        residual[place] = packed[spot, pl.ds(offset, width)] - change
        return values_ahead, low_flow

    def second_sweep(place, carry):
        values, low_flow = carry
        values_ahead = residual[place + 1]
        pairs = [ahead[number, place] for number in range(6)]
        change, low_flow = difference(place, values, values_ahead, low_flow, pairs)
        state[place] = state[place] + (near * values - far * change)
        return values_ahead, low_flow

    lax.fori_loop(0, total, first_sweep, (state[0], zero), unroll=2)
    lax.fori_loop(0, total, second_sweep, (residual[0], zero), unroll=2)


def bounds_of(packed, layers, width):
    bounds = packed[0, pl.ds(2 * layers * width, 8)]
    for spot in range(1, packed.shape[0]):
        bounds = jnp.maximum(bounds, packed[spot, pl.ds(2 * layers * width, 8)])
    return bounds


def first_kernel(rows, width, layers, info, rates, packed, *refs):
    faces, (advanced, third, edge_one, edge_two), (state, residual, ahead) = refs[:6], refs[6:10], refs[10:]
    count = packed.shape[0]
    total = count * layers
    zero = jnp.zeros(state.shape[1:], jnp.float32)
    state[total] = zero
    residual[total] = zero
    for spot in range(count):
        for layer in range(layers):
            state[spot * layers + layer] = packed[spot, pl.ds(layer * width, width)]
    bounds = bounds_of(packed, layers, width)
    for k in range(FINE):
        near, far = coefficients(bounds[k : k + 1])
        one_step(total, width, layers, state, residual, ahead, faces, packed, rates[0, k], near, far)
        if k == FINE - 2:
            third[...] = state[:total, LOW : LOW + rows]
    advanced[...] = state[:total, LOW : LOW + rows]
    edge = min(rows, LOW)
    low, high = state[:total, LOW : LOW + edge], state[:total, LOW + rows - edge : LOW + rows]
    even = info[1] % 2 == 0
    edge_one[...] = jnp.where(even, high, low)
    edge_two[...] = jnp.where(even, low, high)


def second_kernel(rows, width, layers, info, rates, packed, own, halo_one, halo_two, advanced, third, *refs):
    faces, out, (state, residual, ahead) = refs[:6], refs[6], refs[7:]
    total = state.shape[0] - 1
    zero = jnp.zeros(state.shape[1:], jnp.float32)
    state[total] = zero
    residual[total] = zero
    swap = info[2] == 1
    below, above = halo_one[...], halo_two[...]
    low = jnp.where(swap, above, below)
    high = jnp.where(swap, below, above)
    state[:total, :LOW] = jnp.where(info[3] == 1, low, 0.0)
    state[:total, LOW : LOW + rows] = own[...]
    state[:total, LOW + rows : 2 * LOW + rows] = jnp.where(info[4] == 1, high, 0.0)
    if width > 2 * LOW + rows:
        state[:total, 2 * LOW + rows :] = jnp.zeros((total, width - 2 * LOW - rows, state.shape[-1]), jnp.float32)
    bounds = bounds_of(packed, layers, width)
    for k in range(FINE - 1):
        near, far = coefficients(bounds[k : k + 1])
        one_step(total, width, layers, state, residual, ahead, faces, packed, rates[0, k], near, far)
    first = info[0] == 0
    final = jnp.where(first, third[...], state[:total, LOW : LOW + rows])
    shape = out.shape[0:1] + out.shape[2:]
    out[:, 0] = advanced[...].reshape(shape)
    out[:, 1] = final.reshape(shape)


def swapped(array, sizes, partner):
    copies, blocks, count = sizes
    pairs = []
    for c in range(copies):
        for t in range(blocks):
            for s in range(count):
                target = partner(t, s)
                if target is not None:
                    pairs.append(((c * blocks + t) * count + s, (c * blocks + target[0]) * count + target[1]))
    return lax.ppermute(array, AXES, pairs)


def halos(edge_one, edge_two, advanced, sizes, rows, place):
    copies, blocks, count = sizes
    even = place % 2 == 0
    below, above = place > 0, place < count - 1
    if rows >= LOW and blocks == 2 and count % 2 == 0:
        one = swapped(edge_one, sizes, lambda t, s: (1 - t, s ^ 1))
        two = swapped(edge_two, sizes, lambda t, s: (1 - t, ((s + 1) ^ 1) - 1 if 0 < s < count - 1 else s))
        return one, two, even, below, above

    def shifted(values, by):
        return swapped(
            values, sizes, lambda t, s: (t + 1, s + by) if t + 1 < blocks and 0 <= s + by < count else None
        )

    reach = -(-LOW // rows)
    low = jnp.concatenate([shifted(advanced, by) for by in range(reach, 0, -1)], axis=1)[:, -LOW:]
    high = jnp.concatenate([shifted(advanced, -by) for by in range(1, reach + 1)], axis=1)[:, :LOW]
    return low, high, False, True, True


def shards(sizes, initial, source, diffusion, wind_field, buildings, strength):
    copies, blocks, count = sizes
    layers, depth, lanes = diffusion.shape
    total, rows = layers * count, depth // count
    width = -(-(rows + 2 * LOW) // 8) * 8
    block, place = lax.axis_index("tm"), lax.axis_index("space")
    params = pltpu.CompilerParams(vmem_limit_bytes=48 * 1024 * 1024)

    def struct(*shape):
        return jax.ShapeDtypeStruct(shape, jnp.float32)

    half = block % 2
    info = jnp.stack([half, place]).astype(jnp.int32)
    shared = pl.pallas_call(
        functools.partial(pack_shared, rows, width),
        out_shape=struct(count, 2, layers, width, lanes),
        in_specs=[SMEM] + [VMEM] * 3,
        out_specs=VMEM,
        compiler_params=params,
        name="pack_shared",
    )(info, diffusion, wind_field, buildings)
    mine = lax.all_to_all(shared, "space", 0, 0, tiled=True)
    other = swapped(mine, sizes, lambda t, s: (t ^ 1, s))

    out_shape = [struct(total, width, lanes)] * 6 + [struct(count, 2 * layers * width + 8, lanes)]
    *faces, packed = pl.pallas_call(
        functools.partial(face_kernel, rows, width),
        out_shape=out_shape,
        in_specs=[SMEM] * 2 + [VMEM] * 5,
        out_specs=[VMEM] * 7,
        compiler_params=params,
        name="faces",
    )(info, strength, mine, other, initial, source, buildings)
    packed = lax.all_to_all(packed, "space", 0, 0, tiled=True)

    edge = min(rows, LOW)
    scratch = [
        pltpu.VMEM((total + 1, width, lanes), jnp.float32),
        pltpu.VMEM((total + 1, width, lanes), jnp.float32),
        pltpu.VMEM((6, total, width, lanes), jnp.float32),
    ]
    advanced, third, edge_one, edge_two = pl.pallas_call(
        functools.partial(first_kernel, rows, width, layers),
        out_shape=[struct(total, rows, lanes)] * 2 + [struct(total, edge, lanes)] * 2,
        in_specs=[SMEM] * 2 + [VMEM] * 7,
        out_specs=[VMEM] * 4,
        scratch_shapes=scratch,
        compiler_params=params,
        name="four_steps",
    )(info, strength, packed, *faces)

    if blocks == 2:
        own = swapped(advanced, sizes, lambda t, s: (1 - t, s))
    else:
        own = swapped(advanced, sizes, lambda t, s: (t + 1, s) if t + 1 < blocks else None)
    one, two, swap, below, above = halos(edge_one, edge_two, advanced, sizes, rows, place)
    flags = [block, place, swap, below, above]
    info = jnp.stack([jnp.asarray(flag).astype(jnp.int32) for flag in flags])
    result = pl.pallas_call(
        functools.partial(second_kernel, rows, width, layers),
        out_shape=struct(count, 2, layers, rows, lanes),
        in_specs=[SMEM] * 2 + [VMEM] * 12,
        out_specs=VMEM,
        scratch_shapes=scratch,
        compiler_params=params,
        name="three_steps",
    )(info, strength, packed, own, one, two, advanced, third, *faces)
    result = lax.all_to_all(result, "space", 0, 0, tiled=True)
    result = result.transpose(1, 2, 0, 3, 4).reshape(2, 1, layers, depth, lanes)
    return result[0], result[1]


def solution(mesh):
    sizes = tuple(mesh.shape[axis] for axis in AXES)
    in_specs = (
        P(("copy", "tm"), "space", None, None),
        P(("copy", "tm"), "space", None, None),
        P("space", None, None),
        P(None, "space", None, None),
        P("space", None, None),
        P("tm", None),
    )
    out_specs = (P(("copy", "tm"), "space", None, None), P(("copy", "tm"), "space", None, None))
    return jax.shard_map(
        functools.partial(shards, sizes), mesh=mesh, in_specs=in_specs, out_specs=out_specs, check_vma=False
    )
```

time: 164 us -> 88.1 us (0.54)
  waiting for transfers between devices: 56.4 us -> 4.84 us
  starting transfers between devices: 39.5 us -> 0.95 us
  blocking collectives: 22.3 us -> 55.1 us
  other arithmetic: 28.7 us -> 0.08 us
  Pallas kernels: 0 us -> 21.8 us
  between operations: 7.29 us -> 0.72 us
  local copies, waits for them, and re-layouts: 8.9 us -> 4.25 us
    all_to_all x0 -> x3, blocking collectives: none -> 55.1 us  [the longest x1 21.7 us: shards(): mine = lax.all_to_all(shared, 'space', 0, 0, tiled=True)]
    ppermute x17 -> x4, waiting for transfers between devices: 56.4 us -> 4.84 us  [swapped(): return lax.ppermute(array, AXES, pairs)]
    ppermute x17 -> x4, starting transfers between devices: 39.5 us -> 0.95 us  [swapped(): return lax.ppermute(array, AXES, pairs)]
    pmax x1 -> x0, blocking collectives: 22.3 us -> none  [shards(): bound_row.append(lax.pmax(local, 'space'))]
    pallas_call x0 -> x4, Pallas kernels: none -> 21.8 us  [the longest x1 10.3 us: shards(): pl.pallas_call(functools.partial(first_kernel, rows, width, layers), out_...]
    add x21 -> x0, other arithmetic: 18 us -> none  [the longest x15 17.3 us: operate(): conduct * (values - neighbor)]
    slice x68 -> x3, local copies, waits for them, and re-layouts: 7.95 us -> 1.35 us  [shards(): return (result[0], result[1])]
    div x7 -> x0, other arithmetic: 3.55 us -> none  [advance(): update = residual / theta]
  transfers between devices with their start and end apart: 17 -> 4, of which waited for: 11 -> 2; matrix products, arithmetic and copies ran while one was open for 1% -> 0% of each run, Pallas kernels for 0% -> 0%
where the time goes in v1:
time: 88.1 us; the launch traced here: 87.7 us
  blocking collectives  55.1 us (63%)
  Pallas kernels  21.8 us (25%)
  waiting for transfers between devices  4.84 us (5%)
  local copies, waits for them, and re-layouts  4.25 us (5%)
  starting transfers between devices  0.95 us (1%)
    all_to_all x1, blocking collectives, shards(): mine = lax.all_to_all(shared, 'space', 0, 0, tiled=True)  21.7 us
    all_to_all x1, blocking collectives, shards(): packed = lax.all_to_all(packed, 'space', 0, 0, tiled=True)  19.6 us
    all_to_all x1, blocking collectives, shards(): result = lax.all_to_all(result, 'space', 0, 0, tiled=True)  13.7 us
    pallas_call x1, Pallas kernels, shards(): pl.pallas_call(functools.partial(first_kernel, rows, width, layers), out_...  10.3 us
    pallas_call x1, Pallas kernels, shards(): pl.pallas_call(functools.partial(second_kernel, rows, width, layers), out...  7.84 us
    ppermute x4, waiting for transfers between devices, swapped(): return lax.ppermute(array, AXES, pairs)  4.84 us
    pallas_call x1, Pallas kernels, shards(): pl.pallas_call(functools.partial(face_kernel, rows, width), out_shape=out...  3.15 us
    unnamed x12, local copies, waits for them, and re-layouts  2.82 us
  transfers between devices with their start and end apart: 4, of which 2 were waited for; matrix products, arithmetic and copies ran while one was open for 0% of the time, Pallas kernels for 0%

profile of v1, /device:TPU:0, one launch (start us, length us, event | category | flops | bytes accessed | tf_op | source)
XLA Modules:
  0.0 87.7 jit_solution(3840828490327086179)
XLA Ops:
  0.6 0.1 pad_add_fusion.info
  0.7 0.0 copy-start
  0.7 0.9 %copy-done = s32[2,128,128]{2,1,0:T(8,128)S(1)} copy-done((s32[2,128,128]{2,1,0:T(8,128)S(1)}, s32[2,128,128]{2,1,0:T(8,128)}, u32[]{:S(2)}) %copy-start) | copy-done | bytes 131096
  1.6 0.0 copy-start.1
  1.6 1.0 %copy-done.1 = f32[3,2,128,128]{3,2,1,0:T(8,128)S(1)} copy-done((f32[3,2,128,128]{3,2,1,0:T(8,128)S(1)}, f32[3,2,128,128]{3,2,1,0:T(8,128)}, u32[]{:S(2)}) %copy-start.1) | copy-done | bytes 393240
  2.6 0.0 copy-start.2
  2.6 0.9 %copy-done.2 = f32[2,128,128]{2,1,0:T(8,128)S(1)} copy-done((f32[2,128,128]{2,1,0:T(8,128)S(1)}, f32[2,128,128]{2,1,0:T(8,128)}, u32[]{:S(2)}) %copy-start.2) | copy-done | bytes 131096
  3.5 0.6 pack_shared.1
  4.1 0.0 copy-start.3
  4.1 0.0 copy-start.4
  4.1 0.0 copy-start.5
  4.2 21.7 %all_to_all.15.mine = f32[8,2,2,32,128]{4,3,2,1,0:T(8,128)S(1)} all-to-all(f32[8,2,2,32,128]{4,3,2,1,0:T(8,128)S(1)} %pack_shared.1), channel_id=1, replica_groups=mesh['copy'=2,'tm'=2,'space'=8] {'space'}, dimensions={0} | all-to-all | bytes 1048576 | tf_op jit(solution)/shard_map/all_to_all | solution.py:288
  25.9 0.0 collective-permute-start
  25.9 1.9 %collective-permute-done.other = f32[8,2,2,32,128]{4,3,2,1,0:T(8,128)S(1)} collective-permute-done((f32[8,2,2,32,128]{4,3,2,1,0:T(8,128)S(1)}, f32[8,2,2,32,128]{4,3,2,1,0:T(8,128)S(1)}, u32[]{:S(2)}, u32[]{:S(2)}) %collective-permute-start) | collective-permute-done | bytes 524320 | tf_op jit(solution)/shard_map/ppermute | solution.py:244
  27.8 0.0 copy-done.3
  27.8 0.0 copy-done.4
  27.8 0.0 copy-done.5
  27.8 3.2 %faces.1 = (f32[16,32,128]{2,1,0:T(8,128)S(1)}, f32[16,32,128]{2,1,0:T(8,128)S(1)}, f32[16,32,128]{2,1,0:T(8,128)S(1)}, f32[16,32,128]{2,1,0:T(8,128)S(1)}, f32[...) custom-call(s32[2]{0:T(128)S(1)} %pad_add_fusion.info, f32[1,4]{1,0:T(1,128)S(1)} %copy-done.5, ...), custom_call_target="tpu_custom_call" | custom-call | tf_op jit(solution)/shard_map/faces/pallas_call | solution.py:292
  31.0 19.6 %all_to_all.16.packed = f32[8,136,128]{2,1,0:T(8,128)S(1)} all-to-all(f32[8,136,128]{2,1,0:T(8,128)S(1)} %get-tuple-element.13), channel_id=1, replica_groups=mesh['copy'=2,'tm'=2,'space'=8] {'space'}, dimensions={0} | all-to-all | bytes 1114112 | tf_op jit(solution)/shard_map/all_to_all | solution.py:300
  50.6 10.3 %four_steps.1 = (f32[16,16,128]{2,1,0:T(8,128)S(1)}, f32[16,16,128]{2,1,0:T(8,128)S(1)}, f32[16,8,128]{2,1,0:T(8,128)S(1)}, f32[16,8,128]{2,1,0:T(8,128)S(1)}) custom-call(s32[2]{0:T(128)S(1)} %pad_add_fusion.info, f32[1,4]{1,0:T(1,128)S(1)} %copy-done.5, f32[8,136,128]{2,1,0:T(8,128)S(1)} %all_to_all.16.packed, ...), custom_call_target="tpu_custom_call" | custom-call | tf_op jit(solution)/shard_map/four_steps/pallas_call | solution.py:308
  60.9 0.1 collective-permute-start.1
  61.0 0.8 collective-permute-start.2
  61.8 0.1 collective-permute-start.3
  61.8 0.1 stack.42.info
  61.9 2.9 %collective-permute-done.2.halo_one = f32[16,8,128]{2,1,0:T(8,128)S(1)} collective-permute-done((f32[16,8,128]{2,1,0:T(8,128)S(1)}, f32[16,8,128]{2,1,0:T(8,128)S(1)}, u32[]{:S(2)}, u32[]{:S(2)}) %collective-permute-start.2) | collective-permute-done | bytes 65568 | tf_op jit(solution)/shard_map/ppermute | solution.py:244
  64.8 0.0 collective-permute-done.3.halo_two
  64.8 0.0 collective-permute-done.1.own
  64.9 7.8 %three_steps.1 = f32[8,2,2,16,128]{4,3,2,1,0:T(8,128)S(1)} custom-call(s32[5]{0:T(128)S(1)} %stack.42.info, f32[1,4]{1,0:T(1,128)S(1)} %copy-done.5, f32[8,136,128]{2,1,0:T(8,128)S(1)} %all_to_all.16.packed, f32[16,16,128]{2,1,0:T(8,128)S(1)} %collective-permute-done.1.own, f32[16,8,128]{2,1,0:T(8,128)S(1)} %collective-permute-done.2.halo_one, ...), custom_call_target="tpu_custom_call" | custom-call | tf_op jit(solution)/shard_map/three_steps/pallas_call | solution.py:325
  72.7 13.7 %all_to_all.17 = f32[8,2,2,16,128]{4,3,2,1,0:T(8,128)S(1)} all-to-all(f32[8,2,2,16,128]{4,3,2,1,0:T(8,128)S(1)} %three_steps.1), channel_id=1, replica_groups=mesh['copy'=2,'tm'=2,'space'=8] {'space'}, dimensions={0} | all-to-all | bytes 524288 | tf_op jit(solution)/shard_map/all_to_all | solution.py:334
  86.4 0.7 copy.9
  87.1 0.7 copy.8
  (1 shorter events, 0.0 us)
Async XLA Ops:
  0.7 0.9 %copy-start = (s32[2,128,128]{2,1,0:T(8,128)S(1)}, s32[2,128,128]{2,1,0:T(8,128)}, u32[]{:S(2)}) copy-start(s32[2,128,128]{2,1,0:T(8,128)} %buildings.3) | copy-start | bytes 393220
  1.6 1.0 %copy-start.1 = (f32[3,2,128,128]{3,2,1,0:T(8,128)S(1)}, f32[3,2,128,128]{3,2,1,0:T(8,128)}, u32[]{:S(2)}) copy-start(f32[3,2,128,128]{3,2,1,0:T(8,128)} %wind.1) | copy-start | bytes 1179652
  2.6 0.9 %copy-start.2 = (f32[2,128,128]{2,1,0:T(8,128)S(1)}, f32[2,128,128]{2,1,0:T(8,128)}, u32[]{:S(2)}) copy-start(f32[2,128,128]{2,1,0:T(8,128)} %diffusion.1) | copy-start | bytes 393220
  4.1 23.7 %copy-start.3 = (f32[1,2,128,128]{3,2,1,0:T(8,128)S(1)}, f32[1,2,128,128]{3,2,1,0:T(8,128)}, u32[]{:S(2)}) copy-start(f32[1,2,128,128]{3,2,1,0:T(8,128)} %initial.1) | copy-start | bytes 393220
  4.1 23.7 %copy-start.4 = (bf16[1,2,128,128]{3,2,1,0:T(8,128)(2,1)S(1)}, bf16[1,2,128,128]{3,2,1,0:T(8,128)(2,1)}, u32[]{:S(2)}) copy-start(bf16[1,2,128,128]{3,2,1,0:T(8,128)(2,1)} %source.1) | copy-start | bytes 196612
  4.1 23.7 %copy-start.5 = (f32[1,4]{1,0:T(1,128)S(1)}, f32[1,4]{1,0:T(1,128)}, u32[]{:S(2)}) copy-start(f32[1,4]{1,0:T(1,128)} %rates.5) | copy-start | bytes 52
  25.9 1.9 %collective-permute-start = (f32[8,2,2,32,128]{4,3,2,1,0:T(8,128)S(1)}, f32[8,2,2,32,128]{4,3,2,1,0:T(8,128)S(1)}, u32[]{:S(2)}, u32[]{:S(2)}) collective-permute-start(f32[8,2,2,32,128]{4,3,2,1,0:T(8,128)S(1)} %all_to_all.15.mine), channel_id=1, source_target_pairs={{0,8},{1,9},{2,10},{3,11},{4,12},{5,13},{6,14},{7,15},{8,0},{9,1},... | collective-permute-start | bytes 1572872 | tf_op jit(solution)/shard_map/ppermute | solution.py:244
  60.9 4.0 %collective-permute-start.1 = (f32[16,16,128]{2,1,0:T(8,128)S(1)}, f32[16,16,128]{2,1,0:T(8,128)S(1)}, u32[]{:S(2)}, u32[]{:S(2)}) collective-permute-start(f32[16,16,128]{2,1,0:T(8,128)S(1)} %get-tuple-element.20.advanced), channel_id=1, source_target_pairs={{0,8},{1,9},{2,10},{3,11},{4,12},{5,13},{6,14},{7,15},{8,0},{9,1},... | collective-permute-start | bytes 393224 | tf_op jit(solution)/shard_map/ppermute | solution.py:244
  61.0 3.9 %collective-permute-start.2 = (f32[16,8,128]{2,1,0:T(8,128)S(1)}, f32[16,8,128]{2,1,0:T(8,128)S(1)}, u32[]{:S(2)}, u32[]{:S(2)}) collective-permute-start(f32[16,8,128]{2,1,0:T(8,128)S(1)} %get-tuple-element.21), channel_id=1, source_target_pairs={{0,9},{1,8},{2,11},{3,10},{4,13},{5,12},{6,15},{7,14},{8,1},{9,0},... | collective-permute-start | bytes 196616 | tf_op jit(solution)/shard_map/ppermute | solution.py:244
  61.8 3.1 %collective-permute-start.3 = (f32[16,8,128]{2,1,0:T(8,128)S(1)}, f32[16,8,128]{2,1,0:T(8,128)S(1)}, u32[]{:S(2)}, u32[]{:S(2)}) collective-permute-start(f32[16,8,128]{2,1,0:T(8,128)S(1)} %get-tuple-element.22), channel_id=1, source_target_pairs={{0,8},{1,10},{2,9},{3,12},{4,11},{5,14},{6,13},{7,15},{8,0},{9,2},... | collective-permute-start | bytes 196616 | tf_op jit(solution)/shard_map/ppermute | solution.py:244

commit v2 on v1

--- a/solution.py
+++ b/solution.py
@@ -109,7 +109,7 @@
         return next_masked, *following[1:], along_x[0], speeds[0], peaks
 
     start = (*fields(0), zero, zero, (jnp.zeros((rows, lanes), jnp.float32),) * FINE)
-    peaks = lax.fori_loop(0, total, body, start)[-1]
+    peaks = lax.fori_loop(0, total, body, start, unroll=8)[-1]
     bounds = jnp.zeros((8, lanes), jnp.float32)
     place = lax.broadcasted_iota(jnp.int32, (8, lanes), 0)
     for k in range(FINE):
@@ -171,8 +171,8 @@
         state[place] = state[place] + (near * values - far * change)
         return values_ahead, low_flow
 
-    lax.fori_loop(0, total, first_sweep, (state[0], zero), unroll=2)
-    lax.fori_loop(0, total, second_sweep, (residual[0], zero), unroll=2)
+    lax.fori_loop(0, total, first_sweep, (state[0], zero), unroll=8)
+    lax.fori_loop(0, total, second_sweep, (residual[0], zero), unroll=8)
 
 
 def bounds_of(packed, layers, width):

time: 88.1 us -> 74.7 us (0.85)
  Pallas kernels: 21.8 us -> 8.49 us
    pallas_call x1, Pallas kernels: 10.3 us -> 3.65 us  [shards(): pl.pallas_call(functools.partial(first_kernel, rows, width, layers), out_...]
    pallas_call x1, Pallas kernels: 7.84 us -> 2.88 us  [shards(): pl.pallas_call(functools.partial(second_kernel, rows, width, layers), out...]
    pallas_call x1, Pallas kernels: 3.15 us -> 1.37 us  [shards(): pl.pallas_call(functools.partial(face_kernel, rows, width), out_shape=out...]
where the time goes in v2:
time: 74.7 us; the launch traced here: 74.4 us
  blocking collectives  55.1 us (74%)
  Pallas kernels  8.49 us (11%)
  waiting for transfers between devices  4.84 us (6%)
  local copies, waits for them, and re-layouts  4.25 us (6%)
  starting transfers between devices  0.95 us (1%)
    all_to_all x1, blocking collectives, shards(): mine = lax.all_to_all(shared, 'space', 0, 0, tiled=True)  21.7 us
    all_to_all x1, blocking collectives, shards(): packed = lax.all_to_all(packed, 'space', 0, 0, tiled=True)  19.6 us
    all_to_all x1, blocking collectives, shards(): result = lax.all_to_all(result, 'space', 0, 0, tiled=True)  13.7 us
    ppermute x4, waiting for transfers between devices, swapped(): return lax.ppermute(array, AXES, pairs)  4.84 us
    pallas_call x1, Pallas kernels, shards(): pl.pallas_call(functools.partial(first_kernel, rows, width, layers), out_...  3.65 us
    pallas_call x1, Pallas kernels, shards(): pl.pallas_call(functools.partial(second_kernel, rows, width, layers), out...  2.88 us
    unnamed x12, local copies, waits for them, and re-layouts  2.82 us
  transfers between devices with their start and end apart: 4, of which 2 were waited for; matrix products, arithmetic and copies ran while one was open for 0% of the time, Pallas kernels for 0%

profile of v2, /device:TPU:0, one launch (start us, length us, event | category | flops | bytes accessed | tf_op | source)
XLA Modules:
  0.0 74.4 jit_solution(5067450472943346146)
XLA Ops:
  0.6 0.1 pad_add_fusion.info
  0.7 0.0 copy-start
  0.7 0.9 %copy-done = s32[2,128,128]{2,1,0:T(8,128)S(1)} copy-done((s32[2,128,128]{2,1,0:T(8,128)S(1)}, s32[2,128,128]{2,1,0:T(8,128)}, u32[]{:S(2)}) %copy-start) | copy-done | bytes 131096
  1.6 0.0 copy-start.1
  1.6 1.0 %copy-done.1 = f32[3,2,128,128]{3,2,1,0:T(8,128)S(1)} copy-done((f32[3,2,128,128]{3,2,1,0:T(8,128)S(1)}, f32[3,2,128,128]{3,2,1,0:T(8,128)}, u32[]{:S(2)}) %copy-start.1) | copy-done | bytes 393240
  2.6 0.0 copy-start.2
  2.6 0.9 %copy-done.2 = f32[2,128,128]{2,1,0:T(8,128)S(1)} copy-done((f32[2,128,128]{2,1,0:T(8,128)S(1)}, f32[2,128,128]{2,1,0:T(8,128)}, u32[]{:S(2)}) %copy-start.2) | copy-done | bytes 131096
  3.5 0.6 pack_shared.1
  4.1 0.0 copy-start.3
  4.1 0.0 copy-start.4
  4.1 0.0 copy-start.5
  4.2 21.7 %all_to_all.15.mine = f32[8,2,2,32,128]{4,3,2,1,0:T(8,128)S(1)} all-to-all(f32[8,2,2,32,128]{4,3,2,1,0:T(8,128)S(1)} %pack_shared.1), channel_id=1, replica_groups=mesh['copy'=2,'tm'=2,'space'=8] {'space'}, dimensions={0} | all-to-all | bytes 1048576 | tf_op jit(solution)/shard_map/all_to_all | solution.py:288
  25.9 0.0 collective-permute-start
  25.9 1.9 %collective-permute-done.other = f32[8,2,2,32,128]{4,3,2,1,0:T(8,128)S(1)} collective-permute-done((f32[8,2,2,32,128]{4,3,2,1,0:T(8,128)S(1)}, f32[8,2,2,32,128]{4,3,2,1,0:T(8,128)S(1)}, u32[]{:S(2)}, u32[]{:S(2)}) %collective-permute-start) | collective-permute-done | bytes 524320 | tf_op jit(solution)/shard_map/ppermute | solution.py:244
  27.8 0.0 copy-done.3
  27.8 0.0 copy-done.4
  27.8 0.0 copy-done.5
  27.8 1.4 %faces.1 = (f32[16,32,128]{2,1,0:T(8,128)S(1)}, f32[16,32,128]{2,1,0:T(8,128)S(1)}, f32[16,32,128]{2,1,0:T(8,128)S(1)}, f32[16,32,128]{2,1,0:T(8,128)S(1)}, f32[...) custom-call(s32[2]{0:T(128)S(1)} %pad_add_fusion.info, f32[1,4]{1,0:T(1,128)S(1)} %copy-done.5, ...), custom_call_target="tpu_custom_call" | custom-call | tf_op jit(solution)/shard_map/faces/pallas_call | solution.py:292
  29.2 19.6 %all_to_all.16.packed = f32[8,136,128]{2,1,0:T(8,128)S(1)} all-to-all(f32[8,136,128]{2,1,0:T(8,128)S(1)} %get-tuple-element.13), channel_id=1, replica_groups=mesh['copy'=2,'tm'=2,'space'=8] {'space'}, dimensions={0} | all-to-all | bytes 1114112 | tf_op jit(solution)/shard_map/all_to_all | solution.py:300
  48.8 3.6 %four_steps.1 = (f32[16,16,128]{2,1,0:T(8,128)S(1)}, f32[16,16,128]{2,1,0:T(8,128)S(1)}, f32[16,8,128]{2,1,0:T(8,128)S(1)}, f32[16,8,128]{2,1,0:T(8,128)S(1)}) custom-call(s32[2]{0:T(128)S(1)} %pad_add_fusion.info, f32[1,4]{1,0:T(1,128)S(1)} %copy-done.5, f32[8,136,128]{2,1,0:T(8,128)S(1)} %all_to_all.16.packed, ...), custom_call_target="tpu_custom_call" | custom-call | tf_op jit(solution)/shard_map/four_steps/pallas_call | solution.py:308
  52.5 0.1 collective-permute-start.1
  52.6 0.8 %collective-permute-start.2 = (f32[16,8,128]{2,1,0:T(8,128)S(1)}, f32[16,8,128]{2,1,0:T(8,128)S(1)}, u32[]{:S(2)}, u32[]{:S(2)}) collective-permute-start(f32[16,8,128]{2,1,0:T(8,128)S(1)} %get-tuple-element.21), channel_id=1, source_target_pairs={{0,9},{1,8},{2,11},{3,10},{4,13},{5,12},{6,15},{7,14},{8,1},{9,0},... | collective-permute-start | bytes 196616 | tf_op jit(solution)/shard_map/ppermute | solution.py:244
  53.4 0.1 collective-permute-start.3
  53.4 0.1 stack.42.info
  53.5 2.9 %collective-permute-done.2.halo_one = f32[16,8,128]{2,1,0:T(8,128)S(1)} collective-permute-done((f32[16,8,128]{2,1,0:T(8,128)S(1)}, f32[16,8,128]{2,1,0:T(8,128)S(1)}, u32[]{:S(2)}, u32[]{:S(2)}) %collective-permute-start.2) | collective-permute-done | bytes 65568 | tf_op jit(solution)/shard_map/ppermute | solution.py:244
  56.5 0.0 collective-permute-done.3.halo_two
  56.5 0.0 collective-permute-done.1.own
  56.5 2.9 %three_steps.1 = f32[8,2,2,16,128]{4,3,2,1,0:T(8,128)S(1)} custom-call(s32[5]{0:T(128)S(1)} %stack.42.info, f32[1,4]{1,0:T(1,128)S(1)} %copy-done.5, f32[8,136,128]{2,1,0:T(8,128)S(1)} %all_to_all.16.packed, f32[16,16,128]{2,1,0:T(8,128)S(1)} %collective-permute-done.1.own, f32[16,8,128]{2,1,0:T(8,128)S(1)} %collective-permute-done.2.halo_one, ...), custom_call_target="tpu_custom_call" | custom-call | tf_op jit(solution)/shard_map/three_steps/pallas_call | solution.py:325
  59.4 13.7 %all_to_all.17 = f32[8,2,2,16,128]{4,3,2,1,0:T(8,128)S(1)} all-to-all(f32[8,2,2,16,128]{4,3,2,1,0:T(8,128)S(1)} %three_steps.1), channel_id=1, replica_groups=mesh['copy'=2,'tm'=2,'space'=8] {'space'}, dimensions={0} | all-to-all | bytes 524288 | tf_op jit(solution)/shard_map/all_to_all | solution.py:334
  73.1 0.7 copy.9
  73.7 0.7 copy.8
  (1 shorter events, 0.0 us)
Async XLA Ops:
  0.7 0.9 %copy-start = (s32[2,128,128]{2,1,0:T(8,128)S(1)}, s32[2,128,128]{2,1,0:T(8,128)}, u32[]{:S(2)}) copy-start(s32[2,128,128]{2,1,0:T(8,128)} %buildings.3) | copy-start | bytes 393220
  1.6 1.0 %copy-start.1 = (f32[3,2,128,128]{3,2,1,0:T(8,128)S(1)}, f32[3,2,128,128]{3,2,1,0:T(8,128)}, u32[]{:S(2)}) copy-start(f32[3,2,128,128]{3,2,1,0:T(8,128)} %wind.1) | copy-start | bytes 1179652
  2.6 0.9 %copy-start.2 = (f32[2,128,128]{2,1,0:T(8,128)S(1)}, f32[2,128,128]{2,1,0:T(8,128)}, u32[]{:S(2)}) copy-start(f32[2,128,128]{2,1,0:T(8,128)} %diffusion.1) | copy-start | bytes 393220
  4.1 23.7 %copy-start.3 = (f32[1,2,128,128]{3,2,1,0:T(8,128)S(1)}, f32[1,2,128,128]{3,2,1,0:T(8,128)}, u32[]{:S(2)}) copy-start(f32[1,2,128,128]{3,2,1,0:T(8,128)} %initial.1) | copy-start | bytes 393220
  4.1 23.7 %copy-start.4 = (bf16[1,2,128,128]{3,2,1,0:T(8,128)(2,1)S(1)}, bf16[1,2,128,128]{3,2,1,0:T(8,128)(2,1)}, u32[]{:S(2)}) copy-start(bf16[1,2,128,128]{3,2,1,0:T(8,128)(2,1)} %source.1) | copy-start | bytes 196612
  4.1 23.7 %copy-start.5 = (f32[1,4]{1,0:T(1,128)S(1)}, f32[1,4]{1,0:T(1,128)}, u32[]{:S(2)}) copy-start(f32[1,4]{1,0:T(1,128)} %rates.5) | copy-start | bytes 52
  25.9 1.9 %collective-permute-start = (f32[8,2,2,32,128]{4,3,2,1,0:T(8,128)S(1)}, f32[8,2,2,32,128]{4,3,2,1,0:T(8,128)S(1)}, u32[]{:S(2)}, u32[]{:S(2)}) collective-permute-start(f32[8,2,2,32,128]{4,3,2,1,0:T(8,128)S(1)} %all_to_all.15.mine), channel_id=1, source_target_pairs={{0,8},{1,9},{2,10},{3,11},{4,12},{5,13},{6,14},{7,15},{8,0},{9,1},... | collective-permute-start | bytes 1572872 | tf_op jit(solution)/shard_map/ppermute | solution.py:244
  52.5 4.0 %collective-permute-start.1 = (f32[16,16,128]{2,1,0:T(8,128)S(1)}, f32[16,16,128]{2,1,0:T(8,128)S(1)}, u32[]{:S(2)}, u32[]{:S(2)}) collective-permute-start(f32[16,16,128]{2,1,0:T(8,128)S(1)} %get-tuple-element.20.advanced), channel_id=1, source_target_pairs={{0,8},{1,9},{2,10},{3,11},{4,12},{5,13},{6,14},{7,15},{8,0},{9,1},... | collective-permute-start | bytes 393224 | tf_op jit(solution)/shard_map/ppermute | solution.py:244
  52.6 3.9 %collective-permute-start.2 = (f32[16,8,128]{2,1,0:T(8,128)S(1)}, f32[16,8,128]{2,1,0:T(8,128)S(1)}, u32[]{:S(2)}, u32[]{:S(2)}) collective-permute-start(f32[16,8,128]{2,1,0:T(8,128)S(1)} %get-tuple-element.21), channel_id=1, source_target_pairs={{0,9},{1,8},{2,11},{3,10},{4,13},{5,12},{6,15},{7,14},{8,1},{9,0},... | collective-permute-start | bytes 196616 | tf_op jit(solution)/shard_map/ppermute | solution.py:244
  53.4 3.1 %collective-permute-start.3 = (f32[16,8,128]{2,1,0:T(8,128)S(1)}, f32[16,8,128]{2,1,0:T(8,128)S(1)}, u32[]{:S(2)}, u32[]{:S(2)}) collective-permute-start(f32[16,8,128]{2,1,0:T(8,128)S(1)} %get-tuple-element.22), channel_id=1, source_target_pairs={{0,8},{1,10},{2,9},{3,12},{4,11},{5,14},{6,13},{7,15},{8,0},{9,2},... | collective-permute-start | bytes 196616 | tf_op jit(solution)/shard_map/ppermute | solution.py:244

commit v3 on v2

--- a/solution.py
+++ b/solution.py
@@ -28,29 +28,128 @@
     return jnp.concatenate(parts, axis=0) if len(parts) > 1 else parts[0]
 
 
-def pack_shared(rows, width, info, diffusion, wind, buildings, out):
-    first = info[0] == 0
-    for layer in range(diffusion.shape[0]):
-        masked = diffusion[layer] * (1 - buildings[layer]).astype(jnp.float32)
+def load_kernel(info, initial, source, diffusion, wind, buildings, masked, winds, state, forcing, edge_one, edge_two, *rest):
+    fresh, early, late, solid, sems = rest
+    pairs = ((diffusion, fresh), (buildings, solid), (wind, winds), (initial.at[0], early), (source.at[0], late))
+    copies = [pltpu.make_async_copy(*pair, sems.at[number]) for number, pair in enumerate(pairs)]
+    for copy in copies:
+        copy.start()
+    for copy in copies[:3]:
+        copy.wait()
+    opened = (1 - solid[...]).astype(jnp.float32)
+    masked[...] = fresh[...] * opened
+    first, even = info[0] == 0, info[1] % 2 == 0
+    last = masked.shape[0] - 1
+    low = jnp.where(first, masked[0], winds[0, 0])
+    high = jnp.where(first, masked[last], winds[0, last])
+    edge_one[...] = jnp.where(even, high, low)
+    edge_two[...] = jnp.where(even, low, high)
+    for copy in copies[3:]:
+        copy.wait()
+    state[...] = early[...] * opened
+    forcing[...] = late[...].astype(jnp.float32) * opened
+
+
+def pack_shared(rows, width, info, masked, wind, same, across):
+    first, spot = info[0] == 0, info[1]
+    half = same.shape[0]
+    for layer in range(masked.shape[0]):
         pair = (
-            jnp.where(first, masked, wind[1, layer]),
+            jnp.where(first, masked[layer], wind[1, layer]),
             jnp.where(first, wind[0, layer], wind[2, layer]),
         )
         for field in range(2):
-            for place in range(out.shape[0]):
-                out[place, field, layer] = windows(pair[field], place, rows, width)
+            for place in range(half):
+                even = windows(pair[field], 2 * place, rows, width)
+                odd = windows(pair[field], 2 * place + 1, rows, width)
+                swap = spot % 2 == 1
+                same[place ^ (spot // 2), field, layer] = jnp.where(swap, odd, even)
+                across[place ^ (spot // 2), field, layer] = jnp.where(swap, even, odd)
+
+
+def pack_own(rows, width, state, forcing, packed):
+    layers = state.shape[0]
+    for layer in range(layers):
+        for spot in range(packed.shape[0]):
+            packed[spot, pl.ds(layer * width, width)] = windows(state[layer], spot, rows, width)
+            packed[spot, pl.ds((layers + layer) * width, width)] = windows(forcing[layer], spot, rows, width)
+
+
+def bound_kernel(rows, width, info, rates, mine, other, masked, wind, state, forcing, out):
+    first, even = info[0] == 0, info[1] % 2 == 0
+    here, there = (mine[0], mine[1]), (other[0], other[1])
+
+    def sides(one, two, keep):
+        above, below = jnp.where(even, one, two), jnp.where(even, two, one)
+        if keep:
+            below, above = jnp.where(info[2] == 1, below, 0.0), jnp.where(info[3] == 1, above, 0.0)
+        return below, above
+
+    masked_sides = sides(jnp.where(first, here[0], there[0]), jnp.where(first, here[1], there[1]), True)
+    wind_sides = sides(jnp.where(first, there[0], here[0]), jnp.where(first, there[1], here[1]), False)
+    layers, depth, lanes = masked.shape
+    chunk = 32 if depth % 32 == 0 else depth
+    row = lax.broadcasted_iota(jnp.int32, (chunk, lanes), 0)
+    inner_lane = lax.broadcasted_iota(jnp.int32, (chunk, lanes), 1) < lanes - 1
+
+    def face(here, ahead, wind_here, wind_ahead):
+        both = jnp.where((here > 0.0) & (ahead > 0.0), 1.0, 0.0)
+        return jnp.sqrt(here * ahead), jnp.abs(0.5 * (wind_here + wind_ahead) * both)
+
+    peaks = [jnp.zeros((chunk, lanes), jnp.float32)] * FINE
+    edge = [[jnp.zeros((1, lanes), jnp.float32)] * 2 for _ in range(layers)]
+    for start in range(0, depth, chunk):
+        part = pl.ds(start, chunk)
+        fields = [masked_sides[0][start : start + chunk]]
+        fields += [masked[layer, part] for layer in range(layers)]
+        fields += [masked_sides[1][start : start + chunk]]
+        winds = [wind_sides[0][start : start + chunk]]
+        winds += [wind[0, layer, part] for layer in range(layers)]
+        winds += [wind_sides[1][start : start + chunk]]
+        below = face(fields[0], fields[1], winds[0], winds[1])
+        for layer in range(layers):
+            field = fields[layer + 1]
+            above = face(field, fields[layer + 2], winds[layer + 1], winds[layer + 2])
+            sums = [above[0] + below[0], above[1] + below[1]]
+            below = above
+            flow = wind[1, layer, part]
+            if start + chunk < depth:
+                following = pl.ds(start + 1, chunk)
+                pair = face(field, masked[layer, following], flow, wind[1, layer, following])
+            else:
+                pair = face(field, roll_back(field, 0), flow, roll_back(flow, 0))
+                pair = [jnp.where(row < chunk - 1, value, 0.0) for value in pair]
+            for number in range(2):
+                value = pair[number]
+                lower = jnp.where(row == 0, edge[layer][number], pltpu.roll(value, 1, 0))
+                edge[layer][number] = value[chunk - 1 : chunk]
+                sums[number] = sums[number] + value + lower
+            flow = wind[2, layer, part]
+            pair = face(field, roll_back(field, 1), flow, roll_back(flow, 1))
+            for number in range(2):
+                value = jnp.where(inner_lane, pair[number], 0.0)
+                sums[number] = sums[number] + value + pltpu.roll(value, 1, 1)
+            still = 1.0 + 2.0 * sums[0]
+            for k in range(FINE):
+                peaks[k] = jnp.maximum(peaks[k], still + rates[0, k] * sums[1])
+    bounds = jnp.zeros((8, lanes), jnp.float32)
+    place = lax.broadcasted_iota(jnp.int32, (8, lanes), 0)
+    for k in range(FINE):
+        bounds = jnp.where(place == k, jnp.max(peaks[k]), bounds)
+    pack_own(rows, width, state, forcing, out)
+    start = out.shape[1] - 8
+    for spot in range(out.shape[0]):
+        out[spot, pl.ds(start, 8)] = bounds
 
 
 def roll_back(values, axis):
     return pltpu.roll(values, values.shape[axis] - 1, axis)
 
 
-def face_kernel(rows, width, info, rates, mine, other, initial, source, buildings, *outs):
-    faces, packed = outs[:6], outs[6]
-    count, layers = mine.shape[0], mine.shape[2]
+def face_kernel(info, mine, other, *faces):
+    count, layers, width, lanes = mine.shape[0], *mine.shape[2:]
     total = count * layers
-    lanes = mine.shape[-1]
-    first = info[0] == 0
+    first, own = info[0] == 0, info[1]
     row = lax.broadcasted_iota(jnp.int32, (width, lanes), 0)
     lane = lax.broadcasted_iota(jnp.int32, (width, lanes), 1)
     inner_row = row < width - 1
@@ -58,7 +157,7 @@
     zero = jnp.zeros((width, lanes), jnp.float32)
 
     def fields(place):
-        spot, layer = place // layers, place % layers
+        spot, layer = (place // layers) ^ own, place % layers
         here = (mine[spot, 0, layer], mine[spot, 1, layer])
         there = (other[spot, 0, layer], other[spot, 1, layer])
         masked = jnp.where(first, here[0], there[0])
@@ -68,10 +167,9 @@
         return masked, wind_x, wind_y, wind_z
 
     def body(place, carry):
-        masked, wind_x, wind_y, wind_z, low_conduct, low_speed, peaks = carry
+        masked, wind_x, wind_y, wind_z = carry
         following = fields(jnp.minimum(place + 1, total - 1))
-        inside = place < total - 1
-        next_masked = jnp.where(inside, following[0], zero)
+        next_masked = jnp.where(place < total - 1, following[0], zero)
         opened = jnp.where(masked > 0.0, 1.0, 0.0)
 
         def face(masked_ahead, wind_here, wind_ahead, keep):
@@ -86,43 +184,9 @@
         along_z = face(roll_back(masked, 1), wind_z, roll_back(wind_z, 1), inner_lane)
         for number, value in enumerate(along_x + along_y + along_z):
             faces[number][place] = value
-        speeds = [jnp.abs(pair[1]) for pair in (along_x, along_y, along_z)]
-        conduct_sum = (
-            along_x[0]
-            + low_conduct
-            + along_y[0]
-            + pltpu.roll(along_y[0], 1, 0)
-            + along_z[0]
-            + pltpu.roll(along_z[0], 1, 1)
-        )
-        speed_sum = (
-            speeds[0]
-            + low_speed
-            + speeds[1]
-            + pltpu.roll(speeds[1], 1, 0)
-            + speeds[2]
-            + pltpu.roll(speeds[2], 1, 1)
-        )
-        still = (1.0 + 2.0 * conduct_sum)[LOW : LOW + rows]
-        speed_sum = speed_sum[LOW : LOW + rows]
-        peaks = tuple(jnp.maximum(peaks[k], still + rates[0, k] * speed_sum) for k in range(FINE))
-        return next_masked, *following[1:], along_x[0], speeds[0], peaks
-
-    start = (*fields(0), zero, zero, (jnp.zeros((rows, lanes), jnp.float32),) * FINE)
-    peaks = lax.fori_loop(0, total, body, start, unroll=8)[-1]
-    bounds = jnp.zeros((8, lanes), jnp.float32)
-    place = lax.broadcasted_iota(jnp.int32, (8, lanes), 0)
-    for k in range(FINE):
-        bounds = jnp.where(place == k, jnp.max(peaks[k]), bounds)
-    for layer in range(layers):
-        opened = (1 - buildings[layer]).astype(jnp.float32)
-        state = initial[0, layer] * opened
-        forcing = source[0, layer].astype(jnp.float32) * opened
-        for spot in range(count):
-            packed[spot, pl.ds(layer * width, width)] = windows(state, spot, rows, width)
-            packed[spot, pl.ds((layers + layer) * width, width)] = windows(forcing, spot, rows, width)
-    for spot in range(count):
-        packed[spot, pl.ds(2 * layers * width, 8)] = bounds
+        return next_masked, *following[1:]
+
+    lax.fori_loop(0, total, body, fields(0), unroll=8)
 
 
 def coefficients(bound):
@@ -175,24 +239,23 @@
     lax.fori_loop(0, total, second_sweep, (residual[0], zero), unroll=8)
 
 
-def bounds_of(packed, layers, width):
-    bounds = packed[0, pl.ds(2 * layers * width, 8)]
-    for spot in range(1, packed.shape[0]):
-        bounds = jnp.maximum(bounds, packed[spot, pl.ds(2 * layers * width, 8)])
+def bounds_of(packed):
+    part = pl.ds(packed.shape[1] - 8, 8)
+    bounds = packed[0, part]
+    for entry in range(1, packed.shape[0]):
+        bounds = jnp.maximum(bounds, packed[entry, part])
     return bounds
 
 
 def first_kernel(rows, width, layers, info, rates, packed, *refs):
     faces, (advanced, third, edge_one, edge_two), (state, residual, ahead) = refs[:6], refs[6:10], refs[10:]
-    count = packed.shape[0]
-    total = count * layers
+    total = state.shape[0] - 1
     zero = jnp.zeros(state.shape[1:], jnp.float32)
     state[total] = zero
     residual[total] = zero
-    for spot in range(count):
-        for layer in range(layers):
-            state[spot * layers + layer] = packed[spot, pl.ds(layer * width, width)]
-    bounds = bounds_of(packed, layers, width)
+    for place in range(total):
+        state[place] = packed[place // layers, pl.ds(place % layers * width, width)]
+    bounds = bounds_of(packed)
     for k in range(FINE):
         near, far = coefficients(bounds[k : k + 1])
         one_step(total, width, layers, state, residual, ahead, faces, packed, rates[0, k], near, far)
@@ -206,7 +269,7 @@
     edge_two[...] = jnp.where(even, low, high)
 
 
-def second_kernel(rows, width, layers, info, rates, packed, own, halo_one, halo_two, advanced, third, *refs):
+def second_kernel(rows, width, layers, info, rates, packed, passed, halo_one, halo_two, advanced, third, *refs):
     faces, out, (state, residual, ahead) = refs[:6], refs[6], refs[7:]
     total = state.shape[0] - 1
     zero = jnp.zeros(state.shape[1:], jnp.float32)
@@ -217,11 +280,11 @@
     low = jnp.where(swap, above, below)
     high = jnp.where(swap, below, above)
     state[:total, :LOW] = jnp.where(info[3] == 1, low, 0.0)
-    state[:total, LOW : LOW + rows] = own[...]
+    state[:total, LOW : LOW + rows] = passed[...]
     state[:total, LOW + rows : 2 * LOW + rows] = jnp.where(info[4] == 1, high, 0.0)
     if width > 2 * LOW + rows:
         state[:total, 2 * LOW + rows :] = jnp.zeros((total, width - 2 * LOW - rows, state.shape[-1]), jnp.float32)
-    bounds = bounds_of(packed, layers, width)
+    bounds = bounds_of(packed)
     for k in range(FINE - 1):
         near, far = coefficients(bounds[k : k + 1])
         one_step(total, width, layers, state, residual, ahead, faces, packed, rates[0, k], near, far)
@@ -244,6 +307,10 @@
     return lax.ppermute(array, AXES, pairs)
 
 
+def outer_partner(count):
+    return lambda t, s: (t, ((s + 1) ^ 1) - 1) if 0 < s < count - 1 else (t ^ 1, s)
+
+
 def halos(edge_one, edge_two, advanced, sizes, rows, place):
     copies, blocks, count = sizes
     even = place % 2 == 0
@@ -275,29 +342,76 @@
     def struct(*shape):
         return jax.ShapeDtypeStruct(shape, jnp.float32)
 
+    def call(kernel, outs, in_specs, name, *operands, **options):
+        return pl.pallas_call(
+            kernel,
+            out_shape=outs,
+            in_specs=in_specs,
+            out_specs=[VMEM] * len(outs),
+            name=name,
+            **{"compiler_params": params, **options},
+        )(*operands)
+
     half = block % 2
-    info = jnp.stack([half, place]).astype(jnp.int32)
-    shared = pl.pallas_call(
+    flags = [half, place, place > 0, place < count - 1]
+    info = jnp.stack([jnp.asarray(flag).astype(jnp.int32) for flag in flags])
+    slab = struct(layers, depth, lanes)
+    outer = struct(depth, lanes)
+    hold = pltpu.VMEM((layers, depth, lanes), jnp.float32)
+    anywhere = pl.BlockSpec(memory_space=pltpu.HBM)
+    arrays = (initial, source, diffusion, wind_field, buildings)
+    masked, winds, state, forcing, edge_one, edge_two = call(
+        load_kernel,
+        [slab, struct(3, layers, depth, lanes), slab, slab, outer, outer],
+        [SMEM] + [anywhere] * 5,
+        "load",
+        info,
+        *(pltpu.with_memory_space_constraint(array, pltpu.HBM) for array in arrays),
+        scratch_shapes=[
+            hold,
+            hold,
+            pltpu.VMEM((layers, depth, lanes), source.dtype),
+            pltpu.VMEM((layers, depth, lanes), jnp.int32),
+            pltpu.SemaphoreType.DMA((5,)),
+        ],
+    )
+    edge_one = swapped(edge_one, sizes, lambda t, s: (t, s ^ 1))
+    edge_two = swapped(edge_two, sizes, outer_partner(count))
+    same, across = call(
         functools.partial(pack_shared, rows, width),
-        out_shape=struct(count, 2, layers, width, lanes),
-        in_specs=[SMEM] + [VMEM] * 3,
-        out_specs=VMEM,
-        compiler_params=params,
-        name="pack_shared",
-    )(info, diffusion, wind_field, buildings)
-    mine = lax.all_to_all(shared, "space", 0, 0, tiled=True)
+        [struct(count // 2, 2, layers, width, lanes)] * 2,
+        [SMEM] + [VMEM] * 2,
+        "pack_shared",
+        info,
+        masked,
+        winds,
+    )
+    across = swapped(across, sizes, lambda t, s: (t, s ^ 1))
+    even = [swapped(same[step], sizes, lambda t, s: (t, s ^ (2 * step))) for step in range(1, count // 2)]
+    across, *even = lax.optimization_barrier((across, *even))
+    edges = jnp.stack([edge_one, edge_two])
+    other_edges = swapped(edges, sizes, lambda t, s: (t ^ 1, s))
+    (packed,) = call(
+        functools.partial(bound_kernel, rows, width),
+        [struct(count, 2 * layers * width + 8, lanes)],
+        [SMEM] * 2 + [VMEM] * 6,
+        "bounds",
+        info,
+        strength,
+        edges,
+        other_edges,
+        masked,
+        winds,
+        state,
+        forcing,
+    )
+    odd = [swapped(across[step], sizes, lambda t, s: (t, s ^ (2 * step))) for step in range(1, count // 2)]
+    parts = [part for pair in zip([same[0], *even], [across[0], *odd]) for part in pair]
+    *parts, _ = lax.optimization_barrier((*parts, packed))
+    packed = lax.all_to_all(packed, "space", 0, 0, tiled=True)
+    mine = jnp.stack(parts)
     other = swapped(mine, sizes, lambda t, s: (t ^ 1, s))
-
-    out_shape = [struct(total, width, lanes)] * 6 + [struct(count, 2 * layers * width + 8, lanes)]
-    *faces, packed = pl.pallas_call(
-        functools.partial(face_kernel, rows, width),
-        out_shape=out_shape,
-        in_specs=[SMEM] * 2 + [VMEM] * 5,
-        out_specs=[VMEM] * 7,
-        compiler_params=params,
-        name="faces",
-    )(info, strength, mine, other, initial, source, buildings)
-    packed = lax.all_to_all(packed, "space", 0, 0, tiled=True)
+    faces = call(face_kernel, [struct(total, width, lanes)] * 6, [SMEM] + [VMEM] * 2, "faces", info, mine, other)
 
     edge = min(rows, LOW)
     scratch = [

time: 74.7 us -> 69.1 us (0.925)
  blocking collectives: 55.1 us -> 14.5 us
  starting transfers between devices: 0.95 us -> 20.4 us
  waiting for transfers between devices: 4.84 us -> 18.9 us
  Pallas kernels: 8.49 us -> 11.9 us
  local copies, waits for them, and re-layouts: 4.25 us -> 2.18 us
    all_to_all x2 -> x0, blocking collectives: 41.4 us -> none  [the longest x1 21.7 us: shards(): mine = lax.all_to_all(shared, 'space', 0, 0, tiled=True)]
    ppermute x4 -> x14, starting transfers between devices: 0.95 us -> 16.9 us  [swapped(): return lax.ppermute(array, AXES, pairs)]
    all_to_all x0 -> x1, waiting for transfers between devices: none -> 10.6 us  [shards(): packed = lax.all_to_all(packed, 'space', 0, 0, tiled=True)]
    all_to_all x0 -> x1, starting transfers between devices: none -> 3.54 us  [shards(): packed = lax.all_to_all(packed, 'space', 0, 0, tiled=True)]
    ppermute x4 -> x14, waiting for transfers between devices: 4.84 us -> 8.31 us  [swapped(): return lax.ppermute(array, AXES, pairs)]
    pallas_call x2 -> x4, Pallas kernels: 1.95 us -> 5.37 us  [call(): pl.pallas_call(kernel, out_shape=outs, in_specs=in_specs, out_specs=[VMEM...]
    unnamed x12 -> x9, local copies, waits for them, and re-layouts: 2.82 us -> 0.71 us
    all_to_all x1, blocking collectives: 13.7 us -> 14.5 us  [shards(): result = lax.all_to_all(result, 'space', 0, 0, tiled=True)]
  transfers between devices with their start and end apart: 4 -> 15, of which waited for: 2 -> 5; matrix products, arithmetic and copies ran while one was open for 0% -> 0% of each run, Pallas kernels for 0% -> 5%
where the time goes in v3:
time: 69.1 us; the launch traced here: 68.8 us
  starting transfers between devices  20.4 us (30%)
  waiting for transfers between devices  18.9 us (27%)
  blocking collectives  14.5 us (21%)
  Pallas kernels  11.9 us (17%)
  local copies, waits for them, and re-layouts  2.18 us (3%)
  between operations  0.83 us (1%)
    ppermute x14, starting transfers between devices, swapped(): return lax.ppermute(array, AXES, pairs)  16.9 us
    all_to_all x1, blocking collectives, shards(): result = lax.all_to_all(result, 'space', 0, 0, tiled=True)  14.5 us
    all_to_all x1, waiting for transfers between devices, shards(): packed = lax.all_to_all(packed, 'space', 0, 0, tiled=True)  10.6 us
    ppermute x14, waiting for transfers between devices, swapped(): return lax.ppermute(array, AXES, pairs)  8.31 us
    pallas_call x4, Pallas kernels, call(): pl.pallas_call(kernel, out_shape=outs, in_specs=in_specs, out_specs=[VMEM...  5.37 us
    pallas_call x1, Pallas kernels, shards(): pl.pallas_call(functools.partial(first_kernel, rows, width, layers), out_...  3.65 us
    all_to_all x1, starting transfers between devices, shards(): packed = lax.all_to_all(packed, 'space', 0, 0, tiled=True)  3.54 us
    pallas_call x1, Pallas kernels, shards(): pl.pallas_call(functools.partial(second_kernel, rows, width, layers), out...  2.88 us
  transfers between devices with their start and end apart: 15, of which 5 were waited for; matrix products, arithmetic and copies ran while one was open for 0% of the time, Pallas kernels for 5%

profile of v3, /device:TPU:0, one launch (start us, length us, event | category | flops | bytes accessed | tf_op | source)
XLA Modules:
  0.0 68.8 jit_solution(9054305302519692261)
XLA Ops:
  0.6 0.1 pad_add_fusion.info
  0.7 1.8 %load.1 = (f32[2,128,128]{2,1,0:T(8,128)S(1)}, f32[3,2,128,128]{3,2,1,0:T(8,128)S(1)}, f32[2,128,128]{2,1,0:T(8,128)S(1)}, f32[2,128,128]{2,1,0:T(8,128)S(1)}, f...) custom-call(s32[4]{0:T(128)S(1)} %pad_add_fusion.info, f32[1,2,128,128]{3,2,1,0:T(8,128)} %initial.1, ...), custom_call_target="tpu_custom_call" | custom-call | tf_op jit(solution)/shard_map/load/pallas_call | solution.py:346
  2.5 3.0 %collective-permute-start = (f32[128,128]{1,0:T(8,128)S(1)}, f32[128,128]{1,0:T(8,128)S(1)}, u32[]{:S(2)}, u32[]{:S(2)}) collective-permute-start(f32[128,128]{1,0:T(8,128)S(1)} %get-tuple-element.32), channel_id=1, source_target_pairs={{0,1},{1,0},{2,3},{3,2},{4,5},{5,4},{6,7},{7,6},{8,9},{9,8},{10,11... | collective-permute-start | bytes 196616 | tf_op jit(solution)/shard_map/ppermute | solution.py:307
  5.5 0.0 collective-permute-start.1
  5.5 0.6 pack_shared.1
  6.1 3.1 %collective-permute-start.3 = (f32[4,2,2,32,128]{4,3,2,1,0:T(8,128)S(1)}, f32[4,2,2,32,128]{4,3,2,1,0:T(8,128)S(1)}, u32[]{:S(2)}, u32[]{:S(2)}) collective-permute-start(f32[4,2,2,32,128]{4,3,2,1,0:T(8,128)S(1)} %get-tuple-element.39), channel_id=1, source_target_pairs={{0,1},{1,0},{2,3},{3,2},{4,5},{5,4},{6,7},{7,6},{8,9},{9,8},{10,11... | collective-permute-start | bytes 786440 | tf_op jit(solution)/shard_map/ppermute | solution.py:307
  9.3 1.1 %collective-permute-start.6 = (f32[2,2,32,128]{3,2,1,0:T(8,128)S(1)}, f32[2,2,32,128]{3,2,1,0:T(8,128)S(1)}, u32[]{:S(2)}, u32[]{:S(2)}) collective-permute-start(f32[2,2,32,128]{3,2,1,0:T(8,128)S(1)} %get-tuple-element.68), channel_id=1, source_target_pairs={{0,6},{1,7},{2,4},{3,5},{4,2},{5,3},{6,0},{7,1},{8,14},{9,15},{10,... | collective-permute-start | bytes 196616 | tf_op jit(solution)/shard_map/ppermute | solution.py:307
  10.4 2.0 %collective-permute-start.5 = (f32[2,2,32,128]{3,2,1,0:T(8,128)S(1)}, f32[2,2,32,128]{3,2,1,0:T(8,128)S(1)}, u32[]{:S(2)}, u32[]{:S(2)}) collective-permute-start(f32[2,2,32,128]{3,2,1,0:T(8,128)S(1)} %get-tuple-element.69), channel_id=1, source_target_pairs={{0,4},{1,5},{2,6},{3,7},{4,0},{5,1},{6,2},{7,3},{8,12},{9,13},{10,... | collective-permute-start | bytes 196616 | tf_op jit(solution)/shard_map/ppermute | solution.py:307
  12.4 0.0 collective-permute-done
  12.4 1.3 %collective-permute-start.4 = (f32[2,2,32,128]{3,2,1,0:T(8,128)S(1)}, f32[2,2,32,128]{3,2,1,0:T(8,128)S(1)}, u32[]{:S(2)}, u32[]{:S(2)}) collective-permute-start(f32[2,2,32,128]{3,2,1,0:T(8,128)S(1)} %get-tuple-element.70), channel_id=1, source_target_pairs={{0,2},{1,3},{2,0},{3,1},{4,6},{5,7},{6,4},{7,5},{8,10},{9,11},{10,... | collective-permute-start | bytes 196616 | tf_op jit(solution)/shard_map/ppermute | solution.py:307
  13.7 0.0 collective-permute-done.1
  13.7 0.1 collective-permute-start.2
  13.8 2.3 %collective-permute-done.6 = f32[2,2,32,128]{3,2,1,0:T(8,128)S(1)} collective-permute-done((f32[2,2,32,128]{3,2,1,0:T(8,128)S(1)}, f32[2,2,32,128]{3,2,1,0:T(8,128)S(1)}, u32[]{:S(2)}, u32[]{:S(2)}) %collective-permute-start.6) | collective-permute-done | bytes 65568 | tf_op jit(solution)/shard_map/ppermute | solution.py:307
  16.1 1.9 %collective-permute-done.5 = f32[2,2,32,128]{3,2,1,0:T(8,128)S(1)} collective-permute-done((f32[2,2,32,128]{3,2,1,0:T(8,128)S(1)}, f32[2,2,32,128]{3,2,1,0:T(8,128)S(1)}, u32[]{:S(2)}, u32[]{:S(2)}) %collective-permute-start.5) | collective-permute-done | bytes 65568 | tf_op jit(solution)/shard_map/ppermute | solution.py:307
  18.0 0.0 collective-permute-done.4
  18.0 0.0 collective-permute-done.3
  18.1 2.1 %collective-permute-start.9 = (f32[2,2,32,128]{3,2,1,0:T(8,128)S(1)}, f32[2,2,32,128]{3,2,1,0:T(8,128)S(1)}, u32[]{:S(2)}, u32[]{:S(2)}) collective-permute-start(f32[2,2,32,128]{3,2,1,0:T(8,128)S(1)} %get-tuple-element.64), channel_id=1, source_target_pairs={{0,6},{1,7},{2,4},{3,5},{4,2},{5,3},{6,0},{7,1},{8,14},{9,15},{10,... | collective-permute-start | bytes 196616 | tf_op jit(solution)/shard_map/ppermute | solution.py:307
  20.2 0.0 collective-permute-start.8
  20.2 2.3 %collective-permute-start.7 = (f32[2,2,32,128]{3,2,1,0:T(8,128)S(1)}, f32[2,2,32,128]{3,2,1,0:T(8,128)S(1)}, u32[]{:S(2)}, u32[]{:S(2)}) collective-permute-start(f32[2,2,32,128]{3,2,1,0:T(8,128)S(1)} %get-tuple-element.66), channel_id=1, source_target_pairs={{0,2},{1,3},{2,0},{3,1},{4,6},{5,7},{6,4},{7,5},{8,10},{9,11},{10,... | collective-permute-start | bytes 196616 | tf_op jit(solution)/shard_map/ppermute | solution.py:307
  22.5 0.0 collective-permute-done.2.other
  22.5 0.0 copy-start
  22.5 0.7 copy-done
  23.2 1.9 %bounds.1 = f32[8,136,128]{2,1,0:T(8,128)} custom-call(s32[4]{0:T(128)S(1)} %pad_add_fusion.info, f32[1,4]{1,0:T(1,128)S(1)} %copy-done, f32[2,128,128]{2,1,0:T(8,128)S(1)} %pad_maximum_fusion.mine, f32[2,128,128]{2,1,0:T(8,128)S(1)} %collective-permute-done.2.other, f32[2,128,128]{2,1,0:T(8,128)S(1)} %get-tuple-element.34.masked, ...), custom_call_target="tpu_custom_call" | custom-call | tf_op jit(solution)/shard_map/bounds/pallas_call | solution.py:346
  25.1 3.5 %all-to-all-start = ((f32[8,136,128]{2,1,0:T(8,128)}), f32[8,136,128]{2,1,0:T(8,128)S(1)}, u32[]{:S(2)}, u32[]{:S(2)}) async-start(f32[8,136,128]{2,1,0:T(8,128)} %bounds.1), calls=%async_computation | async-start | bytes 1114112 | tf_op jit(solution)/shard_map/all_to_all | solution.py:411
  28.7 0.0 collective-permute-done.9
  28.7 0.0 collective-permute-done.8
  28.7 0.0 collective-permute-done.7
  28.8 0.1 collective-permute-start.10
  28.9 1.9 %collective-permute-done.10.other = f32[8,2,2,32,128]{4,3,2,1,0:T(8,128)S(1)} collective-permute-done((f32[8,2,2,32,128]{4,3,2,1,0:T(8,128)S(1)}, f32[8,2,2,32,128]{4,3,2,1,0:T(8,128)S(1)}, u32[]{:S(2)}, u32[]{:S(2)}) %collective-permute-start.10) | collective-permute-done | bytes 524320 | tf_op jit(solution)/shard_map/ppermute | solution.py:307
  30.8 1.1 %faces.1 = (f32[16,32,128]{2,1,0:T(8,128)S(1)}, f32[16,32,128]{2,1,0:T(8,128)S(1)}, f32[16,32,128]{2,1,0:T(8,128)S(1)}, f32[16,32,128]{2,1,0:T(8,128)S(1)}, f32[...) custom-call(s32[4]{0:T(128)S(1)} %pad_add_fusion.info, ...), custom_call_target="tpu_custom_call" | custom-call | tf_op jit(solution)/shard_map/faces/pallas_call | solution.py:346
  31.9 10.6 %all-to-all-done.packed = f32[8,136,128]{2,1,0:T(8,128)S(1)} async-done(((f32[8,136,128]{2,1,0:T(8,128)}), f32[8,136,128]{2,1,0:T(8,128)S(1)}, u32[]{:S(2)}, u32[]{:S(2)}) %all-to-all-start) | async-done | bytes 557088 | tf_op jit(solution)/shard_map/all_to_all | solution.py:411
  42.4 3.6 %four_steps.1 = (f32[16,16,128]{2,1,0:T(8,128)S(1)}, f32[16,16,128]{2,1,0:T(8,128)S(1)}, f32[16,8,128]{2,1,0:T(8,128)S(1)}, f32[16,8,128]{2,1,0:T(8,128)S(1)}) custom-call(s32[4]{0:T(128)S(1)} %pad_add_fusion.info, f32[1,4]{1,0:T(1,128)S(1)} %copy-done, f32[8,136,128]{2,1,0:T(8,128)S(1)} %all-to-all-done.packed, ...), custom_call_target="tpu_custom_call" | custom-call | tf_op jit(solution)/shard_map/four_steps/pallas_call | solution.py:422
  46.1 0.1 collective-permute-start.11
  46.2 1.6 %collective-permute-start.12 = (f32[16,8,128]{2,1,0:T(8,128)S(1)}, f32[16,8,128]{2,1,0:T(8,128)S(1)}, u32[]{:S(2)}, u32[]{:S(2)}) collective-permute-start(f32[16,8,128]{2,1,0:T(8,128)S(1)} %get-tuple-element.59), channel_id=1, source_target_pairs={{0,9},{1,8},{2,11},{3,10},{4,13},{5,12},{6,15},{7,14},{8,1},{9,0},... | collective-permute-start | bytes 196616 | tf_op jit(solution)/shard_map/ppermute | solution.py:307
  47.8 0.1 collective-permute-start.13
  47.8 0.1 stack.80.info
  47.9 2.2 %collective-permute-done.12.halo_one = f32[16,8,128]{2,1,0:T(8,128)S(1)} collective-permute-done((f32[16,8,128]{2,1,0:T(8,128)S(1)}, f32[16,8,128]{2,1,0:T(8,128)S(1)}, u32[]{:S(2)}, u32[]{:S(2)}) %collective-permute-start.12) | collective-permute-done | bytes 65568 | tf_op jit(solution)/shard_map/ppermute | solution.py:307
  50.1 0.0 collective-permute-done.13.halo_two
  50.1 0.0 collective-permute-done.11.passed
  50.1 2.9 %three_steps.1 = f32[8,2,2,16,128]{4,3,2,1,0:T(8,128)S(1)} custom-call(s32[5]{0:T(128)S(1)} %stack.80.info, f32[1,4]{1,0:T(1,128)S(1)} %copy-done, f32[8,136,128]{2,1,0:T(8,128)S(1)} %all-to-all-done.packed, f32[16,16,128]{2,1,0:T(8,128)S(1)} %collective-permute-done.11.passed, f32[16,8,128]{2,1,0:T(8,128)S(1)} %collective-permute-done.12.halo_one, ...), custom_call_target="tpu_custom_call" | custom-call | tf_op jit(solution)/shard_map/three_steps/pallas_call | solution.py:439
  53.0 14.5 %all_to_all.10 = f32[8,2,2,16,128]{4,3,2,1,0:T(8,128)S(1)} all-to-all(f32[8,2,2,16,128]{4,3,2,1,0:T(8,128)S(1)} %three_steps.1), channel_id=1, replica_groups=mesh['copy'=2,'tm'=2,'space'=8] {'space'}, dimensions={0} | all-to-all | bytes 524288 | tf_op jit(solution)/shard_map/all_to_all | solution.py:448
  67.5 0.7 copy.9
  68.1 0.7 copy.8
  (12 shorter events, 0.1 us)
Async XLA Ops:
  2.5 9.9 %collective-permute-start = (f32[128,128]{1,0:T(8,128)S(1)}, f32[128,128]{1,0:T(8,128)S(1)}, u32[]{:S(2)}, u32[]{:S(2)}) collective-permute-start(f32[128,128]{1,0:T(8,128)S(1)} %get-tuple-element.32), channel_id=1, source_target_pairs={{0,1},{1,0},{2,3},{3,2},{4,5},{5,4},{6,7},{7,6},{8,9},{9,8},{10,11... | collective-permute-start | bytes 196616 | tf_op jit(solution)/shard_map/ppermute | solution.py:307
  5.5 8.2 %collective-permute-start.1 = (f32[128,128]{1,0:T(8,128)S(1)}, f32[128,128]{1,0:T(8,128)S(1)}, u32[]{:S(2)}, u32[]{:S(2)}) collective-permute-start(f32[128,128]{1,0:T(8,128)S(1)} %get-tuple-element.33), channel_id=1, source_target_pairs={{0,8},{1,2},{2,1},{3,4},{4,3},{5,6},{6,5},{7,15},{8,0},{9,10},{10,... | collective-permute-start | bytes 196616 | tf_op jit(solution)/shard_map/ppermute | solution.py:307
  6.1 11.9 %collective-permute-start.3 = (f32[4,2,2,32,128]{4,3,2,1,0:T(8,128)S(1)}, f32[4,2,2,32,128]{4,3,2,1,0:T(8,128)S(1)}, u32[]{:S(2)}, u32[]{:S(2)}) collective-permute-start(f32[4,2,2,32,128]{4,3,2,1,0:T(8,128)S(1)} %get-tuple-element.39), channel_id=1, source_target_pairs={{0,1},{1,0},{2,3},{3,2},{4,5},{5,4},{6,7},{7,6},{8,9},{9,8},{10,11... | collective-permute-start | bytes 786440 | tf_op jit(solution)/shard_map/ppermute | solution.py:307
  9.3 6.8 %collective-permute-start.6 = (f32[2,2,32,128]{3,2,1,0:T(8,128)S(1)}, f32[2,2,32,128]{3,2,1,0:T(8,128)S(1)}, u32[]{:S(2)}, u32[]{:S(2)}) collective-permute-start(f32[2,2,32,128]{3,2,1,0:T(8,128)S(1)} %get-tuple-element.68), channel_id=1, source_target_pairs={{0,6},{1,7},{2,4},{3,5},{4,2},{5,3},{6,0},{7,1},{8,14},{9,15},{10,... | collective-permute-start | bytes 196616 | tf_op jit(solution)/shard_map/ppermute | solution.py:307
  10.4 7.7 %collective-permute-start.5 = (f32[2,2,32,128]{3,2,1,0:T(8,128)S(1)}, f32[2,2,32,128]{3,2,1,0:T(8,128)S(1)}, u32[]{:S(2)}, u32[]{:S(2)}) collective-permute-start(f32[2,2,32,128]{3,2,1,0:T(8,128)S(1)} %get-tuple-element.69), channel_id=1, source_target_pairs={{0,4},{1,5},{2,6},{3,7},{4,0},{5,1},{6,2},{7,3},{8,12},{9,13},{10,... | collective-permute-start | bytes 196616 | tf_op jit(solution)/shard_map/ppermute | solution.py:307
  12.4 5.7 %collective-permute-start.4 = (f32[2,2,32,128]{3,2,1,0:T(8,128)S(1)}, f32[2,2,32,128]{3,2,1,0:T(8,128)S(1)}, u32[]{:S(2)}, u32[]{:S(2)}) collective-permute-start(f32[2,2,32,128]{3,2,1,0:T(8,128)S(1)} %get-tuple-element.70), channel_id=1, source_target_pairs={{0,2},{1,3},{2,0},{3,1},{4,6},{5,7},{6,4},{7,5},{8,10},{9,11},{10,... | collective-permute-start | bytes 196616 | tf_op jit(solution)/shard_map/ppermute | solution.py:307
  13.7 8.8 %collective-permute-start.2 = (f32[2,128,128]{2,1,0:T(8,128)S(1)}, f32[2,128,128]{2,1,0:T(8,128)S(1)}, u32[]{:S(2)}, u32[]{:S(2)}) collective-permute-start(f32[2,128,128]{2,1,0:T(8,128)S(1)} %pad_maximum_fusion.mine), channel_id=1, source_target_pairs={{0,8},{1,9},{2,10},{3,11},{4,12},{5,13},{6,14},{7,15},{8,0},{9,1},... | collective-permute-start | bytes 393224 | tf_op jit(solution)/shard_map/ppermute | solution.py:307
  18.1 10.6 %collective-permute-start.9 = (f32[2,2,32,128]{3,2,1,0:T(8,128)S(1)}, f32[2,2,32,128]{3,2,1,0:T(8,128)S(1)}, u32[]{:S(2)}, u32[]{:S(2)}) collective-permute-start(f32[2,2,32,128]{3,2,1,0:T(8,128)S(1)} %get-tuple-element.64), channel_id=1, source_target_pairs={{0,6},{1,7},{2,4},{3,5},{4,2},{5,3},{6,0},{7,1},{8,14},{9,15},{10,... | collective-permute-start | bytes 196616 | tf_op jit(solution)/shard_map/ppermute | solution.py:307
  20.2 8.5 %collective-permute-start.8 = (f32[2,2,32,128]{3,2,1,0:T(8,128)S(1)}, f32[2,2,32,128]{3,2,1,0:T(8,128)S(1)}, u32[]{:S(2)}, u32[]{:S(2)}) collective-permute-start(f32[2,2,32,128]{3,2,1,0:T(8,128)S(1)} %get-tuple-element.65), channel_id=1, source_target_pairs={{0,4},{1,5},{2,6},{3,7},{4,0},{5,1},{6,2},{7,3},{8,12},{9,13},{10,... | collective-permute-start | bytes 196616 | tf_op jit(solution)/shard_map/ppermute | solution.py:307
  20.2 8.5 %collective-permute-start.7 = (f32[2,2,32,128]{3,2,1,0:T(8,128)S(1)}, f32[2,2,32,128]{3,2,1,0:T(8,128)S(1)}, u32[]{:S(2)}, u32[]{:S(2)}) collective-permute-start(f32[2,2,32,128]{3,2,1,0:T(8,128)S(1)} %get-tuple-element.66), channel_id=1, source_target_pairs={{0,2},{1,3},{2,0},{3,1},{4,6},{5,7},{6,4},{7,5},{8,10},{9,11},{10,... | collective-permute-start | bytes 196616 | tf_op jit(solution)/shard_map/ppermute | solution.py:307
  22.5 0.7 copy-start
  25.1 17.3 %all-to-all-start = ((f32[8,136,128]{2,1,0:T(8,128)}), f32[8,136,128]{2,1,0:T(8,128)S(1)}, u32[]{:S(2)}, u32[]{:S(2)}) async-start(f32[8,136,128]{2,1,0:T(8,128)} %bounds.1), calls=%async_computation | async-start | bytes 1114112 | tf_op jit(solution)/shard_map/all_to_all | solution.py:411
  28.8 2.0 %collective-permute-start.10 = (f32[8,2,2,32,128]{4,3,2,1,0:T(8,128)S(1)}, f32[8,2,2,32,128]{4,3,2,1,0:T(8,128)S(1)}, u32[]{:S(2)}, u32[]{:S(2)}) collective-permute-start(f32[8,2,2,32,128]{4,3,2,1,0:T(8,128)S(1)} %bitcast_dynamic-update-slice_fusion.mine), channel_id=1, source_target_pairs={{0,8},{1,9},{2,10},{3,11},{4,12},{5,13},{6,14},{7,15},{8,0},{9,1},... | collective-permute-start | bytes 1572872 | tf_op jit(solution)/shard_map/ppermute | solution.py:307
  46.1 4.0 %collective-permute-start.11 = (f32[16,16,128]{2,1,0:T(8,128)S(1)}, f32[16,16,128]{2,1,0:T(8,128)S(1)}, u32[]{:S(2)}, u32[]{:S(2)}) collective-permute-start(f32[16,16,128]{2,1,0:T(8,128)S(1)} %get-tuple-element.58.advanced), channel_id=1, source_target_pairs={{0,8},{1,9},{2,10},{3,11},{4,12},{5,13},{6,14},{7,15},{8,0},{9,1},... | collective-permute-start | bytes 393224 | tf_op jit(solution)/shard_map/ppermute | solution.py:307
  46.2 3.9 %collective-permute-start.12 = (f32[16,8,128]{2,1,0:T(8,128)S(1)}, f32[16,8,128]{2,1,0:T(8,128)S(1)}, u32[]{:S(2)}, u32[]{:S(2)}) collective-permute-start(f32[16,8,128]{2,1,0:T(8,128)S(1)} %get-tuple-element.59), channel_id=1, source_target_pairs={{0,9},{1,8},{2,11},{3,10},{4,13},{5,12},{6,15},{7,14},{8,1},{9,0},... | collective-permute-start | bytes 196616 | tf_op jit(solution)/shard_map/ppermute | solution.py:307
  47.8 2.3 %collective-permute-start.13 = (f32[16,8,128]{2,1,0:T(8,128)S(1)}, f32[16,8,128]{2,1,0:T(8,128)S(1)}, u32[]{:S(2)}, u32[]{:S(2)}) collective-permute-start(f32[16,8,128]{2,1,0:T(8,128)S(1)} %get-tuple-element.60), channel_id=1, source_target_pairs={{0,8},{1,10},{2,9},{3,12},{4,11},{5,14},{6,13},{7,15},{8,0},{9,2},... | collective-permute-start | bytes 196616 | tf_op jit(solution)/shard_map/ppermute | solution.py:307

commit v4 on v3

--- a/solution.py
+++ b/solution.py
@@ -28,9 +28,16 @@
     return jnp.concatenate(parts, axis=0) if len(parts) > 1 else parts[0]
 
 
-def load_kernel(info, initial, source, diffusion, wind, buildings, masked, winds, state, forcing, edge_one, edge_two, *rest):
-    fresh, early, late, solid, sems = rest
-    pairs = ((diffusion, fresh), (buildings, solid), (wind, winds), (initial.at[0], early), (source.at[0], late))
+def load_kernel(info, initial, source, diffusion, wind, buildings, strength, *rest):
+    masked, winds, state, forcing, edge_one, edge_two, rates, fresh, early, late, solid, steps, sems = rest
+    pairs = (
+        (diffusion, fresh),
+        (buildings, solid),
+        (wind, winds),
+        (initial.at[0], early),
+        (source.at[0], late),
+        (strength, steps),
+    )
     copies = [pltpu.make_async_copy(*pair, sems.at[number]) for number, pair in enumerate(pairs)]
     for copy in copies:
         copy.start()
@@ -48,23 +55,28 @@
         copy.wait()
     state[...] = early[...] * opened
     forcing[...] = late[...].astype(jnp.float32) * opened
+    place = lax.broadcasted_iota(jnp.int32, rates.shape, 0)
+    table = jnp.zeros(rates.shape, jnp.float32)
+    for k in range(FINE):
+        table = jnp.where(place == k, steps[0, k], table)
+    rates[...] = table
 
 
 def pack_shared(rows, width, info, masked, wind, same, across):
-    first, spot = info[0] == 0, info[1]
+    first, spot, lead = info[0] == 0, info[1], info[4] == 0
     half = same.shape[0]
+    swap = spot % 2 == 1
     for layer in range(masked.shape[0]):
-        pair = (
-            jnp.where(first, masked[layer], wind[1, layer]),
-            jnp.where(first, wind[0, layer], wind[2, layer]),
+        field = jnp.where(
+            first,
+            jnp.where(lead, masked[layer], wind[0, layer]),
+            jnp.where(lead, wind[1, layer], wind[2, layer]),
         )
-        for field in range(2):
-            for place in range(half):
-                even = windows(pair[field], 2 * place, rows, width)
-                odd = windows(pair[field], 2 * place + 1, rows, width)
-                swap = spot % 2 == 1
-                same[place ^ (spot // 2), field, layer] = jnp.where(swap, odd, even)
-                across[place ^ (spot // 2), field, layer] = jnp.where(swap, even, odd)
+        for place in range(half):
+            even = windows(field, 2 * place, rows, width)
+            odd = windows(field, 2 * place + 1, rows, width)
+            same[place ^ (spot // 2), layer] = jnp.where(swap, odd, even)
+            across[place ^ (spot // 2), layer] = jnp.where(swap, even, odd)
 
 
 def pack_own(rows, width, state, forcing, packed):
@@ -131,7 +143,7 @@
                 sums[number] = sums[number] + value + pltpu.roll(value, 1, 1)
             still = 1.0 + 2.0 * sums[0]
             for k in range(FINE):
-                peaks[k] = jnp.maximum(peaks[k], still + rates[0, k] * sums[1])
+                peaks[k] = jnp.maximum(peaks[k], still + rates[pl.ds(k, 1)] * sums[1])
     bounds = jnp.zeros((8, lanes), jnp.float32)
     place = lax.broadcasted_iota(jnp.int32, (8, lanes), 0)
     for k in range(FINE):
@@ -146,10 +158,10 @@
     return pltpu.roll(values, values.shape[axis] - 1, axis)
 
 
-def face_kernel(info, mine, other, *faces):
-    count, layers, width, lanes = mine.shape[0], *mine.shape[2:]
+def face_kernel(info, mine, beside, other, other_beside, *faces):
+    count, layers, width, lanes = mine.shape
     total = count * layers
-    first, own = info[0] == 0, info[1]
+    first, own, lead = info[0] == 0, info[1], info[4] == 0
     row = lax.broadcasted_iota(jnp.int32, (width, lanes), 0)
     lane = lax.broadcasted_iota(jnp.int32, (width, lanes), 1)
     inner_row = row < width - 1
@@ -158,8 +170,12 @@
 
     def fields(place):
         spot, layer = (place // layers) ^ own, place % layers
-        here = (mine[spot, 0, layer], mine[spot, 1, layer])
-        there = (other[spot, 0, layer], other[spot, 1, layer])
+
+        def ordered(one, two):
+            one, two = one[spot, layer], two[spot, layer]
+            return jnp.where(lead, one, two), jnp.where(lead, two, one)
+
+        here, there = ordered(mine, beside), ordered(other, other_beside)
         masked = jnp.where(first, here[0], there[0])
         wind_x = jnp.where(first, here[1], there[1])
         wind_y = jnp.where(first, there[0], here[0])
@@ -258,7 +274,7 @@
     bounds = bounds_of(packed)
     for k in range(FINE):
         near, far = coefficients(bounds[k : k + 1])
-        one_step(total, width, layers, state, residual, ahead, faces, packed, rates[0, k], near, far)
+        one_step(total, width, layers, state, residual, ahead, faces, packed, rates[pl.ds(k, 1)], near, far)
         if k == FINE - 2:
             third[...] = state[:total, LOW : LOW + rows]
     advanced[...] = state[:total, LOW : LOW + rows]
@@ -287,7 +303,7 @@
     bounds = bounds_of(packed)
     for k in range(FINE - 1):
         near, far = coefficients(bounds[k : k + 1])
-        one_step(total, width, layers, state, residual, ahead, faces, packed, rates[0, k], near, far)
+        one_step(total, width, layers, state, residual, ahead, faces, packed, rates[pl.ds(k, 1)], near, far)
     first = info[0] == 0
     final = jnp.where(first, third[...], state[:total, LOW : LOW + rows])
     shape = out.shape[0:1] + out.shape[2:]
@@ -295,7 +311,7 @@
     out[:, 1] = final.reshape(shape)
 
 
-def swapped(array, sizes, partner):
+def swapped(array, sizes, partner, flip=0):
     copies, blocks, count = sizes
     pairs = []
     for c in range(copies):
@@ -303,7 +319,7 @@
             for s in range(count):
                 target = partner(t, s)
                 if target is not None:
-                    pairs.append(((c * blocks + t) * count + s, (c * blocks + target[0]) * count + target[1]))
+                    pairs.append(((c * blocks + t) * count + s, ((c ^ flip) * blocks + target[0]) * count + target[1]))
     return lax.ppermute(array, AXES, pairs)
 
 
@@ -353,17 +369,18 @@
         )(*operands)
 
     half = block % 2
-    flags = [half, place, place > 0, place < count - 1]
+    lead = lax.axis_index("copy") % 2
+    flags = [half, place, place > 0, place < count - 1, lead]
     info = jnp.stack([jnp.asarray(flag).astype(jnp.int32) for flag in flags])
     slab = struct(layers, depth, lanes)
     outer = struct(depth, lanes)
     hold = pltpu.VMEM((layers, depth, lanes), jnp.float32)
     anywhere = pl.BlockSpec(memory_space=pltpu.HBM)
-    arrays = (initial, source, diffusion, wind_field, buildings)
-    masked, winds, state, forcing, edge_one, edge_two = call(
+    arrays = (initial, source, diffusion, wind_field, buildings, strength)
+    masked, winds, state, forcing, edge_one, edge_two, rates = call(
         load_kernel,
-        [slab, struct(3, layers, depth, lanes), slab, slab, outer, outer],
-        [SMEM] + [anywhere] * 5,
+        [slab, struct(3, layers, depth, lanes), slab, slab, outer, outer, struct(8, lanes)],
+        [SMEM] + [anywhere] * 6,
         "load",
         info,
         *(pltpu.with_memory_space_constraint(array, pltpu.HBM) for array in arrays),
@@ -372,14 +389,15 @@
             hold,
             pltpu.VMEM((layers, depth, lanes), source.dtype),
             pltpu.VMEM((layers, depth, lanes), jnp.int32),
-            pltpu.SemaphoreType.DMA((5,)),
+            pltpu.SMEM(strength.shape, jnp.float32),
+            pltpu.SemaphoreType.DMA((6,)),
         ],
     )
     edge_one = swapped(edge_one, sizes, lambda t, s: (t, s ^ 1))
     edge_two = swapped(edge_two, sizes, outer_partner(count))
     same, across = call(
         functools.partial(pack_shared, rows, width),
-        [struct(count // 2, 2, layers, width, lanes)] * 2,
+        [struct(count // 2, layers, width, lanes)] * 2,
         [SMEM] + [VMEM] * 2,
         "pack_shared",
         info,
@@ -387,17 +405,15 @@
         winds,
     )
     across = swapped(across, sizes, lambda t, s: (t, s ^ 1))
-    even = [swapped(same[step], sizes, lambda t, s: (t, s ^ (2 * step))) for step in range(1, count // 2)]
-    across, *even = lax.optimization_barrier((across, *even))
     edges = jnp.stack([edge_one, edge_two])
     other_edges = swapped(edges, sizes, lambda t, s: (t ^ 1, s))
     (packed,) = call(
         functools.partial(bound_kernel, rows, width),
         [struct(count, 2 * layers * width + 8, lanes)],
-        [SMEM] * 2 + [VMEM] * 6,
+        [SMEM] + [VMEM] * 7,
         "bounds",
         info,
-        strength,
+        rates,
         edges,
         other_edges,
         masked,
@@ -405,13 +421,27 @@
         state,
         forcing,
     )
-    odd = [swapped(across[step], sizes, lambda t, s: (t, s ^ (2 * step))) for step in range(1, count // 2)]
-    parts = [part for pair in zip([same[0], *even], [across[0], *odd]) for part in pair]
+    pieces = jnp.stack([same, across], axis=1)
+    parts = [pieces[0]]
+    for step in range(1, count // 2):
+        parts.append(swapped(pieces[step], sizes, lambda t, s: (t, s ^ (2 * step))))
     *parts, _ = lax.optimization_barrier((*parts, packed))
     packed = lax.all_to_all(packed, "space", 0, 0, tiled=True)
-    mine = jnp.stack(parts)
+    mine = jnp.concatenate(parts)
+    beside = swapped(mine, sizes, lambda t, s: (t, s), 1)
     other = swapped(mine, sizes, lambda t, s: (t ^ 1, s))
-    faces = call(face_kernel, [struct(total, width, lanes)] * 6, [SMEM] + [VMEM] * 2, "faces", info, mine, other)
+    other_beside = swapped(beside, sizes, lambda t, s: (t ^ 1, s))
+    faces = call(
+        face_kernel,
+        [struct(total, width, lanes)] * 6,
+        [SMEM] + [VMEM] * 4,
+        "faces",
+        info,
+        mine,
+        beside,
+        other,
+        other_beside,
+    )
 
     edge = min(rows, LOW)
     scratch = [
@@ -422,12 +452,12 @@
     advanced, third, edge_one, edge_two = pl.pallas_call(
         functools.partial(first_kernel, rows, width, layers),
         out_shape=[struct(total, rows, lanes)] * 2 + [struct(total, edge, lanes)] * 2,
-        in_specs=[SMEM] * 2 + [VMEM] * 7,
+        in_specs=[SMEM] + [VMEM] * 8,
         out_specs=[VMEM] * 4,
         scratch_shapes=scratch,
         compiler_params=params,
         name="four_steps",
-    )(info, strength, packed, *faces)
+    )(info, rates, packed, *faces)
 
     if blocks == 2:
         own = swapped(advanced, sizes, lambda t, s: (1 - t, s))
@@ -439,12 +469,12 @@
     result = pl.pallas_call(
         functools.partial(second_kernel, rows, width, layers),
         out_shape=struct(count, 2, layers, rows, lanes),
-        in_specs=[SMEM] * 2 + [VMEM] * 12,
+        in_specs=[SMEM] + [VMEM] * 13,
         out_specs=VMEM,
         scratch_shapes=scratch,
         compiler_params=params,
         name="three_steps",
-    )(info, strength, packed, own, one, two, advanced, third, *faces)
+    )(info, rates, packed, own, one, two, advanced, third, *faces)
     result = lax.all_to_all(result, "space", 0, 0, tiled=True)
     result = result.transpose(1, 2, 0, 3, 4).reshape(2, 1, layers, depth, lanes)
     return result[0], result[1]

time: 69.1 us -> 64.3 us (0.931)
  waiting for transfers between devices: 18.9 us -> 15.9 us
  starting transfers between devices: 20.4 us -> 19.3 us
    all_to_all x1, waiting for transfers between devices: 10.6 us -> 4.46 us  [shards(): packed = lax.all_to_all(packed, 'space', 0, 0, tiled=True)]
    ppermute x14 -> x13, waiting for transfers between devices: 8.31 us -> 11.4 us  [swapped(): return lax.ppermute(array, AXES, pairs)]
    ppermute x14 -> x13, starting transfers between devices: 16.9 us -> 14.3 us  [swapped(): return lax.ppermute(array, AXES, pairs)]
    all_to_all x1, starting transfers between devices: 3.54 us -> 5.02 us  [shards(): packed = lax.all_to_all(packed, 'space', 0, 0, tiled=True)]
  transfers between devices with their start and end apart: 15 -> 14, of which waited for: 5 -> 5; matrix products, arithmetic and copies ran while one was open for 0% -> 0% of each run, Pallas kernels for 5% -> 6%
where the time goes in v4:
time: 64.3 us; the launch traced here: 64 us
  starting transfers between devices  19.3 us (30%)
  waiting for transfers between devices  15.9 us (25%)
  blocking collectives  14.5 us (23%)
  Pallas kernels  11.9 us (19%)
  local copies, waits for them, and re-layouts  1.54 us (2%)
  between operations  0.78 us (1%)
    all_to_all x1, blocking collectives, shards(): result = lax.all_to_all(result, 'space', 0, 0, tiled=True)  14.5 us
    ppermute x13, starting transfers between devices, swapped(): return lax.ppermute(array, AXES, pairs)  14.3 us
    ppermute x13, waiting for transfers between devices, swapped(): return lax.ppermute(array, AXES, pairs)  11.4 us
    pallas_call x4, Pallas kernels, call(): pl.pallas_call(kernel, out_shape=outs, in_specs=in_specs, out_specs=[VMEM...  5.41 us
    all_to_all x1, starting transfers between devices, shards(): packed = lax.all_to_all(packed, 'space', 0, 0, tiled=True)  5.02 us
    all_to_all x1, waiting for transfers between devices, shards(): packed = lax.all_to_all(packed, 'space', 0, 0, tiled=True)  4.46 us
    pallas_call x1, Pallas kernels, shards(): pl.pallas_call(functools.partial(first_kernel, rows, width, layers), out_...  3.65 us
    pallas_call x1, Pallas kernels, shards(): pl.pallas_call(functools.partial(second_kernel, rows, width, layers), out...  2.88 us
  transfers between devices with their start and end apart: 14, of which 5 were waited for; matrix products, arithmetic and copies ran while one was open for 0% of the time, Pallas kernels for 6%

profile of v4, /device:TPU:0, one launch (start us, length us, event | category | flops | bytes accessed | tf_op | source)
XLA Modules:
  0.0 64.0 jit_solution(6001051899743825172)
XLA Ops:
  0.7 0.1 stack.68.info
  0.7 1.8 %load.1 = (f32[2,128,128]{2,1,0:T(8,128)S(1)}, f32[3,2,128,128]{3,2,1,0:T(8,128)S(1)}, f32[2,128,128]{2,1,0:T(8,128)S(1)}, f32[2,128,128]{2,1,0:T(8,128)S(1)}, f...) custom-call(s32[5]{0:T(128)S(1)} %stack.68.info, f32[1,2,128,128]{3,2,1,0:T(8,128)} %initial.1, ...), custom_call_target="tpu_custom_call" | custom-call | tf_op jit(solution)/shard_map/load/pallas_call | solution.py:362
  2.5 3.0 %collective-permute-start = (f32[128,128]{1,0:T(8,128)S(1)}, f32[128,128]{1,0:T(8,128)S(1)}, u32[]{:S(2)}, u32[]{:S(2)}) collective-permute-start(f32[128,128]{1,0:T(8,128)S(1)} %get-tuple-element.26), channel_id=1, source_target_pairs={{0,1},{1,0},{2,3},{3,2},{4,5},{5,4},{6,7},{7,6},{8,9},{9,8},{10,11... | collective-permute-start | bytes 196616 | tf_op jit(solution)/shard_map/ppermute | solution.py:323
  5.6 0.0 collective-permute-start.1
  5.6 0.6 pack_shared.1
  6.2 3.1 %collective-permute-start.3 = (f32[4,2,32,128]{3,2,1,0:T(8,128)S(1)}, f32[4,2,32,128]{3,2,1,0:T(8,128)S(1)}, u32[]{:S(2)}, u32[]{:S(2)}) collective-permute-start(f32[4,2,32,128]{3,2,1,0:T(8,128)S(1)} %get-tuple-element.33), channel_id=1, source_target_pairs={{0,1},{1,0},{2,3},{3,2},{4,5},{5,4},{6,7},{7,6},{8,9},{9,8},{10,11... | collective-permute-start | bytes 393224 | tf_op jit(solution)/shard_map/ppermute | solution.py:323
  9.3 0.0 collective-permute-done
  9.3 0.0 collective-permute-done.1
  9.3 0.1 collective-permute-start.2
  9.4 2.8 %collective-permute-done.3 = f32[4,2,32,128]{3,2,1,0:T(8,128)S(1)} collective-permute-done((f32[4,2,32,128]{3,2,1,0:T(8,128)S(1)}, f32[4,2,32,128]{3,2,1,0:T(8,128)S(1)}, u32[]{:S(2)}, u32[]{:S(2)}) %collective-permute-start.3) | collective-permute-done | bytes 131104 | tf_op jit(solution)/shard_map/ppermute | solution.py:323
  12.2 4.2 %collective-permute-start.6 = (f32[2,2,32,128]{3,2,1,0:T(8,128)S(1)}, f32[2,2,32,128]{3,2,1,0:T(8,128)S(1)}, u32[]{:S(2)}, u32[]{:S(2)}) collective-permute-start(f32[2,2,32,128]{3,2,1,0:T(8,128)S(1)} %get-tuple-element.50), channel_id=1, source_target_pairs={{0,6},{1,7},{2,4},{3,5},{4,2},{5,3},{6,0},{7,1},{8,14},{9,15},{10,... | collective-permute-start | bytes 196616 | tf_op jit(solution)/shard_map/ppermute | solution.py:323
  16.4 0.0 collective-permute-start.4
  16.4 0.6 collective-permute-start.5
  17.0 0.0 collective-permute-done.2.other
  17.0 1.9 %bounds.1 = f32[8,136,128]{2,1,0:T(8,128)} custom-call(s32[5]{0:T(128)S(1)} %stack.68.info, f32[8,128]{1,0:T(8,128)S(1)} %get-tuple-element.25.rates, f32[2,128,128]{2,1,0:T(8,128)S(1)} %pad_maximum_fusion.mine, f32[2,128,128]{2,1,0:T(8,128)S(1)} %collective-permute-done.2.other, f32[2,128,128]{2,1,0:T(8,128)S(1)} %get-tuple-element.28.masked, ...), custom_call_target="tpu_custom_call" | custom-call | tf_op jit(solution)/shard_map/bounds/pallas_call | solution.py:362
  19.0 5.0 %all-to-all-start = ((f32[8,136,128]{2,1,0:T(8,128)}), f32[8,136,128]{2,1,0:T(8,128)S(1)}, u32[]{:S(2)}, u32[]{:S(2)}) async-start(f32[8,136,128]{2,1,0:T(8,128)} %bounds.1), calls=%async_computation | async-start | bytes 1114112 | tf_op jit(solution)/shard_map/all_to_all | solution.py:429
  24.0 0.0 collective-permute-done.6
  24.0 0.0 collective-permute-done.4
  24.0 0.0 collective-permute-done.5
  24.1 1.6 %collective-permute-start.7 = (f32[8,2,32,128]{3,2,1,0:T(8,128)S(1)}, f32[8,2,32,128]{3,2,1,0:T(8,128)S(1)}, u32[]{:S(2)}, u32[]{:S(2)}) collective-permute-start(f32[8,2,32,128]{3,2,1,0:T(8,128)S(1)} %constant_dynamic-update-slice_fusion.mine), channel_id=1, source_target_pairs={{0,16},{1,17},{2,18},{3,19},{4,20},{5,21},{6,22},{7,23},{8,24},{9,... | collective-permute-start | bytes 786440 | tf_op jit(solution)/shard_map/ppermute | solution.py:323
  25.6 0.0 collective-permute-start.8
  25.6 4.9 %collective-permute-done.7.beside = f32[8,2,32,128]{3,2,1,0:T(8,128)S(1)} collective-permute-done((f32[8,2,32,128]{3,2,1,0:T(8,128)S(1)}, f32[8,2,32,128]{3,2,1,0:T(8,128)S(1)}, u32[]{:S(2)}, u32[]{:S(2)}) %collective-permute-start.7) | collective-permute-done | bytes 262176 | tf_op jit(solution)/shard_map/ppermute | solution.py:323
  30.5 0.0 collective-permute-start.9
  30.5 0.0 collective-permute-done.8.other
  30.5 1.5 %collective-permute-done.9.other_beside = f32[8,2,32,128]{3,2,1,0:T(8,128)S(1)} collective-permute-done((f32[8,2,32,128]{3,2,1,0:T(8,128)S(1)}, f32[8,2,32,128]{3,2,1,0:T(8,128)S(1)}, u32[]{:S(2)}, u32[]{:S(2)}) %collective-permute-start.9) | collective-permute-done | bytes 262176 | tf_op jit(solution)/shard_map/ppermute | solution.py:323
  32.0 1.1 %faces.1 = (f32[16,32,128]{2,1,0:T(8,128)S(1)}, f32[16,32,128]{2,1,0:T(8,128)S(1)}, f32[16,32,128]{2,1,0:T(8,128)S(1)}, f32[16,32,128]{2,1,0:T(8,128)S(1)}, f32[...) custom-call(s32[5]{0:T(128)S(1)} %stack.68.info, f32[8,2,32,128]{3,2,1,0:T(8,128)S(1)} %constant_dynamic-update-slice_fusion.mine, ...), custom_call_target="tpu_custom_call" | custom-call | tf_op jit(solution)/shard_map/faces/pallas_call | solution.py:362
  33.2 4.5 %all-to-all-done.packed = f32[8,136,128]{2,1,0:T(8,128)S(1)} async-done(((f32[8,136,128]{2,1,0:T(8,128)}), f32[8,136,128]{2,1,0:T(8,128)S(1)}, u32[]{:S(2)}, u32[]{:S(2)}) %all-to-all-start) | async-done | bytes 557088 | tf_op jit(solution)/shard_map/all_to_all | solution.py:429
  37.6 3.6 %four_steps.1 = (f32[16,16,128]{2,1,0:T(8,128)S(1)}, f32[16,16,128]{2,1,0:T(8,128)S(1)}, f32[16,8,128]{2,1,0:T(8,128)S(1)}, f32[16,8,128]{2,1,0:T(8,128)S(1)}) custom-call(s32[5]{0:T(128)S(1)} %stack.68.info, f32[8,128]{1,0:T(8,128)S(1)} %get-tuple-element.25.rates, f32[8,136,128]{2,1,0:T(8,128)S(1)} %all-to-all-done.packed, ...), custom_call_target="tpu_custom_call" | custom-call | tf_op jit(solution)/shard_map/four_steps/pallas_call | solution.py:452
  41.3 0.1 collective-permute-start.10
  41.4 1.6 %collective-permute-start.11 = (f32[16,8,128]{2,1,0:T(8,128)S(1)}, f32[16,8,128]{2,1,0:T(8,128)S(1)}, u32[]{:S(2)}, u32[]{:S(2)}) collective-permute-start(f32[16,8,128]{2,1,0:T(8,128)S(1)} %get-tuple-element.45), channel_id=1, source_target_pairs={{0,9},{1,8},{2,11},{3,10},{4,13},{5,12},{6,15},{7,14},{8,1},{9,0},... | collective-permute-start | bytes 196616 | tf_op jit(solution)/shard_map/ppermute | solution.py:323
  42.9 0.1 collective-permute-start.12
  43.0 0.1 stack.65.info
  43.1 2.2 %collective-permute-done.11.halo_one = f32[16,8,128]{2,1,0:T(8,128)S(1)} collective-permute-done((f32[16,8,128]{2,1,0:T(8,128)S(1)}, f32[16,8,128]{2,1,0:T(8,128)S(1)}, u32[]{:S(2)}, u32[]{:S(2)}) %collective-permute-start.11) | collective-permute-done | bytes 65568 | tf_op jit(solution)/shard_map/ppermute | solution.py:323
  45.2 0.0 collective-permute-done.12.halo_two
  45.2 0.0 collective-permute-done.10.passed
  45.2 2.9 %three_steps.1 = f32[8,2,2,16,128]{4,3,2,1,0:T(8,128)S(1)} custom-call(s32[5]{0:T(128)S(1)} %stack.65.info, f32[8,128]{1,0:T(8,128)S(1)} %get-tuple-element.25.rates, f32[8,136,128]{2,1,0:T(8,128)S(1)} %all-to-all-done.packed, f32[16,16,128]{2,1,0:T(8,128)S(1)} %collective-permute-done.10.passed, f32[16,8,128]{2,1,0:T(8,128)S(1)} %collective-permute-done.11.halo_one, ...), custom_call_target="tpu_custom_call" | custom-call | tf_op jit(solution)/shard_map/three_steps/pallas_call | solution.py:469
  48.1 14.5 %all_to_all.10 = f32[8,2,2,16,128]{4,3,2,1,0:T(8,128)S(1)} all-to-all(f32[8,2,2,16,128]{4,3,2,1,0:T(8,128)S(1)} %three_steps.1), channel_id=1, replica_groups=mesh['copy'=2,'tm'=2,'space'=8] {'space'}, dimensions={0} | all-to-all | bytes 524288 | tf_op jit(solution)/shard_map/all_to_all | solution.py:478
  62.7 0.7 %copy.9 = f32[1,2,8,16,128]{4,3,2,1,0:T(8,128)} copy(f32[1,2,8,16,128]{4,3,1,0,2:T(8,128)S(1)} %get-tuple-element.48) | data formatting | bytes 262144 | tf_op jit(solution)/shard_map/slice | solution.py:480
  63.3 0.7 %copy.8 = f32[1,2,8,16,128]{4,3,2,1,0:T(8,128)} copy(f32[1,2,8,16,128]{4,3,1,0,2:T(8,128)S(1)} %get-tuple-element.49) | data formatting | bytes 262144 | tf_op jit(solution)/shard_map/slice | solution.py:480
  (7 shorter events, 0.1 us)
Async XLA Ops:
  2.5 6.7 %collective-permute-start = (f32[128,128]{1,0:T(8,128)S(1)}, f32[128,128]{1,0:T(8,128)S(1)}, u32[]{:S(2)}, u32[]{:S(2)}) collective-permute-start(f32[128,128]{1,0:T(8,128)S(1)} %get-tuple-element.26), channel_id=1, source_target_pairs={{0,1},{1,0},{2,3},{3,2},{4,5},{5,4},{6,7},{7,6},{8,9},{9,8},{10,11... | collective-permute-start | bytes 196616 | tf_op jit(solution)/shard_map/ppermute | solution.py:323
  5.6 3.7 %collective-permute-start.1 = (f32[128,128]{1,0:T(8,128)S(1)}, f32[128,128]{1,0:T(8,128)S(1)}, u32[]{:S(2)}, u32[]{:S(2)}) collective-permute-start(f32[128,128]{1,0:T(8,128)S(1)} %get-tuple-element.27), channel_id=1, source_target_pairs={{0,8},{1,2},{2,1},{3,4},{4,3},{5,6},{6,5},{7,15},{8,0},{9,10},{10,... | collective-permute-start | bytes 196616 | tf_op jit(solution)/shard_map/ppermute | solution.py:323
  6.2 6.0 %collective-permute-start.3 = (f32[4,2,32,128]{3,2,1,0:T(8,128)S(1)}, f32[4,2,32,128]{3,2,1,0:T(8,128)S(1)}, u32[]{:S(2)}, u32[]{:S(2)}) collective-permute-start(f32[4,2,32,128]{3,2,1,0:T(8,128)S(1)} %get-tuple-element.33), channel_id=1, source_target_pairs={{0,1},{1,0},{2,3},{3,2},{4,5},{5,4},{6,7},{7,6},{8,9},{9,8},{10,11... | collective-permute-start | bytes 393224 | tf_op jit(solution)/shard_map/ppermute | solution.py:323
  9.3 7.7 %collective-permute-start.2 = (f32[2,128,128]{2,1,0:T(8,128)S(1)}, f32[2,128,128]{2,1,0:T(8,128)S(1)}, u32[]{:S(2)}, u32[]{:S(2)}) collective-permute-start(f32[2,128,128]{2,1,0:T(8,128)S(1)} %pad_maximum_fusion.mine), channel_id=1, source_target_pairs={{0,8},{1,9},{2,10},{3,11},{4,12},{5,13},{6,14},{7,15},{8,0},{9,1},... | collective-permute-start | bytes 393224 | tf_op jit(solution)/shard_map/ppermute | solution.py:323
  12.2 11.8 %collective-permute-start.6 = (f32[2,2,32,128]{3,2,1,0:T(8,128)S(1)}, f32[2,2,32,128]{3,2,1,0:T(8,128)S(1)}, u32[]{:S(2)}, u32[]{:S(2)}) collective-permute-start(f32[2,2,32,128]{3,2,1,0:T(8,128)S(1)} %get-tuple-element.50), channel_id=1, source_target_pairs={{0,6},{1,7},{2,4},{3,5},{4,2},{5,3},{6,0},{7,1},{8,14},{9,15},{10,... | collective-permute-start | bytes 196616 | tf_op jit(solution)/shard_map/ppermute | solution.py:323
  16.4 7.6 %collective-permute-start.4 = (f32[2,2,32,128]{3,2,1,0:T(8,128)S(1)}, f32[2,2,32,128]{3,2,1,0:T(8,128)S(1)}, u32[]{:S(2)}, u32[]{:S(2)}) collective-permute-start(f32[2,2,32,128]{3,2,1,0:T(8,128)S(1)} %get-tuple-element.52), channel_id=1, source_target_pairs={{0,2},{1,3},{2,0},{3,1},{4,6},{5,7},{6,4},{7,5},{8,10},{9,11},{10,... | collective-permute-start | bytes 196616 | tf_op jit(solution)/shard_map/ppermute | solution.py:323
  16.4 7.6 %collective-permute-start.5 = (f32[2,2,32,128]{3,2,1,0:T(8,128)S(1)}, f32[2,2,32,128]{3,2,1,0:T(8,128)S(1)}, u32[]{:S(2)}, u32[]{:S(2)}) collective-permute-start(f32[2,2,32,128]{3,2,1,0:T(8,128)S(1)} %get-tuple-element.53), channel_id=1, source_target_pairs={{0,4},{1,5},{2,6},{3,7},{4,0},{5,1},{6,2},{7,3},{8,12},{9,13},{10,... | collective-permute-start | bytes 196616 | tf_op jit(solution)/shard_map/ppermute | solution.py:323
  19.0 18.7 %all-to-all-start = ((f32[8,136,128]{2,1,0:T(8,128)}), f32[8,136,128]{2,1,0:T(8,128)S(1)}, u32[]{:S(2)}, u32[]{:S(2)}) async-start(f32[8,136,128]{2,1,0:T(8,128)} %bounds.1), calls=%async_computation | async-start | bytes 1114112 | tf_op jit(solution)/shard_map/all_to_all | solution.py:429
  24.1 6.4 %collective-permute-start.7 = (f32[8,2,32,128]{3,2,1,0:T(8,128)S(1)}, f32[8,2,32,128]{3,2,1,0:T(8,128)S(1)}, u32[]{:S(2)}, u32[]{:S(2)}) collective-permute-start(f32[8,2,32,128]{3,2,1,0:T(8,128)S(1)} %constant_dynamic-update-slice_fusion.mine), channel_id=1, source_target_pairs={{0,16},{1,17},{2,18},{3,19},{4,20},{5,21},{6,22},{7,23},{8,24},{9,... | collective-permute-start | bytes 786440 | tf_op jit(solution)/shard_map/ppermute | solution.py:323
  25.6 4.9 %collective-permute-start.8 = (f32[8,2,32,128]{3,2,1,0:T(8,128)S(1)}, f32[8,2,32,128]{3,2,1,0:T(8,128)S(1)}, u32[]{:S(2)}, u32[]{:S(2)}) collective-permute-start(f32[8,2,32,128]{3,2,1,0:T(8,128)S(1)} %constant_dynamic-update-slice_fusion.mine), channel_id=1, source_target_pairs={{0,8},{1,9},{2,10},{3,11},{4,12},{5,13},{6,14},{7,15},{8,0},{9,1},... | collective-permute-start | bytes 786440 | tf_op jit(solution)/shard_map/ppermute | solution.py:323
  30.5 1.5 %collective-permute-start.9 = (f32[8,2,32,128]{3,2,1,0:T(8,128)S(1)}, f32[8,2,32,128]{3,2,1,0:T(8,128)S(1)}, u32[]{:S(2)}, u32[]{:S(2)}) collective-permute-start(f32[8,2,32,128]{3,2,1,0:T(8,128)S(1)} %collective-permute-done.7.beside), channel_id=1, source_target_pairs={{0,8},{1,9},{2,10},{3,11},{4,12},{5,13},{6,14},{7,15},{8,0},{9,1},... | collective-permute-start | bytes 786440 | tf_op jit(solution)/shard_map/ppermute | solution.py:323
  41.3 4.0 %collective-permute-start.10 = (f32[16,16,128]{2,1,0:T(8,128)S(1)}, f32[16,16,128]{2,1,0:T(8,128)S(1)}, u32[]{:S(2)}, u32[]{:S(2)}) collective-permute-start(f32[16,16,128]{2,1,0:T(8,128)S(1)} %get-tuple-element.44.advanced), channel_id=1, source_target_pairs={{0,8},{1,9},{2,10},{3,11},{4,12},{5,13},{6,14},{7,15},{8,0},{9,1},... | collective-permute-start | bytes 393224 | tf_op jit(solution)/shard_map/ppermute | solution.py:323
  41.4 3.9 %collective-permute-start.11 = (f32[16,8,128]{2,1,0:T(8,128)S(1)}, f32[16,8,128]{2,1,0:T(8,128)S(1)}, u32[]{:S(2)}, u32[]{:S(2)}) collective-permute-start(f32[16,8,128]{2,1,0:T(8,128)S(1)} %get-tuple-element.45), channel_id=1, source_target_pairs={{0,9},{1,8},{2,11},{3,10},{4,13},{5,12},{6,15},{7,14},{8,1},{9,0},... | collective-permute-start | bytes 196616 | tf_op jit(solution)/shard_map/ppermute | solution.py:323
  42.9 2.3 %collective-permute-start.12 = (f32[16,8,128]{2,1,0:T(8,128)S(1)}, f32[16,8,128]{2,1,0:T(8,128)S(1)}, u32[]{:S(2)}, u32[]{:S(2)}) collective-permute-start(f32[16,8,128]{2,1,0:T(8,128)S(1)} %get-tuple-element.46), channel_id=1, source_target_pairs={{0,8},{1,10},{2,9},{3,12},{4,11},{5,14},{6,13},{7,15},{8,0},{9,2},... | collective-permute-start | bytes 196616 | tf_op jit(solution)/shard_map/ppermute | solution.py:323

commit v5 on v4

--- a/solution.py
+++ b/solution.py
@@ -13,6 +13,10 @@
 AXES = ("copy", "tm", "space")
 VMEM = pl.BlockSpec(memory_space=pltpu.VMEM)
 SMEM = pl.BlockSpec(memory_space=pltpu.SMEM)
+
+
+def slab_of(place, count):
+    return place ^ (place // 2 % 2) if count == 8 else place
 
 
 def windows(values, place, rows, width):
@@ -73,8 +77,8 @@
             jnp.where(lead, wind[1, layer], wind[2, layer]),
         )
         for place in range(half):
-            even = windows(field, 2 * place, rows, width)
-            odd = windows(field, 2 * place + 1, rows, width)
+            even = windows(field, slab_of(2 * place, 2 * half), rows, width)
+            odd = windows(field, slab_of(2 * place + 1, 2 * half), rows, width)
             same[place ^ (spot // 2), layer] = jnp.where(swap, odd, even)
             across[place ^ (spot // 2), layer] = jnp.where(swap, even, odd)
 
@@ -83,8 +87,8 @@
     layers = state.shape[0]
     for layer in range(layers):
         for spot in range(packed.shape[0]):
-            packed[spot, pl.ds(layer * width, width)] = windows(state[layer], spot, rows, width)
-            packed[spot, pl.ds((layers + layer) * width, width)] = windows(forcing[layer], spot, rows, width)
+            packed[spot, pl.ds(layer * width, width)] = windows(state[layer], slab_of(spot, packed.shape[0]), rows, width)
+            packed[spot, pl.ds((layers + layer) * width, width)] = windows(forcing[layer], slab_of(spot, packed.shape[0]), rows, width)
 
 
 def bound_kernel(rows, width, info, rates, mine, other, masked, wind, state, forcing, out):
@@ -233,8 +237,9 @@
         pairs = []
         for dim in range(3):
             conduct, speed = faces[2 * dim][place], faces[2 * dim + 1][place]
-            pairs.append(conduct + rate * jnp.maximum(speed, 0.0))
-            pairs.append(rate * jnp.minimum(speed, 0.0) - conduct)
+            speed = rate * speed
+            pairs.append(conduct + jnp.maximum(speed, 0.0))
+            pairs.append(jnp.minimum(speed, 0.0) - conduct)
         for number in range(6):
             ahead[number, place] = pairs[number]
         change, low_flow = difference(place, values, values_ahead, low_flow, pairs)
@@ -252,7 +257,7 @@
         return values_ahead, low_flow
 
     lax.fori_loop(0, total, first_sweep, (state[0], zero), unroll=8)
-    lax.fori_loop(0, total, second_sweep, (residual[0], zero), unroll=8)
+    lax.fori_loop(0, total, second_sweep, (residual[0], zero), unroll=16)
 
 
 def bounds_of(packed):
@@ -280,7 +285,7 @@
     advanced[...] = state[:total, LOW : LOW + rows]
     edge = min(rows, LOW)
     low, high = state[:total, LOW : LOW + edge], state[:total, LOW + rows - edge : LOW + rows]
-    even = info[1] % 2 == 0
+    even = info[5] % 2 == 0
     edge_one[...] = jnp.where(even, high, low)
     edge_two[...] = jnp.where(even, low, high)
 
@@ -311,6 +316,20 @@
     out[:, 1] = final.reshape(shape)
 
 
+def unpack_kernel(result, *refs):
+    outs, sems = refs[:2], refs[2]
+    count, rows = result.shape[0], result.shape[3]
+    copies = []
+    for number, out in enumerate(outs):
+        for spot in range(count):
+            target = out.at[0, :, pl.ds(slab_of(spot, count) * rows, rows)]
+            copies.append(pltpu.make_async_copy(result.at[spot, number], target, sems.at[number, spot]))
+    for copy in copies:
+        copy.start()
+    for copy in copies:
+        copy.wait()
+
+
 def swapped(array, sizes, partner, flip=0):
     copies, blocks, count = sizes
     pairs = []
@@ -327,13 +346,17 @@
     return lambda t, s: (t, ((s + 1) ^ 1) - 1) if 0 < s < count - 1 else (t ^ 1, s)
 
 
-def halos(edge_one, edge_two, advanced, sizes, rows, place):
+def halos(edge_one, edge_two, advanced, sizes, rows, slab):
     copies, blocks, count = sizes
-    even = place % 2 == 0
-    below, above = place > 0, place < count - 1
+    even = slab % 2 == 0
+    below, above = slab > 0, slab < count - 1
     if rows >= LOW and blocks == 2 and count % 2 == 0:
+        def partner(t, s):
+            own = slab_of(s, count)
+            return 1 - t, slab_of(((own + 1) ^ 1) - 1, count) if 0 < own < count - 1 else s
+
         one = swapped(edge_one, sizes, lambda t, s: (1 - t, s ^ 1))
-        two = swapped(edge_two, sizes, lambda t, s: (1 - t, ((s + 1) ^ 1) - 1 if 0 < s < count - 1 else s))
+        two = swapped(edge_two, sizes, partner)
         return one, two, even, below, above
 
     def shifted(values, by):
@@ -370,16 +393,17 @@
 
     half = block % 2
     lead = lax.axis_index("copy") % 2
-    flags = [half, place, place > 0, place < count - 1, lead]
+    slab = slab_of(place, count)
+    flags = [half, place, place > 0, place < count - 1, lead, slab]
     info = jnp.stack([jnp.asarray(flag).astype(jnp.int32) for flag in flags])
-    slab = struct(layers, depth, lanes)
+    field = struct(layers, depth, lanes)
     outer = struct(depth, lanes)
     hold = pltpu.VMEM((layers, depth, lanes), jnp.float32)
     anywhere = pl.BlockSpec(memory_space=pltpu.HBM)
     arrays = (initial, source, diffusion, wind_field, buildings, strength)
     masked, winds, state, forcing, edge_one, edge_two, rates = call(
         load_kernel,
-        [slab, struct(3, layers, depth, lanes), slab, slab, outer, outer, struct(8, lanes)],
+        [field, struct(3, layers, depth, lanes), field, field, outer, outer, struct(8, lanes)],
         [SMEM] + [anywhere] * 6,
         "load",
         info,
@@ -393,8 +417,6 @@
             pltpu.SemaphoreType.DMA((6,)),
         ],
     )
-    edge_one = swapped(edge_one, sizes, lambda t, s: (t, s ^ 1))
-    edge_two = swapped(edge_two, sizes, outer_partner(count))
     same, across = call(
         functools.partial(pack_shared, rows, width),
         [struct(count // 2, layers, width, lanes)] * 2,
@@ -405,6 +427,8 @@
         winds,
     )
     across = swapped(across, sizes, lambda t, s: (t, s ^ 1))
+    edge_one = swapped(edge_one, sizes, lambda t, s: (t, s ^ 1))
+    edge_two = swapped(edge_two, sizes, outer_partner(count))
     edges = jnp.stack([edge_one, edge_two])
     other_edges = swapped(edges, sizes, lambda t, s: (t ^ 1, s))
     (packed,) = call(
@@ -463,7 +487,7 @@
         own = swapped(advanced, sizes, lambda t, s: (1 - t, s))
     else:
         own = swapped(advanced, sizes, lambda t, s: (t + 1, s) if t + 1 < blocks else None)
-    one, two, swap, below, above = halos(edge_one, edge_two, advanced, sizes, rows, place)
+    one, two, swap, below, above = halos(edge_one, edge_two, advanced, sizes, rows, slab)
     flags = [block, place, swap, below, above]
     info = jnp.stack([jnp.asarray(flag).astype(jnp.int32) for flag in flags])
     result = pl.pallas_call(
@@ -476,8 +500,20 @@
         name="three_steps",
     )(info, rates, packed, own, one, two, advanced, third, *faces)
     result = lax.all_to_all(result, "space", 0, 0, tiled=True)
-    result = result.transpose(1, 2, 0, 3, 4).reshape(2, 1, layers, depth, lanes)
-    return result[0], result[1]
+    if rows % 8:
+        result = result.transpose(1, 2, 0, 3, 4).reshape(2, 1, layers, depth, lanes)
+        return result[0], result[1]
+    return tuple(
+        pl.pallas_call(
+            unpack_kernel,
+            out_shape=[struct(1, layers, depth, lanes)] * 2,
+            in_specs=[VMEM],
+            out_specs=[pl.BlockSpec(memory_space=pl.ANY)] * 2,
+            scratch_shapes=[pltpu.SemaphoreType.DMA((2, count))],
+            compiler_params=params,
+            name="unpack",
+        )(result)
+    )
 
 
 def solution(mesh):

time: 64.3 us -> 61.8 us (0.961)
  local copies, waits for them, and re-layouts: 1.54 us -> 0.2 us
  blocking collectives: 14.5 us -> 13.2 us
    slice x3 -> x0, local copies, waits for them, and re-layouts: 1.35 us -> none  [shards(): return (result[0], result[1])]
    all_to_all x1, blocking collectives: 14.5 us -> 13.2 us  [shards(): result = lax.all_to_all(result, 'space', 0, 0, tiled=True)]
    pallas_call x0 -> x1, Pallas kernels: none -> 0.83 us  [shards(): pl.pallas_call(unpack_kernel, out_shape=[struct(1, layers, depth, lanes)]...]
where the time goes in v5:
time: 61.8 us; the launch traced here: 61.5 us
  starting transfers between devices  19.3 us (31%)
  waiting for transfers between devices  15.9 us (26%)
  blocking collectives  13.2 us (21%)
  Pallas kernels  12.1 us (20%)
  between operations  0.8 us (1%)
    ppermute x13, starting transfers between devices, swapped(): return lax.ppermute(array, AXES, pairs)  14.3 us
    all_to_all x1, blocking collectives, shards(): result = lax.all_to_all(result, 'space', 0, 0, tiled=True)  13.2 us
    ppermute x13, waiting for transfers between devices, swapped(): return lax.ppermute(array, AXES, pairs)  11.4 us
    pallas_call x4, Pallas kernels, call(): pl.pallas_call(kernel, out_shape=outs, in_specs=in_specs, out_specs=[VMEM...  5.41 us
    all_to_all x1, starting transfers between devices, shards(): packed = lax.all_to_all(packed, 'space', 0, 0, tiled=True)  5.02 us
    all_to_all x1, waiting for transfers between devices, shards(): packed = lax.all_to_all(packed, 'space', 0, 0, tiled=True)  4.46 us
    pallas_call x1, Pallas kernels, shards(): pl.pallas_call(functools.partial(first_kernel, rows, width, layers), out_...  3.25 us
    pallas_call x1, Pallas kernels, shards(): pl.pallas_call(functools.partial(second_kernel, rows, width, layers), out...  2.6 us
  transfers between devices with their start and end apart: 14, of which 5 were waited for; matrix products, arithmetic and copies ran while one was open for 0% of the time, Pallas kernels for 6%

profile of v5, /device:TPU:0, one launch (start us, length us, event | category | flops | bytes accessed | tf_op | source)
XLA Modules:
  0.0 61.5 jit_solution(14021293179296870910)
XLA Ops:
  0.7 0.1 stack.86.info
  0.8 1.8 %load.1 = (f32[2,128,128]{2,1,0:T(8,128)S(1)}, f32[3,2,128,128]{3,2,1,0:T(8,128)S(1)}, f32[2,128,128]{2,1,0:T(8,128)S(1)}, f32[2,128,128]{2,1,0:T(8,128)S(1)}, f...) custom-call(s32[6]{0:T(128)S(1)} %stack.86.info, f32[1,2,128,128]{3,2,1,0:T(8,128)} %initial.1, ...), custom_call_target="tpu_custom_call" | custom-call | tf_op jit(solution)/shard_map/load/pallas_call | solution.py:385
  2.6 3.0 %collective-permute-start = (f32[128,128]{1,0:T(8,128)S(1)}, f32[128,128]{1,0:T(8,128)S(1)}, u32[]{:S(2)}, u32[]{:S(2)}) collective-permute-start(f32[128,128]{1,0:T(8,128)S(1)} %get-tuple-element.26), channel_id=1, source_target_pairs={{0,1},{1,0},{2,3},{3,2},{4,5},{5,4},{6,7},{7,6},{8,9},{9,8},{10,11... | collective-permute-start | bytes 196616 | tf_op jit(solution)/shard_map/ppermute | solution.py:342
  5.6 0.0 collective-permute-start.1
  5.6 0.6 pack_shared.1
  6.2 3.1 %collective-permute-start.3 = (f32[4,2,32,128]{3,2,1,0:T(8,128)S(1)}, f32[4,2,32,128]{3,2,1,0:T(8,128)S(1)}, u32[]{:S(2)}, u32[]{:S(2)}) collective-permute-start(f32[4,2,32,128]{3,2,1,0:T(8,128)S(1)} %get-tuple-element.33), channel_id=1, source_target_pairs={{0,1},{1,0},{2,3},{3,2},{4,5},{5,4},{6,7},{7,6},{8,9},{9,8},{10,11... | collective-permute-start | bytes 393224 | tf_op jit(solution)/shard_map/ppermute | solution.py:342
  9.3 0.0 collective-permute-done
  9.3 0.0 collective-permute-done.1
  9.3 0.1 collective-permute-start.2
  9.4 2.8 %collective-permute-done.3 = f32[4,2,32,128]{3,2,1,0:T(8,128)S(1)} collective-permute-done((f32[4,2,32,128]{3,2,1,0:T(8,128)S(1)}, f32[4,2,32,128]{3,2,1,0:T(8,128)S(1)}, u32[]{:S(2)}, u32[]{:S(2)}) %collective-permute-start.3) | collective-permute-done | bytes 131104 | tf_op jit(solution)/shard_map/ppermute | solution.py:342
  12.3 4.2 %collective-permute-start.6 = (f32[2,2,32,128]{3,2,1,0:T(8,128)S(1)}, f32[2,2,32,128]{3,2,1,0:T(8,128)S(1)}, u32[]{:S(2)}, u32[]{:S(2)}) collective-permute-start(f32[2,2,32,128]{3,2,1,0:T(8,128)S(1)} %get-tuple-element.48), channel_id=1, source_target_pairs={{0,6},{1,7},{2,4},{3,5},{4,2},{5,3},{6,0},{7,1},{8,14},{9,15},{10,... | collective-permute-start | bytes 196616 | tf_op jit(solution)/shard_map/ppermute | solution.py:342
  16.4 0.0 collective-permute-start.4
  16.4 0.6 %collective-permute-start.5 = (f32[2,2,32,128]{3,2,1,0:T(8,128)S(1)}, f32[2,2,32,128]{3,2,1,0:T(8,128)S(1)}, u32[]{:S(2)}, u32[]{:S(2)}) collective-permute-start(f32[2,2,32,128]{3,2,1,0:T(8,128)S(1)} %get-tuple-element.51), channel_id=1, source_target_pairs={{0,4},{1,5},{2,6},{3,7},{4,0},{5,1},{6,2},{7,3},{8,12},{9,13},{10,... | collective-permute-start | bytes 196616 | tf_op jit(solution)/shard_map/ppermute | solution.py:342
  17.1 0.0 collective-permute-done.2.other
  17.1 1.9 %bounds.1 = f32[8,136,128]{2,1,0:T(8,128)} custom-call(s32[6]{0:T(128)S(1)} %stack.86.info, f32[8,128]{1,0:T(8,128)S(1)} %get-tuple-element.25.rates, f32[2,128,128]{2,1,0:T(8,128)S(1)} %pad_maximum_fusion.mine, f32[2,128,128]{2,1,0:T(8,128)S(1)} %collective-permute-done.2.other, f32[2,128,128]{2,1,0:T(8,128)S(1)} %get-tuple-element.28.masked, ...), custom_call_target="tpu_custom_call" | custom-call | tf_op jit(solution)/shard_map/bounds/pallas_call | solution.py:385
  19.0 5.0 %all-to-all-start = ((f32[8,136,128]{2,1,0:T(8,128)}), f32[8,136,128]{2,1,0:T(8,128)S(1)}, u32[]{:S(2)}, u32[]{:S(2)}) async-start(f32[8,136,128]{2,1,0:T(8,128)} %bounds.1), calls=%async_computation | async-start | bytes 1114112 | tf_op jit(solution)/shard_map/all_to_all | solution.py:453
  24.0 0.0 collective-permute-done.6
  24.0 0.0 collective-permute-done.4
  24.0 0.0 collective-permute-done.5
  24.1 1.6 %collective-permute-start.7 = (f32[8,2,32,128]{3,2,1,0:T(8,128)S(1)}, f32[8,2,32,128]{3,2,1,0:T(8,128)S(1)}, u32[]{:S(2)}, u32[]{:S(2)}) collective-permute-start(f32[8,2,32,128]{3,2,1,0:T(8,128)S(1)} %constant_dynamic-update-slice_fusion.mine), channel_id=1, source_target_pairs={{0,16},{1,17},{2,18},{3,19},{4,20},{5,21},{6,22},{7,23},{8,24},{9,... | collective-permute-start | bytes 786440 | tf_op jit(solution)/shard_map/ppermute | solution.py:342
  25.7 0.0 collective-permute-start.8
  25.7 4.9 %collective-permute-done.7.beside = f32[8,2,32,128]{3,2,1,0:T(8,128)S(1)} collective-permute-done((f32[8,2,32,128]{3,2,1,0:T(8,128)S(1)}, f32[8,2,32,128]{3,2,1,0:T(8,128)S(1)}, u32[]{:S(2)}, u32[]{:S(2)}) %collective-permute-start.7) | collective-permute-done | bytes 262176 | tf_op jit(solution)/shard_map/ppermute | solution.py:342
  30.5 0.0 collective-permute-start.9
  30.5 0.0 collective-permute-done.8.other
  30.5 1.5 %collective-permute-done.9.other_beside = f32[8,2,32,128]{3,2,1,0:T(8,128)S(1)} collective-permute-done((f32[8,2,32,128]{3,2,1,0:T(8,128)S(1)}, f32[8,2,32,128]{3,2,1,0:T(8,128)S(1)}, u32[]{:S(2)}, u32[]{:S(2)}) %collective-permute-start.9) | collective-permute-done | bytes 262176 | tf_op jit(solution)/shard_map/ppermute | solution.py:342
  32.1 1.1 %faces.1 = (f32[16,32,128]{2,1,0:T(8,128)S(1)}, f32[16,32,128]{2,1,0:T(8,128)S(1)}, f32[16,32,128]{2,1,0:T(8,128)S(1)}, f32[16,32,128]{2,1,0:T(8,128)S(1)}, f32[...) custom-call(s32[6]{0:T(128)S(1)} %stack.86.info, f32[8,2,32,128]{3,2,1,0:T(8,128)S(1)} %constant_dynamic-update-slice_fusion.mine, ...), custom_call_target="tpu_custom_call" | custom-call | tf_op jit(solution)/shard_map/faces/pallas_call | solution.py:385
  33.2 4.5 %all-to-all-done.packed = f32[8,136,128]{2,1,0:T(8,128)S(1)} async-done(((f32[8,136,128]{2,1,0:T(8,128)}), f32[8,136,128]{2,1,0:T(8,128)S(1)}, u32[]{:S(2)}, u32[]{:S(2)}) %all-to-all-start) | async-done | bytes 557088 | tf_op jit(solution)/shard_map/all_to_all | solution.py:453
  37.6 3.3 %four_steps.1 = (f32[16,16,128]{2,1,0:T(8,128)S(1)}, f32[16,16,128]{2,1,0:T(8,128)S(1)}, f32[16,8,128]{2,1,0:T(8,128)S(1)}, f32[16,8,128]{2,1,0:T(8,128)S(1)}) custom-call(s32[6]{0:T(128)S(1)} %stack.86.info, f32[8,128]{1,0:T(8,128)S(1)} %get-tuple-element.25.rates, f32[8,136,128]{2,1,0:T(8,128)S(1)} %all-to-all-done.packed, ...), custom_call_target="tpu_custom_call" | custom-call | tf_op jit(solution)/shard_map/four_steps/pallas_call | solution.py:476
  40.9 0.1 collective-permute-start.10
  41.0 1.6 %collective-permute-start.11 = (f32[16,8,128]{2,1,0:T(8,128)S(1)}, f32[16,8,128]{2,1,0:T(8,128)S(1)}, u32[]{:S(2)}, u32[]{:S(2)}) collective-permute-start(f32[16,8,128]{2,1,0:T(8,128)S(1)} %get-tuple-element.45), channel_id=1, source_target_pairs={{0,9},{1,8},{2,11},{3,10},{4,13},{5,12},{6,15},{7,14},{8,1},{9,0},... | collective-permute-start | bytes 196616 | tf_op jit(solution)/shard_map/ppermute | solution.py:342
  42.6 0.1 collective-permute-start.12
  42.6 0.1 stack.78.info
  42.7 2.2 %collective-permute-done.11.halo_one = f32[16,8,128]{2,1,0:T(8,128)S(1)} collective-permute-done((f32[16,8,128]{2,1,0:T(8,128)S(1)}, f32[16,8,128]{2,1,0:T(8,128)S(1)}, u32[]{:S(2)}, u32[]{:S(2)}) %collective-permute-start.11) | collective-permute-done | bytes 65568 | tf_op jit(solution)/shard_map/ppermute | solution.py:342
  44.9 0.0 collective-permute-done.12.halo_two
  44.9 0.0 collective-permute-done.10.passed
  44.9 2.6 %three_steps.1 = f32[8,2,2,16,128]{4,3,2,1,0:T(8,128)S(1)} custom-call(s32[5]{0:T(128)S(1)} %stack.78.info, f32[8,128]{1,0:T(8,128)S(1)} %get-tuple-element.25.rates, f32[8,136,128]{2,1,0:T(8,128)S(1)} %all-to-all-done.packed, f32[16,16,128]{2,1,0:T(8,128)S(1)} %collective-permute-done.10.passed, f32[16,8,128]{2,1,0:T(8,128)S(1)} %collective-permute-done.11.halo_one, ...), custom_call_target="tpu_custom_call" | custom-call | tf_op jit(solution)/shard_map/three_steps/pallas_call | solution.py:493
  47.5 13.2 %all_to_all.10.result = f32[8,2,2,16,128]{4,3,2,1,0:T(8,128)S(1)} all-to-all(f32[8,2,2,16,128]{4,3,2,1,0:T(8,128)S(1)} %three_steps.1), channel_id=1, replica_groups=mesh['copy'=2,'tm'=2,'space'=8] {'space'}, dimensions={0} | all-to-all | bytes 524288 | tf_op jit(solution)/shard_map/all_to_all | solution.py:502
  60.7 0.8 %unpack.1 = (f32[1,2,128,128]{3,2,1,0:T(8,128)}, f32[1,2,128,128]{3,2,1,0:T(8,128)}) custom-call(f32[8,2,2,16,128]{4,3,2,1,0:T(8,128)S(1)} %all_to_all.10.result), custom_call_target="tpu_custom_call" | custom-call | tf_op jit(solution)/shard_map/unpack/pallas_call | solution.py:507
  (6 shorter events, 0.1 us)
Async XLA Ops:
  2.6 6.7 %collective-permute-start = (f32[128,128]{1,0:T(8,128)S(1)}, f32[128,128]{1,0:T(8,128)S(1)}, u32[]{:S(2)}, u32[]{:S(2)}) collective-permute-start(f32[128,128]{1,0:T(8,128)S(1)} %get-tuple-element.26), channel_id=1, source_target_pairs={{0,1},{1,0},{2,3},{3,2},{4,5},{5,4},{6,7},{7,6},{8,9},{9,8},{10,11... | collective-permute-start | bytes 196616 | tf_op jit(solution)/shard_map/ppermute | solution.py:342
  5.6 3.7 %collective-permute-start.1 = (f32[128,128]{1,0:T(8,128)S(1)}, f32[128,128]{1,0:T(8,128)S(1)}, u32[]{:S(2)}, u32[]{:S(2)}) collective-permute-start(f32[128,128]{1,0:T(8,128)S(1)} %get-tuple-element.27), channel_id=1, source_target_pairs={{0,8},{1,2},{2,1},{3,4},{4,3},{5,6},{6,5},{7,15},{8,0},{9,10},{10,... | collective-permute-start | bytes 196616 | tf_op jit(solution)/shard_map/ppermute | solution.py:342
  6.2 6.0 %collective-permute-start.3 = (f32[4,2,32,128]{3,2,1,0:T(8,128)S(1)}, f32[4,2,32,128]{3,2,1,0:T(8,128)S(1)}, u32[]{:S(2)}, u32[]{:S(2)}) collective-permute-start(f32[4,2,32,128]{3,2,1,0:T(8,128)S(1)} %get-tuple-element.33), channel_id=1, source_target_pairs={{0,1},{1,0},{2,3},{3,2},{4,5},{5,4},{6,7},{7,6},{8,9},{9,8},{10,11... | collective-permute-start | bytes 393224 | tf_op jit(solution)/shard_map/ppermute | solution.py:342
  9.3 7.7 %collective-permute-start.2 = (f32[2,128,128]{2,1,0:T(8,128)S(1)}, f32[2,128,128]{2,1,0:T(8,128)S(1)}, u32[]{:S(2)}, u32[]{:S(2)}) collective-permute-start(f32[2,128,128]{2,1,0:T(8,128)S(1)} %pad_maximum_fusion.mine), channel_id=1, source_target_pairs={{0,8},{1,9},{2,10},{3,11},{4,12},{5,13},{6,14},{7,15},{8,0},{9,1},... | collective-permute-start | bytes 393224 | tf_op jit(solution)/shard_map/ppermute | solution.py:342
  12.3 11.8 %collective-permute-start.6 = (f32[2,2,32,128]{3,2,1,0:T(8,128)S(1)}, f32[2,2,32,128]{3,2,1,0:T(8,128)S(1)}, u32[]{:S(2)}, u32[]{:S(2)}) collective-permute-start(f32[2,2,32,128]{3,2,1,0:T(8,128)S(1)} %get-tuple-element.48), channel_id=1, source_target_pairs={{0,6},{1,7},{2,4},{3,5},{4,2},{5,3},{6,0},{7,1},{8,14},{9,15},{10,... | collective-permute-start | bytes 196616 | tf_op jit(solution)/shard_map/ppermute | solution.py:342
  16.4 7.6 %collective-permute-start.4 = (f32[2,2,32,128]{3,2,1,0:T(8,128)S(1)}, f32[2,2,32,128]{3,2,1,0:T(8,128)S(1)}, u32[]{:S(2)}, u32[]{:S(2)}) collective-permute-start(f32[2,2,32,128]{3,2,1,0:T(8,128)S(1)} %get-tuple-element.50), channel_id=1, source_target_pairs={{0,2},{1,3},{2,0},{3,1},{4,6},{5,7},{6,4},{7,5},{8,10},{9,11},{10,... | collective-permute-start | bytes 196616 | tf_op jit(solution)/shard_map/ppermute | solution.py:342
  16.4 7.6 %collective-permute-start.5 = (f32[2,2,32,128]{3,2,1,0:T(8,128)S(1)}, f32[2,2,32,128]{3,2,1,0:T(8,128)S(1)}, u32[]{:S(2)}, u32[]{:S(2)}) collective-permute-start(f32[2,2,32,128]{3,2,1,0:T(8,128)S(1)} %get-tuple-element.51), channel_id=1, source_target_pairs={{0,4},{1,5},{2,6},{3,7},{4,0},{5,1},{6,2},{7,3},{8,12},{9,13},{10,... | collective-permute-start | bytes 196616 | tf_op jit(solution)/shard_map/ppermute | solution.py:342
  19.0 18.7 %all-to-all-start = ((f32[8,136,128]{2,1,0:T(8,128)}), f32[8,136,128]{2,1,0:T(8,128)S(1)}, u32[]{:S(2)}, u32[]{:S(2)}) async-start(f32[8,136,128]{2,1,0:T(8,128)} %bounds.1), calls=%async_computation | async-start | bytes 1114112 | tf_op jit(solution)/shard_map/all_to_all | solution.py:453
  24.1 6.4 %collective-permute-start.7 = (f32[8,2,32,128]{3,2,1,0:T(8,128)S(1)}, f32[8,2,32,128]{3,2,1,0:T(8,128)S(1)}, u32[]{:S(2)}, u32[]{:S(2)}) collective-permute-start(f32[8,2,32,128]{3,2,1,0:T(8,128)S(1)} %constant_dynamic-update-slice_fusion.mine), channel_id=1, source_target_pairs={{0,16},{1,17},{2,18},{3,19},{4,20},{5,21},{6,22},{7,23},{8,24},{9,... | collective-permute-start | bytes 786440 | tf_op jit(solution)/shard_map/ppermute | solution.py:342
  25.7 4.9 %collective-permute-start.8 = (f32[8,2,32,128]{3,2,1,0:T(8,128)S(1)}, f32[8,2,32,128]{3,2,1,0:T(8,128)S(1)}, u32[]{:S(2)}, u32[]{:S(2)}) collective-permute-start(f32[8,2,32,128]{3,2,1,0:T(8,128)S(1)} %constant_dynamic-update-slice_fusion.mine), channel_id=1, source_target_pairs={{0,8},{1,9},{2,10},{3,11},{4,12},{5,13},{6,14},{7,15},{8,0},{9,1},... | collective-permute-start | bytes 786440 | tf_op jit(solution)/shard_map/ppermute | solution.py:342
  30.5 1.5 %collective-permute-start.9 = (f32[8,2,32,128]{3,2,1,0:T(8,128)S(1)}, f32[8,2,32,128]{3,2,1,0:T(8,128)S(1)}, u32[]{:S(2)}, u32[]{:S(2)}) collective-permute-start(f32[8,2,32,128]{3,2,1,0:T(8,128)S(1)} %collective-permute-done.7.beside), channel_id=1, source_target_pairs={{0,8},{1,9},{2,10},{3,11},{4,12},{5,13},{6,14},{7,15},{8,0},{9,1},... | collective-permute-start | bytes 786440 | tf_op jit(solution)/shard_map/ppermute | solution.py:342
  40.9 4.0 %collective-permute-start.10 = (f32[16,16,128]{2,1,0:T(8,128)S(1)}, f32[16,16,128]{2,1,0:T(8,128)S(1)}, u32[]{:S(2)}, u32[]{:S(2)}) collective-permute-start(f32[16,16,128]{2,1,0:T(8,128)S(1)} %get-tuple-element.44.advanced), channel_id=1, source_target_pairs={{0,8},{1,9},{2,10},{3,11},{4,12},{5,13},{6,14},{7,15},{8,0},{9,1},... | collective-permute-start | bytes 393224 | tf_op jit(solution)/shard_map/ppermute | solution.py:342
  41.0 3.9 %collective-permute-start.11 = (f32[16,8,128]{2,1,0:T(8,128)S(1)}, f32[16,8,128]{2,1,0:T(8,128)S(1)}, u32[]{:S(2)}, u32[]{:S(2)}) collective-permute-start(f32[16,8,128]{2,1,0:T(8,128)S(1)} %get-tuple-element.45), channel_id=1, source_target_pairs={{0,9},{1,8},{2,11},{3,10},{4,13},{5,12},{6,15},{7,14},{8,1},{9,0},... | collective-permute-start | bytes 196616 | tf_op jit(solution)/shard_map/ppermute | solution.py:342
  42.6 2.3 %collective-permute-start.12 = (f32[16,8,128]{2,1,0:T(8,128)S(1)}, f32[16,8,128]{2,1,0:T(8,128)S(1)}, u32[]{:S(2)}, u32[]{:S(2)}) collective-permute-start(f32[16,8,128]{2,1,0:T(8,128)S(1)} %get-tuple-element.46), channel_id=1, source_target_pairs={{0,8},{1,11},{2,12},{3,9},{4,10},{5,15},{6,14},{7,13},{8,0},{9,3},... | collective-permute-start | bytes 196616 | tf_op jit(solution)/shard_map/ppermute | solution.py:342

commit v6 on v5

--- a/solution.py
+++ b/solution.py
@@ -220,7 +220,7 @@
     return alpha - beta, beta
 
 
-def one_step(total, width, layers, state, residual, ahead, faces, packed, rate, near, far):
+def one_step(total, width, layers, state, result, residual, ahead, faces, packed, rate, near, far, rows=0, store=None):
     lanes = state.shape[-1]
     zero = jnp.zeros((width, lanes), jnp.float32)
 
@@ -253,11 +253,28 @@
         values_ahead = residual[place + 1]
         pairs = [ahead[number, place] for number in range(6)]
         change, low_flow = difference(place, values, values_ahead, low_flow, pairs)
-        state[place] = state[place] + (near * values - far * change)
+        result[place] = state[place] + (near * values - far * change)
         return values_ahead, low_flow
 
     lax.fori_loop(0, total, first_sweep, (state[0], zero), unroll=8)
-    lax.fori_loop(0, total, second_sweep, (residual[0], zero), unroll=16)
+    inner, below, above = pl.ds(LOW, rows), pl.ds(LOW - 1, rows), pl.ds(LOW + 1, rows)
+
+    def inner_sweep(place, carry):
+        values, low_flow = carry
+        values_ahead = residual[place + 1, inner]
+        pairs = [ahead[number, place, inner] for number in range(6)]
+        flow_x = pairs[0] * values + pairs[1] * values_ahead
+        flow_y = pairs[2] * values + pairs[3] * residual[place, above]
+        under_y = ahead[2, place, below] * residual[place, below] + ahead[3, place, below] * values
+        flow_z = pairs[4] * values + pairs[5] * roll_back(values, 1)
+        change = (flow_x - low_flow) + (flow_y - under_y) + (flow_z - pltpu.roll(flow_z, 1, 1))
+        store(place, state[place, inner] + (near * values - far * change))
+        return values_ahead, flow_x
+
+    if store is None:
+        lax.fori_loop(0, total, second_sweep, (residual[0], zero), unroll=16)
+    else:
+        lax.fori_loop(0, total, inner_sweep, (residual[0, inner], zero[:rows]), unroll=16)
 
 
 def bounds_of(packed):
@@ -269,32 +286,47 @@
 
 
 def first_kernel(rows, width, layers, info, rates, packed, *refs):
-    faces, (advanced, third, edge_one, edge_two), (state, residual, ahead) = refs[:6], refs[6:10], refs[10:]
+    def store(place, values):
+        advanced[place] = values
+
+    faces, (advanced, third, edge_one, edge_two), (state, spare, residual, ahead) = refs[:6], refs[6:10], refs[10:]
     total = state.shape[0] - 1
     zero = jnp.zeros(state.shape[1:], jnp.float32)
     state[total] = zero
+    spare[total] = zero
     residual[total] = zero
     for place in range(total):
         state[place] = packed[place // layers, pl.ds(place % layers * width, width)]
     bounds = bounds_of(packed)
     for k in range(FINE):
         near, far = coefficients(bounds[k : k + 1])
-        one_step(total, width, layers, state, residual, ahead, faces, packed, rates[pl.ds(k, 1)], near, far)
+        states = (state, spare) if k % 2 == 0 else (spare, state)
+        step = (*states, residual, ahead, faces, packed, rates[pl.ds(k, 1)], near, far)
+        if k < FINE - 1:
+            one_step(total, width, layers, *step)
+        else:
+            one_step(total, width, layers, *step, rows, store)
         if k == FINE - 2:
-            third[...] = state[:total, LOW : LOW + rows]
-    advanced[...] = state[:total, LOW : LOW + rows]
+            third[...] = states[1][:total, LOW : LOW + rows]
     edge = min(rows, LOW)
-    low, high = state[:total, LOW : LOW + edge], state[:total, LOW + rows - edge : LOW + rows]
+    low, high = advanced[:, :edge], advanced[:, rows - edge :]
     even = info[5] % 2 == 0
     edge_one[...] = jnp.where(even, high, low)
     edge_two[...] = jnp.where(even, low, high)
 
 
 def second_kernel(rows, width, layers, info, rates, packed, passed, halo_one, halo_two, advanced, third, *refs):
-    faces, out, (state, residual, ahead) = refs[:6], refs[6], refs[7:]
+    first = info[0] == 0
+
+    def store(place, values):
+        out[place // layers, 0, place % layers] = advanced[place]
+        out[place // layers, 1, place % layers] = jnp.where(first, third[place], values)
+
+    faces, out, (state, spare, residual, ahead) = refs[:6], refs[6], refs[7:]
     total = state.shape[0] - 1
     zero = jnp.zeros(state.shape[1:], jnp.float32)
     state[total] = zero
+    spare[total] = zero
     residual[total] = zero
     swap = info[2] == 1
     below, above = halo_one[...], halo_two[...]
@@ -308,12 +340,12 @@
     bounds = bounds_of(packed)
     for k in range(FINE - 1):
         near, far = coefficients(bounds[k : k + 1])
-        one_step(total, width, layers, state, residual, ahead, faces, packed, rates[pl.ds(k, 1)], near, far)
-    first = info[0] == 0
-    final = jnp.where(first, third[...], state[:total, LOW : LOW + rows])
-    shape = out.shape[0:1] + out.shape[2:]
-    out[:, 0] = advanced[...].reshape(shape)
-    out[:, 1] = final.reshape(shape)
+        states = (state, spare) if k % 2 == 0 else (spare, state)
+        step = (*states, residual, ahead, faces, packed, rates[pl.ds(k, 1)], near, far)
+        if k < FINE - 2:
+            one_step(total, width, layers, *step)
+        else:
+            one_step(total, width, layers, *step, rows, store)
 
 
 def unpack_kernel(result, *refs):
@@ -469,6 +501,7 @@
 
     edge = min(rows, LOW)
     scratch = [
+        pltpu.VMEM((total + 1, width, lanes), jnp.float32),
         pltpu.VMEM((total + 1, width, lanes), jnp.float32),
         pltpu.VMEM((total + 1, width, lanes), jnp.float32),
         pltpu.VMEM((6, total, width, lanes), jnp.float32),

time: 61.8 us -> 61.7 us (level)
  no operation moved by 1% of the time
where the time goes in v6:
time: 61.7 us; the launch traced here: 61.4 us
  starting transfers between devices  19.3 us (31%)
  waiting for transfers between devices  15.9 us (26%)
  blocking collectives  13.2 us (21%)
  Pallas kernels  11.9 us (19%)
  between operations  0.8 us (1%)
    ppermute x13, starting transfers between devices, swapped(): return lax.ppermute(array, AXES, pairs)  14.3 us
    all_to_all x1, blocking collectives, shards(): result = lax.all_to_all(result, 'space', 0, 0, tiled=True)  13.2 us
    ppermute x13, waiting for transfers between devices, swapped(): return lax.ppermute(array, AXES, pairs)  11.4 us
    pallas_call x4, Pallas kernels, call(): pl.pallas_call(kernel, out_shape=outs, in_specs=in_specs, out_specs=[VMEM...  5.41 us
    all_to_all x1, starting transfers between devices, shards(): packed = lax.all_to_all(packed, 'space', 0, 0, tiled=True)  5.02 us
    all_to_all x1, waiting for transfers between devices, shards(): packed = lax.all_to_all(packed, 'space', 0, 0, tiled=True)  4.46 us
    pallas_call x1, Pallas kernels, shards(): pl.pallas_call(functools.partial(first_kernel, rows, width, layers), out_...  3.18 us
    pallas_call x1, Pallas kernels, shards(): pl.pallas_call(functools.partial(second_kernel, rows, width, layers), out...  2.53 us
  transfers between devices with their start and end apart: 14, of which 5 were waited for; matrix products, arithmetic and copies ran while one was open for 0% of the time, Pallas kernels for 6%

profile of v6, /device:TPU:0, one launch (start us, length us, event | category | flops | bytes accessed | tf_op | source)
XLA Modules:
  0.0 61.4 jit_solution(6226828530877470499)
XLA Ops:
  0.7 0.1 stack.86.info
  0.8 1.8 %load.1 = (f32[2,128,128]{2,1,0:T(8,128)S(1)}, f32[3,2,128,128]{3,2,1,0:T(8,128)S(1)}, f32[2,128,128]{2,1,0:T(8,128)S(1)}, f32[2,128,128]{2,1,0:T(8,128)S(1)}, f...) custom-call(s32[6]{0:T(128)S(1)} %stack.86.info, f32[1,2,128,128]{3,2,1,0:T(8,128)} %initial.1, ...), custom_call_target="tpu_custom_call" | custom-call | tf_op jit(solution)/shard_map/load/pallas_call | solution.py:417
  2.6 3.0 %collective-permute-start = (f32[128,128]{1,0:T(8,128)S(1)}, f32[128,128]{1,0:T(8,128)S(1)}, u32[]{:S(2)}, u32[]{:S(2)}) collective-permute-start(f32[128,128]{1,0:T(8,128)S(1)} %get-tuple-element.26), channel_id=1, source_target_pairs={{0,1},{1,0},{2,3},{3,2},{4,5},{5,4},{6,7},{7,6},{8,9},{9,8},{10,11... | collective-permute-start | bytes 196616 | tf_op jit(solution)/shard_map/ppermute | solution.py:374
  5.6 0.0 collective-permute-start.1
  5.6 0.6 pack_shared.1
  6.2 3.1 %collective-permute-start.3 = (f32[4,2,32,128]{3,2,1,0:T(8,128)S(1)}, f32[4,2,32,128]{3,2,1,0:T(8,128)S(1)}, u32[]{:S(2)}, u32[]{:S(2)}) collective-permute-start(f32[4,2,32,128]{3,2,1,0:T(8,128)S(1)} %get-tuple-element.33), channel_id=1, source_target_pairs={{0,1},{1,0},{2,3},{3,2},{4,5},{5,4},{6,7},{7,6},{8,9},{9,8},{10,11... | collective-permute-start | bytes 393224 | tf_op jit(solution)/shard_map/ppermute | solution.py:374
  9.3 0.0 collective-permute-done
  9.3 0.0 collective-permute-done.1
  9.3 0.1 collective-permute-start.2
  9.4 2.8 %collective-permute-done.3 = f32[4,2,32,128]{3,2,1,0:T(8,128)S(1)} collective-permute-done((f32[4,2,32,128]{3,2,1,0:T(8,128)S(1)}, f32[4,2,32,128]{3,2,1,0:T(8,128)S(1)}, u32[]{:S(2)}, u32[]{:S(2)}) %collective-permute-start.3) | collective-permute-done | bytes 131104 | tf_op jit(solution)/shard_map/ppermute | solution.py:374
  12.3 4.2 %collective-permute-start.6 = (f32[2,2,32,128]{3,2,1,0:T(8,128)S(1)}, f32[2,2,32,128]{3,2,1,0:T(8,128)S(1)}, u32[]{:S(2)}, u32[]{:S(2)}) collective-permute-start(f32[2,2,32,128]{3,2,1,0:T(8,128)S(1)} %get-tuple-element.48), channel_id=1, source_target_pairs={{0,6},{1,7},{2,4},{3,5},{4,2},{5,3},{6,0},{7,1},{8,14},{9,15},{10,... | collective-permute-start | bytes 196616 | tf_op jit(solution)/shard_map/ppermute | solution.py:374
  16.4 0.0 collective-permute-start.4
  16.4 0.6 %collective-permute-start.5 = (f32[2,2,32,128]{3,2,1,0:T(8,128)S(1)}, f32[2,2,32,128]{3,2,1,0:T(8,128)S(1)}, u32[]{:S(2)}, u32[]{:S(2)}) collective-permute-start(f32[2,2,32,128]{3,2,1,0:T(8,128)S(1)} %get-tuple-element.51), channel_id=1, source_target_pairs={{0,4},{1,5},{2,6},{3,7},{4,0},{5,1},{6,2},{7,3},{8,12},{9,13},{10,... | collective-permute-start | bytes 196616 | tf_op jit(solution)/shard_map/ppermute | solution.py:374
  17.1 0.0 collective-permute-done.2.other
  17.1 1.9 %bounds.1 = f32[8,136,128]{2,1,0:T(8,128)} custom-call(s32[6]{0:T(128)S(1)} %stack.86.info, f32[8,128]{1,0:T(8,128)S(1)} %get-tuple-element.25.rates, f32[2,128,128]{2,1,0:T(8,128)S(1)} %pad_maximum_fusion.mine, f32[2,128,128]{2,1,0:T(8,128)S(1)} %collective-permute-done.2.other, f32[2,128,128]{2,1,0:T(8,128)S(1)} %get-tuple-element.28.masked, ...), custom_call_target="tpu_custom_call" | custom-call | tf_op jit(solution)/shard_map/bounds/pallas_call | solution.py:417
  19.0 5.0 %all-to-all-start = ((f32[8,136,128]{2,1,0:T(8,128)}), f32[8,136,128]{2,1,0:T(8,128)S(1)}, u32[]{:S(2)}, u32[]{:S(2)}) async-start(f32[8,136,128]{2,1,0:T(8,128)} %bounds.1), calls=%async_computation | async-start | bytes 1114112 | tf_op jit(solution)/shard_map/all_to_all | solution.py:485
  24.0 0.0 collective-permute-done.6
  24.0 0.0 collective-permute-done.4
  24.0 0.0 collective-permute-done.5
  24.1 1.6 %collective-permute-start.7 = (f32[8,2,32,128]{3,2,1,0:T(8,128)S(1)}, f32[8,2,32,128]{3,2,1,0:T(8,128)S(1)}, u32[]{:S(2)}, u32[]{:S(2)}) collective-permute-start(f32[8,2,32,128]{3,2,1,0:T(8,128)S(1)} %constant_dynamic-update-slice_fusion.mine), channel_id=1, source_target_pairs={{0,16},{1,17},{2,18},{3,19},{4,20},{5,21},{6,22},{7,23},{8,24},{9,... | collective-permute-start | bytes 786440 | tf_op jit(solution)/shard_map/ppermute | solution.py:374
  25.7 0.0 collective-permute-start.8
  25.7 4.9 %collective-permute-done.7.beside = f32[8,2,32,128]{3,2,1,0:T(8,128)S(1)} collective-permute-done((f32[8,2,32,128]{3,2,1,0:T(8,128)S(1)}, f32[8,2,32,128]{3,2,1,0:T(8,128)S(1)}, u32[]{:S(2)}, u32[]{:S(2)}) %collective-permute-start.7) | collective-permute-done | bytes 262176 | tf_op jit(solution)/shard_map/ppermute | solution.py:374
  30.5 0.0 collective-permute-start.9
  30.5 0.0 collective-permute-done.8.other
  30.5 1.5 %collective-permute-done.9.other_beside = f32[8,2,32,128]{3,2,1,0:T(8,128)S(1)} collective-permute-done((f32[8,2,32,128]{3,2,1,0:T(8,128)S(1)}, f32[8,2,32,128]{3,2,1,0:T(8,128)S(1)}, u32[]{:S(2)}, u32[]{:S(2)}) %collective-permute-start.9) | collective-permute-done | bytes 262176 | tf_op jit(solution)/shard_map/ppermute | solution.py:374
  32.1 1.1 %faces.1 = (f32[16,32,128]{2,1,0:T(8,128)S(1)}, f32[16,32,128]{2,1,0:T(8,128)S(1)}, f32[16,32,128]{2,1,0:T(8,128)S(1)}, f32[16,32,128]{2,1,0:T(8,128)S(1)}, f32[...) custom-call(s32[6]{0:T(128)S(1)} %stack.86.info, f32[8,2,32,128]{3,2,1,0:T(8,128)S(1)} %constant_dynamic-update-slice_fusion.mine, ...), custom_call_target="tpu_custom_call" | custom-call | tf_op jit(solution)/shard_map/faces/pallas_call | solution.py:417
  33.2 4.5 %all-to-all-done.packed = f32[8,136,128]{2,1,0:T(8,128)S(1)} async-done(((f32[8,136,128]{2,1,0:T(8,128)}), f32[8,136,128]{2,1,0:T(8,128)S(1)}, u32[]{:S(2)}, u32[]{:S(2)}) %all-to-all-start) | async-done | bytes 557088 | tf_op jit(solution)/shard_map/all_to_all | solution.py:485
  37.6 3.2 %four_steps.1 = (f32[16,16,128]{2,1,0:T(8,128)S(1)}, f32[16,16,128]{2,1,0:T(8,128)S(1)}, f32[16,8,128]{2,1,0:T(8,128)S(1)}, f32[16,8,128]{2,1,0:T(8,128)S(1)}) custom-call(s32[6]{0:T(128)S(1)} %stack.86.info, f32[8,128]{1,0:T(8,128)S(1)} %get-tuple-element.25.rates, f32[8,136,128]{2,1,0:T(8,128)S(1)} %all-to-all-done.packed, ...), custom_call_target="tpu_custom_call" | custom-call | tf_op jit(solution)/shard_map/four_steps/pallas_call | solution.py:509
  40.8 0.1 collective-permute-start.10
  40.9 1.6 %collective-permute-start.11 = (f32[16,8,128]{2,1,0:T(8,128)S(1)}, f32[16,8,128]{2,1,0:T(8,128)S(1)}, u32[]{:S(2)}, u32[]{:S(2)}) collective-permute-start(f32[16,8,128]{2,1,0:T(8,128)S(1)} %get-tuple-element.45), channel_id=1, source_target_pairs={{0,9},{1,8},{2,11},{3,10},{4,13},{5,12},{6,15},{7,14},{8,1},{9,0},... | collective-permute-start | bytes 196616 | tf_op jit(solution)/shard_map/ppermute | solution.py:374
  42.5 0.1 collective-permute-start.12
  42.6 0.1 stack.78.info
  42.6 2.2 %collective-permute-done.11.halo_one = f32[16,8,128]{2,1,0:T(8,128)S(1)} collective-permute-done((f32[16,8,128]{2,1,0:T(8,128)S(1)}, f32[16,8,128]{2,1,0:T(8,128)S(1)}, u32[]{:S(2)}, u32[]{:S(2)}) %collective-permute-start.11) | collective-permute-done | bytes 65568 | tf_op jit(solution)/shard_map/ppermute | solution.py:374
  44.8 0.0 collective-permute-done.12.halo_two
  44.8 0.0 collective-permute-done.10.passed
  44.8 2.5 %three_steps.1 = f32[8,2,2,16,128]{4,3,2,1,0:T(8,128)S(1)} custom-call(s32[5]{0:T(128)S(1)} %stack.78.info, f32[8,128]{1,0:T(8,128)S(1)} %get-tuple-element.25.rates, f32[8,136,128]{2,1,0:T(8,128)S(1)} %all-to-all-done.packed, f32[16,16,128]{2,1,0:T(8,128)S(1)} %collective-permute-done.10.passed, f32[16,8,128]{2,1,0:T(8,128)S(1)} %collective-permute-done.11.halo_one, ...), custom_call_target="tpu_custom_call" | custom-call | tf_op jit(solution)/shard_map/three_steps/pallas_call | solution.py:526
  47.3 13.2 %all_to_all.10.result = f32[8,2,2,16,128]{4,3,2,1,0:T(8,128)S(1)} all-to-all(f32[8,2,2,16,128]{4,3,2,1,0:T(8,128)S(1)} %three_steps.1), channel_id=1, replica_groups=mesh['copy'=2,'tm'=2,'space'=8] {'space'}, dimensions={0} | all-to-all | bytes 524288 | tf_op jit(solution)/shard_map/all_to_all | solution.py:535
  60.6 0.8 %unpack.1 = (f32[1,2,128,128]{3,2,1,0:T(8,128)}, f32[1,2,128,128]{3,2,1,0:T(8,128)}) custom-call(f32[8,2,2,16,128]{4,3,2,1,0:T(8,128)S(1)} %all_to_all.10.result), custom_call_target="tpu_custom_call" | custom-call | tf_op jit(solution)/shard_map/unpack/pallas_call | solution.py:540
  (6 shorter events, 0.1 us)
Async XLA Ops:
  2.6 6.7 %collective-permute-start = (f32[128,128]{1,0:T(8,128)S(1)}, f32[128,128]{1,0:T(8,128)S(1)}, u32[]{:S(2)}, u32[]{:S(2)}) collective-permute-start(f32[128,128]{1,0:T(8,128)S(1)} %get-tuple-element.26), channel_id=1, source_target_pairs={{0,1},{1,0},{2,3},{3,2},{4,5},{5,4},{6,7},{7,6},{8,9},{9,8},{10,11... | collective-permute-start | bytes 196616 | tf_op jit(solution)/shard_map/ppermute | solution.py:374
  5.6 3.7 %collective-permute-start.1 = (f32[128,128]{1,0:T(8,128)S(1)}, f32[128,128]{1,0:T(8,128)S(1)}, u32[]{:S(2)}, u32[]{:S(2)}) collective-permute-start(f32[128,128]{1,0:T(8,128)S(1)} %get-tuple-element.27), channel_id=1, source_target_pairs={{0,8},{1,2},{2,1},{3,4},{4,3},{5,6},{6,5},{7,15},{8,0},{9,10},{10,... | collective-permute-start | bytes 196616 | tf_op jit(solution)/shard_map/ppermute | solution.py:374
  6.2 6.0 %collective-permute-start.3 = (f32[4,2,32,128]{3,2,1,0:T(8,128)S(1)}, f32[4,2,32,128]{3,2,1,0:T(8,128)S(1)}, u32[]{:S(2)}, u32[]{:S(2)}) collective-permute-start(f32[4,2,32,128]{3,2,1,0:T(8,128)S(1)} %get-tuple-element.33), channel_id=1, source_target_pairs={{0,1},{1,0},{2,3},{3,2},{4,5},{5,4},{6,7},{7,6},{8,9},{9,8},{10,11... | collective-permute-start | bytes 393224 | tf_op jit(solution)/shard_map/ppermute | solution.py:374
  9.3 7.7 %collective-permute-start.2 = (f32[2,128,128]{2,1,0:T(8,128)S(1)}, f32[2,128,128]{2,1,0:T(8,128)S(1)}, u32[]{:S(2)}, u32[]{:S(2)}) collective-permute-start(f32[2,128,128]{2,1,0:T(8,128)S(1)} %pad_maximum_fusion.mine), channel_id=1, source_target_pairs={{0,8},{1,9},{2,10},{3,11},{4,12},{5,13},{6,14},{7,15},{8,0},{9,1},... | collective-permute-start | bytes 393224 | tf_op jit(solution)/shard_map/ppermute | solution.py:374
  12.3 11.8 %collective-permute-start.6 = (f32[2,2,32,128]{3,2,1,0:T(8,128)S(1)}, f32[2,2,32,128]{3,2,1,0:T(8,128)S(1)}, u32[]{:S(2)}, u32[]{:S(2)}) collective-permute-start(f32[2,2,32,128]{3,2,1,0:T(8,128)S(1)} %get-tuple-element.48), channel_id=1, source_target_pairs={{0,6},{1,7},{2,4},{3,5},{4,2},{5,3},{6,0},{7,1},{8,14},{9,15},{10,... | collective-permute-start | bytes 196616 | tf_op jit(solution)/shard_map/ppermute | solution.py:374
  16.4 7.6 %collective-permute-start.4 = (f32[2,2,32,128]{3,2,1,0:T(8,128)S(1)}, f32[2,2,32,128]{3,2,1,0:T(8,128)S(1)}, u32[]{:S(2)}, u32[]{:S(2)}) collective-permute-start(f32[2,2,32,128]{3,2,1,0:T(8,128)S(1)} %get-tuple-element.50), channel_id=1, source_target_pairs={{0,2},{1,3},{2,0},{3,1},{4,6},{5,7},{6,4},{7,5},{8,10},{9,11},{10,... | collective-permute-start | bytes 196616 | tf_op jit(solution)/shard_map/ppermute | solution.py:374
  16.4 7.6 %collective-permute-start.5 = (f32[2,2,32,128]{3,2,1,0:T(8,128)S(1)}, f32[2,2,32,128]{3,2,1,0:T(8,128)S(1)}, u32[]{:S(2)}, u32[]{:S(2)}) collective-permute-start(f32[2,2,32,128]{3,2,1,0:T(8,128)S(1)} %get-tuple-element.51), channel_id=1, source_target_pairs={{0,4},{1,5},{2,6},{3,7},{4,0},{5,1},{6,2},{7,3},{8,12},{9,13},{10,... | collective-permute-start | bytes 196616 | tf_op jit(solution)/shard_map/ppermute | solution.py:374
  19.0 18.7 %all-to-all-start = ((f32[8,136,128]{2,1,0:T(8,128)}), f32[8,136,128]{2,1,0:T(8,128)S(1)}, u32[]{:S(2)}, u32[]{:S(2)}) async-start(f32[8,136,128]{2,1,0:T(8,128)} %bounds.1), calls=%async_computation | async-start | bytes 1114112 | tf_op jit(solution)/shard_map/all_to_all | solution.py:485
  24.1 6.4 %collective-permute-start.7 = (f32[8,2,32,128]{3,2,1,0:T(8,128)S(1)}, f32[8,2,32,128]{3,2,1,0:T(8,128)S(1)}, u32[]{:S(2)}, u32[]{:S(2)}) collective-permute-start(f32[8,2,32,128]{3,2,1,0:T(8,128)S(1)} %constant_dynamic-update-slice_fusion.mine), channel_id=1, source_target_pairs={{0,16},{1,17},{2,18},{3,19},{4,20},{5,21},{6,22},{7,23},{8,24},{9,... | collective-permute-start | bytes 786440 | tf_op jit(solution)/shard_map/ppermute | solution.py:374
  25.7 4.9 %collective-permute-start.8 = (f32[8,2,32,128]{3,2,1,0:T(8,128)S(1)}, f32[8,2,32,128]{3,2,1,0:T(8,128)S(1)}, u32[]{:S(2)}, u32[]{:S(2)}) collective-permute-start(f32[8,2,32,128]{3,2,1,0:T(8,128)S(1)} %constant_dynamic-update-slice_fusion.mine), channel_id=1, source_target_pairs={{0,8},{1,9},{2,10},{3,11},{4,12},{5,13},{6,14},{7,15},{8,0},{9,1},... | collective-permute-start | bytes 786440 | tf_op jit(solution)/shard_map/ppermute | solution.py:374
  30.5 1.5 %collective-permute-start.9 = (f32[8,2,32,128]{3,2,1,0:T(8,128)S(1)}, f32[8,2,32,128]{3,2,1,0:T(8,128)S(1)}, u32[]{:S(2)}, u32[]{:S(2)}) collective-permute-start(f32[8,2,32,128]{3,2,1,0:T(8,128)S(1)} %collective-permute-done.7.beside), channel_id=1, source_target_pairs={{0,8},{1,9},{2,10},{3,11},{4,12},{5,13},{6,14},{7,15},{8,0},{9,1},... | collective-permute-start | bytes 786440 | tf_op jit(solution)/shard_map/ppermute | solution.py:374
  40.8 4.0 %collective-permute-start.10 = (f32[16,16,128]{2,1,0:T(8,128)S(1)}, f32[16,16,128]{2,1,0:T(8,128)S(1)}, u32[]{:S(2)}, u32[]{:S(2)}) collective-permute-start(f32[16,16,128]{2,1,0:T(8,128)S(1)} %get-tuple-element.44.advanced), channel_id=1, source_target_pairs={{0,8},{1,9},{2,10},{3,11},{4,12},{5,13},{6,14},{7,15},{8,0},{9,1},... | collective-permute-start | bytes 393224 | tf_op jit(solution)/shard_map/ppermute | solution.py:374
  40.9 3.9 %collective-permute-start.11 = (f32[16,8,128]{2,1,0:T(8,128)S(1)}, f32[16,8,128]{2,1,0:T(8,128)S(1)}, u32[]{:S(2)}, u32[]{:S(2)}) collective-permute-start(f32[16,8,128]{2,1,0:T(8,128)S(1)} %get-tuple-element.45), channel_id=1, source_target_pairs={{0,9},{1,8},{2,11},{3,10},{4,13},{5,12},{6,15},{7,14},{8,1},{9,0},... | collective-permute-start | bytes 196616 | tf_op jit(solution)/shard_map/ppermute | solution.py:374
  42.5 2.3 %collective-permute-start.12 = (f32[16,8,128]{2,1,0:T(8,128)S(1)}, f32[16,8,128]{2,1,0:T(8,128)S(1)}, u32[]{:S(2)}, u32[]{:S(2)}) collective-permute-start(f32[16,8,128]{2,1,0:T(8,128)S(1)} %get-tuple-element.46), channel_id=1, source_target_pairs={{0,8},{1,11},{2,12},{3,9},{4,10},{5,15},{6,14},{7,13},{8,0},{9,3},... | collective-permute-start | bytes 196616 | tf_op jit(solution)/shard_map/ppermute | solution.py:374

commit v7 on v6

--- a/solution.py
+++ b/solution.py
@@ -91,7 +91,14 @@
             packed[spot, pl.ds((layers + layer) * width, width)] = windows(forcing[layer], slab_of(spot, packed.shape[0]), rows, width)
 
 
-def bound_kernel(rows, width, info, rates, mine, other, masked, wind, state, forcing, out):
+def bound_kernel(rows, width, info, rates, mine, other, masked, wind, state, forcing, out, bulk, tail, sems):
+    size = bulk.shape[1]
+    pack_own(rows, width, state, forcing, bulk)
+    copies = [
+        pltpu.make_async_copy(bulk, out.at[:, pl.ds(0, size)], sems.at[0]),
+        pltpu.make_async_copy(tail, out.at[:, pl.ds(size, tail.shape[1])], sems.at[1]),
+    ]
+    copies[0].start()
     first, even = info[0] == 0, info[1] % 2 == 0
     here, there = (mine[0], mine[1]), (other[0], other[1])
 
@@ -104,7 +111,7 @@
     masked_sides = sides(jnp.where(first, here[0], there[0]), jnp.where(first, here[1], there[1]), True)
     wind_sides = sides(jnp.where(first, there[0], here[0]), jnp.where(first, there[1], here[1]), False)
     layers, depth, lanes = masked.shape
-    chunk = 32 if depth % 32 == 0 else depth
+    chunk = 16 if depth % 16 == 0 else depth
     row = lax.broadcasted_iota(jnp.int32, (chunk, lanes), 0)
     inner_lane = lax.broadcasted_iota(jnp.int32, (chunk, lanes), 1) < lanes - 1
 
@@ -112,7 +119,7 @@
         both = jnp.where((here > 0.0) & (ahead > 0.0), 1.0, 0.0)
         return jnp.sqrt(here * ahead), jnp.abs(0.5 * (wind_here + wind_ahead) * both)
 
-    peaks = [jnp.zeros((chunk, lanes), jnp.float32)] * FINE
+    peaks = [jnp.zeros((8, lanes), jnp.float32)] * FINE
     edge = [[jnp.zeros((1, lanes), jnp.float32)] * 2 for _ in range(layers)]
     for start in range(0, depth, chunk):
         part = pl.ds(start, chunk)
@@ -147,15 +154,17 @@
                 sums[number] = sums[number] + value + pltpu.roll(value, 1, 1)
             still = 1.0 + 2.0 * sums[0]
             for k in range(FINE):
-                peaks[k] = jnp.maximum(peaks[k], still + rates[pl.ds(k, 1)] * sums[1])
+                bound = still + rates[pl.ds(k, 1)] * sums[1]
+                for first_row in range(0, chunk, 8):
+                    peaks[k] = jnp.maximum(peaks[k], bound[first_row : first_row + 8])
     bounds = jnp.zeros((8, lanes), jnp.float32)
     place = lax.broadcasted_iota(jnp.int32, (8, lanes), 0)
     for k in range(FINE):
         bounds = jnp.where(place == k, jnp.max(peaks[k]), bounds)
-    pack_own(rows, width, state, forcing, out)
-    start = out.shape[1] - 8
-    for spot in range(out.shape[0]):
-        out[spot, pl.ds(start, 8)] = bounds
+    tail[...] = jnp.broadcast_to(bounds, tail.shape)
+    copies[1].start()
+    for copy in copies:
+        copy.wait()
 
 
 def roll_back(values, axis):
@@ -463,20 +472,20 @@
     edge_two = swapped(edge_two, sizes, outer_partner(count))
     edges = jnp.stack([edge_one, edge_two])
     other_edges = swapped(edges, sizes, lambda t, s: (t ^ 1, s))
-    (packed,) = call(
+    size = 2 * layers * width
+    packed = pl.pallas_call(
         functools.partial(bound_kernel, rows, width),
-        [struct(count, 2 * layers * width + 8, lanes)],
-        [SMEM] + [VMEM] * 7,
-        "bounds",
-        info,
-        rates,
-        edges,
-        other_edges,
-        masked,
-        winds,
-        state,
-        forcing,
-    )
+        out_shape=struct(count, size + 8, lanes),
+        in_specs=[SMEM] + [VMEM] * 7,
+        out_specs=pl.BlockSpec(memory_space=pl.ANY),
+        scratch_shapes=[
+            pltpu.VMEM((count, size, lanes), jnp.float32),
+            pltpu.VMEM((count, 8, lanes), jnp.float32),
+            pltpu.SemaphoreType.DMA((2,)),
+        ],
+        compiler_params=params,
+        name="bounds",
+    )(info, rates, edges, other_edges, masked, winds, state, forcing)
     pieces = jnp.stack([same, across], axis=1)
     parts = [pieces[0]]
     for step in range(1, count // 2):

time: 61.7 us -> 61.6 us (level)
    pallas_call x4 -> x3, Pallas kernels: 5.41 us -> 3.47 us  [call(): pl.pallas_call(kernel, out_shape=outs, in_specs=in_specs, out_specs=[VMEM...]
    pallas_call x0 -> x1, Pallas kernels: none -> 1.85 us  [shards(): pl.pallas_call(functools.partial(bound_kernel, rows, width), out_shape=st...]
where the time goes in v7:
time: 61.6 us; the launch traced here: 61.3 us
  starting transfers between devices  19.3 us (31%)
  waiting for transfers between devices  15.9 us (26%)
  blocking collectives  13.2 us (21%)
  Pallas kernels  11.9 us (19%)
  between operations  0.81 us (1%)
    ppermute x13, starting transfers between devices, swapped(): return lax.ppermute(array, AXES, pairs)  14.3 us
    all_to_all x1, blocking collectives, shards(): result = lax.all_to_all(result, 'space', 0, 0, tiled=True)  13.2 us
    ppermute x13, waiting for transfers between devices, swapped(): return lax.ppermute(array, AXES, pairs)  11.4 us
    all_to_all x1, starting transfers between devices, shards(): packed = lax.all_to_all(packed, 'space', 0, 0, tiled=True)  5.03 us
    all_to_all x1, waiting for transfers between devices, shards(): packed = lax.all_to_all(packed, 'space', 0, 0, tiled=True)  4.46 us
    pallas_call x3, Pallas kernels, call(): pl.pallas_call(kernel, out_shape=outs, in_specs=in_specs, out_specs=[VMEM...  3.47 us
    pallas_call x1, Pallas kernels, shards(): pl.pallas_call(functools.partial(first_kernel, rows, width, layers), out_...  3.18 us
    pallas_call x1, Pallas kernels, shards(): pl.pallas_call(functools.partial(second_kernel, rows, width, layers), out...  2.53 us
  transfers between devices with their start and end apart: 14, of which 5 were waited for; matrix products, arithmetic and copies ran while one was open for 0% of the time, Pallas kernels for 6%

profile of v7, /device:TPU:0, one launch (start us, length us, event | category | flops | bytes accessed | tf_op | source)
XLA Modules:
  0.0 61.3 jit_solution(691352540293878662)
XLA Ops:
  0.7 0.1 stack.86.info
  0.8 1.8 %load.1 = (f32[2,128,128]{2,1,0:T(8,128)S(1)}, f32[3,2,128,128]{3,2,1,0:T(8,128)S(1)}, f32[2,128,128]{2,1,0:T(8,128)S(1)}, f32[2,128,128]{2,1,0:T(8,128)S(1)}, f...) custom-call(s32[6]{0:T(128)S(1)} %stack.86.info, f32[1,2,128,128]{3,2,1,0:T(8,128)} %initial.1, ...), custom_call_target="tpu_custom_call" | custom-call | tf_op jit(solution)/shard_map/load/pallas_call | solution.py:426
  2.6 3.0 %collective-permute-start = (f32[128,128]{1,0:T(8,128)S(1)}, f32[128,128]{1,0:T(8,128)S(1)}, u32[]{:S(2)}, u32[]{:S(2)}) collective-permute-start(f32[128,128]{1,0:T(8,128)S(1)} %get-tuple-element.26), channel_id=1, source_target_pairs={{0,1},{1,0},{2,3},{3,2},{4,5},{5,4},{6,7},{7,6},{8,9},{9,8},{10,11... | collective-permute-start | bytes 196616 | tf_op jit(solution)/shard_map/ppermute | solution.py:383
  5.6 0.0 collective-permute-start.1
  5.6 0.6 pack_shared.1
  6.2 3.1 %collective-permute-start.3 = (f32[4,2,32,128]{3,2,1,0:T(8,128)S(1)}, f32[4,2,32,128]{3,2,1,0:T(8,128)S(1)}, u32[]{:S(2)}, u32[]{:S(2)}) collective-permute-start(f32[4,2,32,128]{3,2,1,0:T(8,128)S(1)} %get-tuple-element.33), channel_id=1, source_target_pairs={{0,1},{1,0},{2,3},{3,2},{4,5},{5,4},{6,7},{7,6},{8,9},{9,8},{10,11... | collective-permute-start | bytes 393224 | tf_op jit(solution)/shard_map/ppermute | solution.py:383
  9.3 0.0 collective-permute-done
  9.3 0.0 collective-permute-done.1
  9.3 0.1 collective-permute-start.2
  9.4 2.8 %collective-permute-done.3 = f32[4,2,32,128]{3,2,1,0:T(8,128)S(1)} collective-permute-done((f32[4,2,32,128]{3,2,1,0:T(8,128)S(1)}, f32[4,2,32,128]{3,2,1,0:T(8,128)S(1)}, u32[]{:S(2)}, u32[]{:S(2)}) %collective-permute-start.3) | collective-permute-done | bytes 131104 | tf_op jit(solution)/shard_map/ppermute | solution.py:383
  12.3 4.2 %collective-permute-start.6 = (f32[2,2,32,128]{3,2,1,0:T(8,128)S(1)}, f32[2,2,32,128]{3,2,1,0:T(8,128)S(1)}, u32[]{:S(2)}, u32[]{:S(2)}) collective-permute-start(f32[2,2,32,128]{3,2,1,0:T(8,128)S(1)} %get-tuple-element.48), channel_id=1, source_target_pairs={{0,6},{1,7},{2,4},{3,5},{4,2},{5,3},{6,0},{7,1},{8,14},{9,15},{10,... | collective-permute-start | bytes 196616 | tf_op jit(solution)/shard_map/ppermute | solution.py:383
  16.4 0.0 collective-permute-start.4
  16.4 0.6 %collective-permute-start.5 = (f32[2,2,32,128]{3,2,1,0:T(8,128)S(1)}, f32[2,2,32,128]{3,2,1,0:T(8,128)S(1)}, u32[]{:S(2)}, u32[]{:S(2)}) collective-permute-start(f32[2,2,32,128]{3,2,1,0:T(8,128)S(1)} %get-tuple-element.51), channel_id=1, source_target_pairs={{0,4},{1,5},{2,6},{3,7},{4,0},{5,1},{6,2},{7,3},{8,12},{9,13},{10,... | collective-permute-start | bytes 196616 | tf_op jit(solution)/shard_map/ppermute | solution.py:383
  17.1 0.0 collective-permute-done.2.other
  17.1 1.9 %bounds.1 = f32[8,136,128]{2,1,0:T(8,128)} custom-call(s32[6]{0:T(128)S(1)} %stack.86.info, f32[8,128]{1,0:T(8,128)S(1)} %get-tuple-element.25.rates, f32[2,128,128]{2,1,0:T(8,128)S(1)} %pad_maximum_fusion.mine, f32[2,128,128]{2,1,0:T(8,128)S(1)} %collective-permute-done.2.other, f32[2,128,128]{2,1,0:T(8,128)S(1)} %get-tuple-element.28.masked, ...), custom_call_target="tpu_custom_call" | custom-call | tf_op jit(solution)/shard_map/bounds/pallas_call | solution.py:476
  18.9 5.0 %all-to-all-start = ((f32[8,136,128]{2,1,0:T(8,128)}), f32[8,136,128]{2,1,0:T(8,128)S(1)}, u32[]{:S(2)}, u32[]{:S(2)}) async-start(f32[8,136,128]{2,1,0:T(8,128)} %bounds.1), calls=%async_computation | async-start | bytes 1114112 | tf_op jit(solution)/shard_map/all_to_all | solution.py:494
  23.9 0.0 collective-permute-done.6
  24.0 0.0 collective-permute-done.4
  24.0 0.0 collective-permute-done.5
  24.0 1.6 %collective-permute-start.7 = (f32[8,2,32,128]{3,2,1,0:T(8,128)S(1)}, f32[8,2,32,128]{3,2,1,0:T(8,128)S(1)}, u32[]{:S(2)}, u32[]{:S(2)}) collective-permute-start(f32[8,2,32,128]{3,2,1,0:T(8,128)S(1)} %constant_dynamic-update-slice_fusion.mine), channel_id=1, source_target_pairs={{0,16},{1,17},{2,18},{3,19},{4,20},{5,21},{6,22},{7,23},{8,24},{9,... | collective-permute-start | bytes 786440 | tf_op jit(solution)/shard_map/ppermute | solution.py:383
  25.6 0.0 collective-permute-start.8
  25.6 4.9 %collective-permute-done.7.beside = f32[8,2,32,128]{3,2,1,0:T(8,128)S(1)} collective-permute-done((f32[8,2,32,128]{3,2,1,0:T(8,128)S(1)}, f32[8,2,32,128]{3,2,1,0:T(8,128)S(1)}, u32[]{:S(2)}, u32[]{:S(2)}) %collective-permute-start.7) | collective-permute-done | bytes 262176 | tf_op jit(solution)/shard_map/ppermute | solution.py:383
  30.5 0.0 collective-permute-start.9
  30.5 0.0 collective-permute-done.8.other
  30.5 1.5 %collective-permute-done.9.other_beside = f32[8,2,32,128]{3,2,1,0:T(8,128)S(1)} collective-permute-done((f32[8,2,32,128]{3,2,1,0:T(8,128)S(1)}, f32[8,2,32,128]{3,2,1,0:T(8,128)S(1)}, u32[]{:S(2)}, u32[]{:S(2)}) %collective-permute-start.9) | collective-permute-done | bytes 262176 | tf_op jit(solution)/shard_map/ppermute | solution.py:383
  32.0 1.1 %faces.1 = (f32[16,32,128]{2,1,0:T(8,128)S(1)}, f32[16,32,128]{2,1,0:T(8,128)S(1)}, f32[16,32,128]{2,1,0:T(8,128)S(1)}, f32[16,32,128]{2,1,0:T(8,128)S(1)}, f32[...) custom-call(s32[6]{0:T(128)S(1)} %stack.86.info, f32[8,2,32,128]{3,2,1,0:T(8,128)S(1)} %constant_dynamic-update-slice_fusion.mine, ...), custom_call_target="tpu_custom_call" | custom-call | tf_op jit(solution)/shard_map/faces/pallas_call | solution.py:426
  33.1 4.5 %all-to-all-done.packed = f32[8,136,128]{2,1,0:T(8,128)S(1)} async-done(((f32[8,136,128]{2,1,0:T(8,128)}), f32[8,136,128]{2,1,0:T(8,128)S(1)}, u32[]{:S(2)}, u32[]{:S(2)}) %all-to-all-start) | async-done | bytes 557088 | tf_op jit(solution)/shard_map/all_to_all | solution.py:494
  37.6 3.2 %four_steps.1 = (f32[16,16,128]{2,1,0:T(8,128)S(1)}, f32[16,16,128]{2,1,0:T(8,128)S(1)}, f32[16,8,128]{2,1,0:T(8,128)S(1)}, f32[16,8,128]{2,1,0:T(8,128)S(1)}) custom-call(s32[6]{0:T(128)S(1)} %stack.86.info, f32[8,128]{1,0:T(8,128)S(1)} %get-tuple-element.25.rates, f32[8,136,128]{2,1,0:T(8,128)S(1)} %all-to-all-done.packed, ...), custom_call_target="tpu_custom_call" | custom-call | tf_op jit(solution)/shard_map/four_steps/pallas_call | solution.py:518
  40.8 0.1 collective-permute-start.10
  40.8 1.6 %collective-permute-start.11 = (f32[16,8,128]{2,1,0:T(8,128)S(1)}, f32[16,8,128]{2,1,0:T(8,128)S(1)}, u32[]{:S(2)}, u32[]{:S(2)}) collective-permute-start(f32[16,8,128]{2,1,0:T(8,128)S(1)} %get-tuple-element.45), channel_id=1, source_target_pairs={{0,9},{1,8},{2,11},{3,10},{4,13},{5,12},{6,15},{7,14},{8,1},{9,0},... | collective-permute-start | bytes 196616 | tf_op jit(solution)/shard_map/ppermute | solution.py:383
  42.4 0.1 collective-permute-start.12
  42.5 0.1 stack.78.info
  42.6 2.2 %collective-permute-done.11.halo_one = f32[16,8,128]{2,1,0:T(8,128)S(1)} collective-permute-done((f32[16,8,128]{2,1,0:T(8,128)S(1)}, f32[16,8,128]{2,1,0:T(8,128)S(1)}, u32[]{:S(2)}, u32[]{:S(2)}) %collective-permute-start.11) | collective-permute-done | bytes 65568 | tf_op jit(solution)/shard_map/ppermute | solution.py:383
  44.7 0.0 collective-permute-done.12.halo_two
  44.7 0.0 collective-permute-done.10.passed
  44.7 2.5 %three_steps.1 = f32[8,2,2,16,128]{4,3,2,1,0:T(8,128)S(1)} custom-call(s32[5]{0:T(128)S(1)} %stack.78.info, f32[8,128]{1,0:T(8,128)S(1)} %get-tuple-element.25.rates, f32[8,136,128]{2,1,0:T(8,128)S(1)} %all-to-all-done.packed, f32[16,16,128]{2,1,0:T(8,128)S(1)} %collective-permute-done.10.passed, f32[16,8,128]{2,1,0:T(8,128)S(1)} %collective-permute-done.11.halo_one, ...), custom_call_target="tpu_custom_call" | custom-call | tf_op jit(solution)/shard_map/three_steps/pallas_call | solution.py:535
  47.3 13.2 %all_to_all.10.result = f32[8,2,2,16,128]{4,3,2,1,0:T(8,128)S(1)} all-to-all(f32[8,2,2,16,128]{4,3,2,1,0:T(8,128)S(1)} %three_steps.1), channel_id=1, replica_groups=mesh['copy'=2,'tm'=2,'space'=8] {'space'}, dimensions={0} | all-to-all | bytes 524288 | tf_op jit(solution)/shard_map/all_to_all | solution.py:544
  60.5 0.8 %unpack.1 = (f32[1,2,128,128]{3,2,1,0:T(8,128)}, f32[1,2,128,128]{3,2,1,0:T(8,128)}) custom-call(f32[8,2,2,16,128]{4,3,2,1,0:T(8,128)S(1)} %all_to_all.10.result), custom_call_target="tpu_custom_call" | custom-call | tf_op jit(solution)/shard_map/unpack/pallas_call | solution.py:549
  (6 shorter events, 0.1 us)
Async XLA Ops:
  2.6 6.7 %collective-permute-start = (f32[128,128]{1,0:T(8,128)S(1)}, f32[128,128]{1,0:T(8,128)S(1)}, u32[]{:S(2)}, u32[]{:S(2)}) collective-permute-start(f32[128,128]{1,0:T(8,128)S(1)} %get-tuple-element.26), channel_id=1, source_target_pairs={{0,1},{1,0},{2,3},{3,2},{4,5},{5,4},{6,7},{7,6},{8,9},{9,8},{10,11... | collective-permute-start | bytes 196616 | tf_op jit(solution)/shard_map/ppermute | solution.py:383
  5.6 3.7 %collective-permute-start.1 = (f32[128,128]{1,0:T(8,128)S(1)}, f32[128,128]{1,0:T(8,128)S(1)}, u32[]{:S(2)}, u32[]{:S(2)}) collective-permute-start(f32[128,128]{1,0:T(8,128)S(1)} %get-tuple-element.27), channel_id=1, source_target_pairs={{0,8},{1,2},{2,1},{3,4},{4,3},{5,6},{6,5},{7,15},{8,0},{9,10},{10,... | collective-permute-start | bytes 196616 | tf_op jit(solution)/shard_map/ppermute | solution.py:383
  6.2 6.0 %collective-permute-start.3 = (f32[4,2,32,128]{3,2,1,0:T(8,128)S(1)}, f32[4,2,32,128]{3,2,1,0:T(8,128)S(1)}, u32[]{:S(2)}, u32[]{:S(2)}) collective-permute-start(f32[4,2,32,128]{3,2,1,0:T(8,128)S(1)} %get-tuple-element.33), channel_id=1, source_target_pairs={{0,1},{1,0},{2,3},{3,2},{4,5},{5,4},{6,7},{7,6},{8,9},{9,8},{10,11... | collective-permute-start | bytes 393224 | tf_op jit(solution)/shard_map/ppermute | solution.py:383
  9.3 7.7 %collective-permute-start.2 = (f32[2,128,128]{2,1,0:T(8,128)S(1)}, f32[2,128,128]{2,1,0:T(8,128)S(1)}, u32[]{:S(2)}, u32[]{:S(2)}) collective-permute-start(f32[2,128,128]{2,1,0:T(8,128)S(1)} %pad_maximum_fusion.mine), channel_id=1, source_target_pairs={{0,8},{1,9},{2,10},{3,11},{4,12},{5,13},{6,14},{7,15},{8,0},{9,1},... | collective-permute-start | bytes 393224 | tf_op jit(solution)/shard_map/ppermute | solution.py:383
  12.3 11.7 %collective-permute-start.6 = (f32[2,2,32,128]{3,2,1,0:T(8,128)S(1)}, f32[2,2,32,128]{3,2,1,0:T(8,128)S(1)}, u32[]{:S(2)}, u32[]{:S(2)}) collective-permute-start(f32[2,2,32,128]{3,2,1,0:T(8,128)S(1)} %get-tuple-element.48), channel_id=1, source_target_pairs={{0,6},{1,7},{2,4},{3,5},{4,2},{5,3},{6,0},{7,1},{8,14},{9,15},{10,... | collective-permute-start | bytes 196616 | tf_op jit(solution)/shard_map/ppermute | solution.py:383
  16.4 7.5 %collective-permute-start.4 = (f32[2,2,32,128]{3,2,1,0:T(8,128)S(1)}, f32[2,2,32,128]{3,2,1,0:T(8,128)S(1)}, u32[]{:S(2)}, u32[]{:S(2)}) collective-permute-start(f32[2,2,32,128]{3,2,1,0:T(8,128)S(1)} %get-tuple-element.50), channel_id=1, source_target_pairs={{0,2},{1,3},{2,0},{3,1},{4,6},{5,7},{6,4},{7,5},{8,10},{9,11},{10,... | collective-permute-start | bytes 196616 | tf_op jit(solution)/shard_map/ppermute | solution.py:383
  16.4 7.6 %collective-permute-start.5 = (f32[2,2,32,128]{3,2,1,0:T(8,128)S(1)}, f32[2,2,32,128]{3,2,1,0:T(8,128)S(1)}, u32[]{:S(2)}, u32[]{:S(2)}) collective-permute-start(f32[2,2,32,128]{3,2,1,0:T(8,128)S(1)} %get-tuple-element.51), channel_id=1, source_target_pairs={{0,4},{1,5},{2,6},{3,7},{4,0},{5,1},{6,2},{7,3},{8,12},{9,13},{10,... | collective-permute-start | bytes 196616 | tf_op jit(solution)/shard_map/ppermute | solution.py:383
  18.9 18.7 %all-to-all-start = ((f32[8,136,128]{2,1,0:T(8,128)}), f32[8,136,128]{2,1,0:T(8,128)S(1)}, u32[]{:S(2)}, u32[]{:S(2)}) async-start(f32[8,136,128]{2,1,0:T(8,128)} %bounds.1), calls=%async_computation | async-start | bytes 1114112 | tf_op jit(solution)/shard_map/all_to_all | solution.py:494
  24.0 6.4 %collective-permute-start.7 = (f32[8,2,32,128]{3,2,1,0:T(8,128)S(1)}, f32[8,2,32,128]{3,2,1,0:T(8,128)S(1)}, u32[]{:S(2)}, u32[]{:S(2)}) collective-permute-start(f32[8,2,32,128]{3,2,1,0:T(8,128)S(1)} %constant_dynamic-update-slice_fusion.mine), channel_id=1, source_target_pairs={{0,16},{1,17},{2,18},{3,19},{4,20},{5,21},{6,22},{7,23},{8,24},{9,... | collective-permute-start | bytes 786440 | tf_op jit(solution)/shard_map/ppermute | solution.py:383
  25.6 4.9 %collective-permute-start.8 = (f32[8,2,32,128]{3,2,1,0:T(8,128)S(1)}, f32[8,2,32,128]{3,2,1,0:T(8,128)S(1)}, u32[]{:S(2)}, u32[]{:S(2)}) collective-permute-start(f32[8,2,32,128]{3,2,1,0:T(8,128)S(1)} %constant_dynamic-update-slice_fusion.mine), channel_id=1, source_target_pairs={{0,8},{1,9},{2,10},{3,11},{4,12},{5,13},{6,14},{7,15},{8,0},{9,1},... | collective-permute-start | bytes 786440 | tf_op jit(solution)/shard_map/ppermute | solution.py:383
  30.5 1.5 %collective-permute-start.9 = (f32[8,2,32,128]{3,2,1,0:T(8,128)S(1)}, f32[8,2,32,128]{3,2,1,0:T(8,128)S(1)}, u32[]{:S(2)}, u32[]{:S(2)}) collective-permute-start(f32[8,2,32,128]{3,2,1,0:T(8,128)S(1)} %collective-permute-done.7.beside), channel_id=1, source_target_pairs={{0,8},{1,9},{2,10},{3,11},{4,12},{5,13},{6,14},{7,15},{8,0},{9,1},... | collective-permute-start | bytes 786440 | tf_op jit(solution)/shard_map/ppermute | solution.py:383
  40.8 4.0 %collective-permute-start.10 = (f32[16,16,128]{2,1,0:T(8,128)S(1)}, f32[16,16,128]{2,1,0:T(8,128)S(1)}, u32[]{:S(2)}, u32[]{:S(2)}) collective-permute-start(f32[16,16,128]{2,1,0:T(8,128)S(1)} %get-tuple-element.44.advanced), channel_id=1, source_target_pairs={{0,8},{1,9},{2,10},{3,11},{4,12},{5,13},{6,14},{7,15},{8,0},{9,1},... | collective-permute-start | bytes 393224 | tf_op jit(solution)/shard_map/ppermute | solution.py:383
  40.8 3.9 %collective-permute-start.11 = (f32[16,8,128]{2,1,0:T(8,128)S(1)}, f32[16,8,128]{2,1,0:T(8,128)S(1)}, u32[]{:S(2)}, u32[]{:S(2)}) collective-permute-start(f32[16,8,128]{2,1,0:T(8,128)S(1)} %get-tuple-element.45), channel_id=1, source_target_pairs={{0,9},{1,8},{2,11},{3,10},{4,13},{5,12},{6,15},{7,14},{8,1},{9,0},... | collective-permute-start | bytes 196616 | tf_op jit(solution)/shard_map/ppermute | solution.py:383
  42.4 2.3 %collective-permute-start.12 = (f32[16,8,128]{2,1,0:T(8,128)S(1)}, f32[16,8,128]{2,1,0:T(8,128)S(1)}, u32[]{:S(2)}, u32[]{:S(2)}) collective-permute-start(f32[16,8,128]{2,1,0:T(8,128)S(1)} %get-tuple-element.46), channel_id=1, source_target_pairs={{0,8},{1,11},{2,12},{3,9},{4,10},{5,15},{6,14},{7,13},{8,0},{9,3},... | collective-permute-start | bytes 196616 | tf_op jit(solution)/shard_map/ppermute | solution.py:383

commit v8 on v6

--- a/solution.py
+++ b/solution.py
@@ -32,8 +32,8 @@
     return jnp.concatenate(parts, axis=0) if len(parts) > 1 else parts[0]
 
 
-def load_kernel(info, initial, source, diffusion, wind, buildings, strength, *rest):
-    masked, winds, state, forcing, edge_one, edge_two, rates, fresh, early, late, solid, steps, sems = rest
+def load_kernel(rows, width, info, initial, source, diffusion, wind, buildings, strength, *rest):
+    masked, winds, state, forcing, edge_one, edge_two, rates, same, across, fresh, early, late, solid, steps, sems = rest
     pairs = (
         (diffusion, fresh),
         (buildings, solid),
@@ -55,6 +55,7 @@
     high = jnp.where(first, masked[last], winds[0, last])
     edge_one[...] = jnp.where(even, high, low)
     edge_two[...] = jnp.where(even, low, high)
+    pack_shared(rows, width, info, masked, winds, same, across)
     for copy in copies[3:]:
         copy.wait()
     state[...] = early[...] * opened
@@ -79,8 +80,9 @@
         for place in range(half):
             even = windows(field, slab_of(2 * place, 2 * half), rows, width)
             odd = windows(field, slab_of(2 * place + 1, 2 * half), rows, width)
-            same[place ^ (spot // 2), layer] = jnp.where(swap, odd, even)
-            across[place ^ (spot // 2), layer] = jnp.where(swap, even, odd)
+            entry = place ^ (spot // 2)
+            same[entry, layer] = jnp.where(swap, odd, even)
+            across[entry, layer] = jnp.where(swap, even, odd)
 
 
 def pack_own(rows, width, state, forcing, packed):
@@ -433,9 +435,10 @@
     hold = pltpu.VMEM((layers, depth, lanes), jnp.float32)
     anywhere = pl.BlockSpec(memory_space=pltpu.HBM)
     arrays = (initial, source, diffusion, wind_field, buildings, strength)
-    masked, winds, state, forcing, edge_one, edge_two, rates = call(
-        load_kernel,
-        [field, struct(3, layers, depth, lanes), field, field, outer, outer, struct(8, lanes)],
+    shared = [struct(count // 2, layers, width, lanes)] * 2
+    masked, winds, state, forcing, edge_one, edge_two, rates, same, across = call(
+        functools.partial(load_kernel, rows, width),
+        [field, struct(3, layers, depth, lanes), field, field, outer, outer, struct(8, lanes), *shared],
         [SMEM] + [anywhere] * 6,
         "load",
         info,
@@ -448,15 +451,6 @@
             pltpu.SMEM(strength.shape, jnp.float32),
             pltpu.SemaphoreType.DMA((6,)),
         ],
-    )
-    same, across = call(
-        functools.partial(pack_shared, rows, width),
-        [struct(count // 2, layers, width, lanes)] * 2,
-        [SMEM] + [VMEM] * 2,
-        "pack_shared",
-        info,
-        masked,
-        winds,
     )
     across = swapped(across, sizes, lambda t, s: (t, s ^ 1))
     edge_one = swapped(edge_one, sizes, lambda t, s: (t, s ^ 1))

time: 61.7 us -> 62 us (level)
    pallas_call x4 -> x3, Pallas kernels: 5.41 us -> 4.86 us  [call(): pl.pallas_call(kernel, out_shape=outs, in_specs=in_specs, out_specs=[VMEM...]
  transfers between devices with their start and end apart: 14 -> 14, of which waited for: 5 -> 6; matrix products, arithmetic and copies ran while one was open for 0% -> 0% of each run, Pallas kernels for 6% -> 5%
where the time goes in v8:
time: 62 us; the launch traced here: 61.7 us
  starting transfers between devices  19.7 us (32%)
  waiting for transfers between devices  16.3 us (26%)
  blocking collectives  13.2 us (21%)
  Pallas kernels  11.4 us (18%)
  between operations  0.79 us (1%)
    ppermute x13, starting transfers between devices, swapped(): return lax.ppermute(array, AXES, pairs)  14.7 us
    all_to_all x1, blocking collectives, shards(): result = lax.all_to_all(result, 'space', 0, 0, tiled=True)  13.2 us
    ppermute x13, waiting for transfers between devices, swapped(): return lax.ppermute(array, AXES, pairs)  11.7 us
    all_to_all x1, starting transfers between devices, shards(): packed = lax.all_to_all(packed, 'space', 0, 0, tiled=True)  5.02 us
    pallas_call x3, Pallas kernels, call(): pl.pallas_call(kernel, out_shape=outs, in_specs=in_specs, out_specs=[VMEM...  4.86 us
    all_to_all x1, waiting for transfers between devices, shards(): packed = lax.all_to_all(packed, 'space', 0, 0, tiled=True)  4.63 us
    pallas_call x1, Pallas kernels, shards(): pl.pallas_call(functools.partial(first_kernel, rows, width, layers), out_...  3.18 us
    pallas_call x1, Pallas kernels, shards(): pl.pallas_call(functools.partial(second_kernel, rows, width, layers), out...  2.53 us
  transfers between devices with their start and end apart: 14, of which 6 were waited for; matrix products, arithmetic and copies ran while one was open for 0% of the time, Pallas kernels for 5%

profile of v8, /device:TPU:0, one launch (start us, length us, event | category | flops | bytes accessed | tf_op | source)
XLA Modules:
  0.0 61.7 jit_solution(10170492869590714322)
XLA Ops:
  0.7 0.1 stack.86.info
  0.8 1.8 %load.1 = (f32[2,128,128]{2,1,0:T(8,128)S(1)}, f32[3,2,128,128]{3,2,1,0:T(8,128)S(1)}, f32[2,128,128]{2,1,0:T(8,128)S(1)}, f32[2,128,128]{2,1,0:T(8,128)S(1)}, f...) custom-call(s32[6]{0:T(128)S(1)} %stack.86.info, ...), custom_call_target="tpu_custom_call" | custom-call | tf_op jit(solution)/shard_map/load/pallas_call | solution.py:419
  2.6 3.0 %collective-permute-start = (f32[128,128]{1,0:T(8,128)S(1)}, f32[128,128]{1,0:T(8,128)S(1)}, u32[]{:S(2)}, u32[]{:S(2)}) collective-permute-start(f32[128,128]{1,0:T(8,128)S(1)} %get-tuple-element.26), channel_id=1, source_target_pairs={{0,1},{1,0},{2,3},{3,2},{4,5},{5,4},{6,7},{7,6},{8,9},{9,8},{10,11... | collective-permute-start | bytes 196616 | tf_op jit(solution)/shard_map/ppermute | solution.py:376
  5.6 0.0 collective-permute-start.1
  5.6 3.0 %collective-permute-start.3 = (f32[4,2,32,128]{3,2,1,0:T(8,128)S(1)}, f32[4,2,32,128]{3,2,1,0:T(8,128)S(1)}, u32[]{:S(2)}, u32[]{:S(2)}) collective-permute-start(f32[4,2,32,128]{3,2,1,0:T(8,128)S(1)} %get-tuple-element.33), channel_id=1, source_target_pairs={{0,1},{1,0},{2,3},{3,2},{4,5},{5,4},{6,7},{7,6},{8,9},{9,8},{10,11... | collective-permute-start | bytes 393224 | tf_op jit(solution)/shard_map/ppermute | solution.py:376
  8.7 0.1 collective-permute-done
  8.8 0.0 collective-permute-done.1
  8.8 0.1 collective-permute-start.2
  8.9 2.8 %collective-permute-done.3 = f32[4,2,32,128]{3,2,1,0:T(8,128)S(1)} collective-permute-done((f32[4,2,32,128]{3,2,1,0:T(8,128)S(1)}, f32[4,2,32,128]{3,2,1,0:T(8,128)S(1)}, u32[]{:S(2)}, u32[]{:S(2)}) %collective-permute-start.3) | collective-permute-done | bytes 131104 | tf_op jit(solution)/shard_map/ppermute | solution.py:376
  11.6 4.6 %collective-permute-start.6 = (f32[2,2,32,128]{3,2,1,0:T(8,128)S(1)}, f32[2,2,32,128]{3,2,1,0:T(8,128)S(1)}, u32[]{:S(2)}, u32[]{:S(2)}) collective-permute-start(f32[2,2,32,128]{3,2,1,0:T(8,128)S(1)} %get-tuple-element.48), channel_id=1, source_target_pairs={{0,6},{1,7},{2,4},{3,5},{4,2},{5,3},{6,0},{7,1},{8,14},{9,15},{10,... | collective-permute-start | bytes 196616 | tf_op jit(solution)/shard_map/ppermute | solution.py:376
  16.3 0.0 collective-permute-start.4
  16.3 0.6 %collective-permute-start.5 = (f32[2,2,32,128]{3,2,1,0:T(8,128)S(1)}, f32[2,2,32,128]{3,2,1,0:T(8,128)S(1)}, u32[]{:S(2)}, u32[]{:S(2)}) collective-permute-start(f32[2,2,32,128]{3,2,1,0:T(8,128)S(1)} %get-tuple-element.51), channel_id=1, source_target_pairs={{0,4},{1,5},{2,6},{3,7},{4,0},{5,1},{6,2},{7,3},{8,12},{9,13},{10,... | collective-permute-start | bytes 196616 | tf_op jit(solution)/shard_map/ppermute | solution.py:376
  16.9 0.0 collective-permute-done.2.other
  16.9 1.9 %bounds.1 = f32[8,136,128]{2,1,0:T(8,128)} custom-call(s32[6]{0:T(128)S(1)} %stack.86.info, f32[8,128]{1,0:T(8,128)S(1)} %get-tuple-element.25.rates, f32[2,128,128]{2,1,0:T(8,128)S(1)} %pad_maximum_fusion.mine, f32[2,128,128]{2,1,0:T(8,128)S(1)} %collective-permute-done.2.other, f32[2,128,128]{2,1,0:T(8,128)S(1)} %get-tuple-element.28.masked, ...), custom_call_target="tpu_custom_call" | custom-call | tf_op jit(solution)/shard_map/bounds/pallas_call | solution.py:419
  18.9 5.0 %all-to-all-start = ((f32[8,136,128]{2,1,0:T(8,128)}), f32[8,136,128]{2,1,0:T(8,128)S(1)}, u32[]{:S(2)}, u32[]{:S(2)}) async-start(f32[8,136,128]{2,1,0:T(8,128)} %bounds.1), calls=%async_computation | async-start | bytes 1114112 | tf_op jit(solution)/shard_map/all_to_all | solution.py:479
  23.9 0.0 collective-permute-done.6
  23.9 0.0 collective-permute-done.4
  23.9 0.0 collective-permute-done.5
  24.0 1.6 %collective-permute-start.7 = (f32[8,2,32,128]{3,2,1,0:T(8,128)S(1)}, f32[8,2,32,128]{3,2,1,0:T(8,128)S(1)}, u32[]{:S(2)}, u32[]{:S(2)}) collective-permute-start(f32[8,2,32,128]{3,2,1,0:T(8,128)S(1)} %constant_dynamic-update-slice_fusion.mine), channel_id=1, source_target_pairs={{0,16},{1,17},{2,18},{3,19},{4,20},{5,21},{6,22},{7,23},{8,24},{9,... | collective-permute-start | bytes 786440 | tf_op jit(solution)/shard_map/ppermute | solution.py:376
  25.5 0.0 collective-permute-start.8
  25.5 5.1 %collective-permute-done.7.beside = f32[8,2,32,128]{3,2,1,0:T(8,128)S(1)} collective-permute-done((f32[8,2,32,128]{3,2,1,0:T(8,128)S(1)}, f32[8,2,32,128]{3,2,1,0:T(8,128)S(1)}, u32[]{:S(2)}, u32[]{:S(2)}) %collective-permute-start.7) | collective-permute-done | bytes 262176 | tf_op jit(solution)/shard_map/ppermute | solution.py:376
  30.7 0.0 collective-permute-start.9
  30.7 0.0 collective-permute-done.8.other
  30.7 1.5 %collective-permute-done.9.other_beside = f32[8,2,32,128]{3,2,1,0:T(8,128)S(1)} collective-permute-done((f32[8,2,32,128]{3,2,1,0:T(8,128)S(1)}, f32[8,2,32,128]{3,2,1,0:T(8,128)S(1)}, u32[]{:S(2)}, u32[]{:S(2)}) %collective-permute-start.9) | collective-permute-done | bytes 262176 | tf_op jit(solution)/shard_map/ppermute | solution.py:376
  32.2 1.1 %faces.1 = (f32[16,32,128]{2,1,0:T(8,128)S(1)}, f32[16,32,128]{2,1,0:T(8,128)S(1)}, f32[16,32,128]{2,1,0:T(8,128)S(1)}, f32[16,32,128]{2,1,0:T(8,128)S(1)}, f32[...) custom-call(s32[6]{0:T(128)S(1)} %stack.86.info, f32[8,2,32,128]{3,2,1,0:T(8,128)S(1)} %constant_dynamic-update-slice_fusion.mine, ...), custom_call_target="tpu_custom_call" | custom-call | tf_op jit(solution)/shard_map/faces/pallas_call | solution.py:419
  33.3 4.6 %all-to-all-done.packed = f32[8,136,128]{2,1,0:T(8,128)S(1)} async-done(((f32[8,136,128]{2,1,0:T(8,128)}), f32[8,136,128]{2,1,0:T(8,128)S(1)}, u32[]{:S(2)}, u32[]{:S(2)}) %all-to-all-start) | async-done | bytes 557088 | tf_op jit(solution)/shard_map/all_to_all | solution.py:479
  37.9 3.2 %four_steps.1 = (f32[16,16,128]{2,1,0:T(8,128)S(1)}, f32[16,16,128]{2,1,0:T(8,128)S(1)}, f32[16,8,128]{2,1,0:T(8,128)S(1)}, f32[16,8,128]{2,1,0:T(8,128)S(1)}) custom-call(s32[6]{0:T(128)S(1)} %stack.86.info, f32[8,128]{1,0:T(8,128)S(1)} %get-tuple-element.25.rates, f32[8,136,128]{2,1,0:T(8,128)S(1)} %all-to-all-done.packed, ...), custom_call_target="tpu_custom_call" | custom-call | tf_op jit(solution)/shard_map/four_steps/pallas_call | solution.py:503
  41.1 0.1 collective-permute-start.10
  41.2 1.6 %collective-permute-start.11 = (f32[16,8,128]{2,1,0:T(8,128)S(1)}, f32[16,8,128]{2,1,0:T(8,128)S(1)}, u32[]{:S(2)}, u32[]{:S(2)}) collective-permute-start(f32[16,8,128]{2,1,0:T(8,128)S(1)} %get-tuple-element.45), channel_id=1, source_target_pairs={{0,9},{1,8},{2,11},{3,10},{4,13},{5,12},{6,15},{7,14},{8,1},{9,0},... | collective-permute-start | bytes 196616 | tf_op jit(solution)/shard_map/ppermute | solution.py:376
  42.8 0.1 collective-permute-start.12
  42.8 0.1 stack.78.info
  42.9 2.2 %collective-permute-done.11.halo_one = f32[16,8,128]{2,1,0:T(8,128)S(1)} collective-permute-done((f32[16,8,128]{2,1,0:T(8,128)S(1)}, f32[16,8,128]{2,1,0:T(8,128)S(1)}, u32[]{:S(2)}, u32[]{:S(2)}) %collective-permute-start.11) | collective-permute-done | bytes 65568 | tf_op jit(solution)/shard_map/ppermute | solution.py:376
  45.1 0.0 collective-permute-done.12.halo_two
  45.1 0.0 collective-permute-done.10.passed
  45.1 2.5 %three_steps.1 = f32[8,2,2,16,128]{4,3,2,1,0:T(8,128)S(1)} custom-call(s32[5]{0:T(128)S(1)} %stack.78.info, f32[8,128]{1,0:T(8,128)S(1)} %get-tuple-element.25.rates, f32[8,136,128]{2,1,0:T(8,128)S(1)} %all-to-all-done.packed, f32[16,16,128]{2,1,0:T(8,128)S(1)} %collective-permute-done.10.passed, f32[16,8,128]{2,1,0:T(8,128)S(1)} %collective-permute-done.11.halo_one, ...), custom_call_target="tpu_custom_call" | custom-call | tf_op jit(solution)/shard_map/three_steps/pallas_call | solution.py:520
  47.6 13.2 %all_to_all.10.result = f32[8,2,2,16,128]{4,3,2,1,0:T(8,128)S(1)} all-to-all(f32[8,2,2,16,128]{4,3,2,1,0:T(8,128)S(1)} %three_steps.1), channel_id=1, replica_groups=mesh['copy'=2,'tm'=2,'space'=8] {'space'}, dimensions={0} | all-to-all | bytes 524288 | tf_op jit(solution)/shard_map/all_to_all | solution.py:529
  60.9 0.8 %unpack.1 = (f32[1,2,128,128]{3,2,1,0:T(8,128)}, f32[1,2,128,128]{3,2,1,0:T(8,128)}) custom-call(f32[8,2,2,16,128]{4,3,2,1,0:T(8,128)S(1)} %all_to_all.10.result), custom_call_target="tpu_custom_call" | custom-call | tf_op jit(solution)/shard_map/unpack/pallas_call | solution.py:534
  (6 shorter events, 0.1 us)
Async XLA Ops:
  2.6 6.2 %collective-permute-start = (f32[128,128]{1,0:T(8,128)S(1)}, f32[128,128]{1,0:T(8,128)S(1)}, u32[]{:S(2)}, u32[]{:S(2)}) collective-permute-start(f32[128,128]{1,0:T(8,128)S(1)} %get-tuple-element.26), channel_id=1, source_target_pairs={{0,1},{1,0},{2,3},{3,2},{4,5},{5,4},{6,7},{7,6},{8,9},{9,8},{10,11... | collective-permute-start | bytes 196616 | tf_op jit(solution)/shard_map/ppermute | solution.py:376
  5.6 3.1 %collective-permute-start.1 = (f32[128,128]{1,0:T(8,128)S(1)}, f32[128,128]{1,0:T(8,128)S(1)}, u32[]{:S(2)}, u32[]{:S(2)}) collective-permute-start(f32[128,128]{1,0:T(8,128)S(1)} %get-tuple-element.27), channel_id=1, source_target_pairs={{0,8},{1,2},{2,1},{3,4},{4,3},{5,6},{6,5},{7,15},{8,0},{9,10},{10,... | collective-permute-start | bytes 196616 | tf_op jit(solution)/shard_map/ppermute | solution.py:376
  5.6 6.0 %collective-permute-start.3 = (f32[4,2,32,128]{3,2,1,0:T(8,128)S(1)}, f32[4,2,32,128]{3,2,1,0:T(8,128)S(1)}, u32[]{:S(2)}, u32[]{:S(2)}) collective-permute-start(f32[4,2,32,128]{3,2,1,0:T(8,128)S(1)} %get-tuple-element.33), channel_id=1, source_target_pairs={{0,1},{1,0},{2,3},{3,2},{4,5},{5,4},{6,7},{7,6},{8,9},{9,8},{10,11... | collective-permute-start | bytes 393224 | tf_op jit(solution)/shard_map/ppermute | solution.py:376
  8.8 8.2 %collective-permute-start.2 = (f32[2,128,128]{2,1,0:T(8,128)S(1)}, f32[2,128,128]{2,1,0:T(8,128)S(1)}, u32[]{:S(2)}, u32[]{:S(2)}) collective-permute-start(f32[2,128,128]{2,1,0:T(8,128)S(1)} %pad_maximum_fusion.mine), channel_id=1, source_target_pairs={{0,8},{1,9},{2,10},{3,11},{4,12},{5,13},{6,14},{7,15},{8,0},{9,1},... | collective-permute-start | bytes 393224 | tf_op jit(solution)/shard_map/ppermute | solution.py:376
  11.6 12.2 %collective-permute-start.6 = (f32[2,2,32,128]{3,2,1,0:T(8,128)S(1)}, f32[2,2,32,128]{3,2,1,0:T(8,128)S(1)}, u32[]{:S(2)}, u32[]{:S(2)}) collective-permute-start(f32[2,2,32,128]{3,2,1,0:T(8,128)S(1)} %get-tuple-element.48), channel_id=1, source_target_pairs={{0,6},{1,7},{2,4},{3,5},{4,2},{5,3},{6,0},{7,1},{8,14},{9,15},{10,... | collective-permute-start | bytes 196616 | tf_op jit(solution)/shard_map/ppermute | solution.py:376
  16.3 7.6 %collective-permute-start.4 = (f32[2,2,32,128]{3,2,1,0:T(8,128)S(1)}, f32[2,2,32,128]{3,2,1,0:T(8,128)S(1)}, u32[]{:S(2)}, u32[]{:S(2)}) collective-permute-start(f32[2,2,32,128]{3,2,1,0:T(8,128)S(1)} %get-tuple-element.50), channel_id=1, source_target_pairs={{0,2},{1,3},{2,0},{3,1},{4,6},{5,7},{6,4},{7,5},{8,10},{9,11},{10,... | collective-permute-start | bytes 196616 | tf_op jit(solution)/shard_map/ppermute | solution.py:376
  16.3 7.6 %collective-permute-start.5 = (f32[2,2,32,128]{3,2,1,0:T(8,128)S(1)}, f32[2,2,32,128]{3,2,1,0:T(8,128)S(1)}, u32[]{:S(2)}, u32[]{:S(2)}) collective-permute-start(f32[2,2,32,128]{3,2,1,0:T(8,128)S(1)} %get-tuple-element.51), channel_id=1, source_target_pairs={{0,4},{1,5},{2,6},{3,7},{4,0},{5,1},{6,2},{7,3},{8,12},{9,13},{10,... | collective-permute-start | bytes 196616 | tf_op jit(solution)/shard_map/ppermute | solution.py:376
  18.9 19.1 %all-to-all-start = ((f32[8,136,128]{2,1,0:T(8,128)}), f32[8,136,128]{2,1,0:T(8,128)S(1)}, u32[]{:S(2)}, u32[]{:S(2)}) async-start(f32[8,136,128]{2,1,0:T(8,128)} %bounds.1), calls=%async_computation | async-start | bytes 1114112 | tf_op jit(solution)/shard_map/all_to_all | solution.py:479
  24.0 6.7 %collective-permute-start.7 = (f32[8,2,32,128]{3,2,1,0:T(8,128)S(1)}, f32[8,2,32,128]{3,2,1,0:T(8,128)S(1)}, u32[]{:S(2)}, u32[]{:S(2)}) collective-permute-start(f32[8,2,32,128]{3,2,1,0:T(8,128)S(1)} %constant_dynamic-update-slice_fusion.mine), channel_id=1, source_target_pairs={{0,16},{1,17},{2,18},{3,19},{4,20},{5,21},{6,22},{7,23},{8,24},{9,... | collective-permute-start | bytes 786440 | tf_op jit(solution)/shard_map/ppermute | solution.py:376
  25.5 5.1 %collective-permute-start.8 = (f32[8,2,32,128]{3,2,1,0:T(8,128)S(1)}, f32[8,2,32,128]{3,2,1,0:T(8,128)S(1)}, u32[]{:S(2)}, u32[]{:S(2)}) collective-permute-start(f32[8,2,32,128]{3,2,1,0:T(8,128)S(1)} %constant_dynamic-update-slice_fusion.mine), channel_id=1, source_target_pairs={{0,8},{1,9},{2,10},{3,11},{4,12},{5,13},{6,14},{7,15},{8,0},{9,1},... | collective-permute-start | bytes 786440 | tf_op jit(solution)/shard_map/ppermute | solution.py:376
  30.7 1.5 %collective-permute-start.9 = (f32[8,2,32,128]{3,2,1,0:T(8,128)S(1)}, f32[8,2,32,128]{3,2,1,0:T(8,128)S(1)}, u32[]{:S(2)}, u32[]{:S(2)}) collective-permute-start(f32[8,2,32,128]{3,2,1,0:T(8,128)S(1)} %collective-permute-done.7.beside), channel_id=1, source_target_pairs={{0,8},{1,9},{2,10},{3,11},{4,12},{5,13},{6,14},{7,15},{8,0},{9,1},... | collective-permute-start | bytes 786440 | tf_op jit(solution)/shard_map/ppermute | solution.py:376
  41.1 4.0 %collective-permute-start.10 = (f32[16,16,128]{2,1,0:T(8,128)S(1)}, f32[16,16,128]{2,1,0:T(8,128)S(1)}, u32[]{:S(2)}, u32[]{:S(2)}) collective-permute-start(f32[16,16,128]{2,1,0:T(8,128)S(1)} %get-tuple-element.44.advanced), channel_id=1, source_target_pairs={{0,8},{1,9},{2,10},{3,11},{4,12},{5,13},{6,14},{7,15},{8,0},{9,1},... | collective-permute-start | bytes 393224 | tf_op jit(solution)/shard_map/ppermute | solution.py:376
  41.2 3.9 %collective-permute-start.11 = (f32[16,8,128]{2,1,0:T(8,128)S(1)}, f32[16,8,128]{2,1,0:T(8,128)S(1)}, u32[]{:S(2)}, u32[]{:S(2)}) collective-permute-start(f32[16,8,128]{2,1,0:T(8,128)S(1)} %get-tuple-element.45), channel_id=1, source_target_pairs={{0,9},{1,8},{2,11},{3,10},{4,13},{5,12},{6,15},{7,14},{8,1},{9,0},... | collective-permute-start | bytes 196616 | tf_op jit(solution)/shard_map/ppermute | solution.py:376
  42.8 2.3 %collective-permute-start.12 = (f32[16,8,128]{2,1,0:T(8,128)S(1)}, f32[16,8,128]{2,1,0:T(8,128)S(1)}, u32[]{:S(2)}, u32[]{:S(2)}) collective-permute-start(f32[16,8,128]{2,1,0:T(8,128)S(1)} %get-tuple-element.46), channel_id=1, source_target_pairs={{0,8},{1,11},{2,12},{3,9},{4,10},{5,15},{6,14},{7,13},{8,0},{9,3},... | collective-permute-start | bytes 196616 | tf_op jit(solution)/shard_map/ppermute | solution.py:376
